TPU v7x, 128 devices: a whole 4x4x4 slice. The times are simulated.
128 devices in a mesh: tm: 8 (over y, z_hi), space: 16 (over x, z_lo, core).
Axes of the slice: x: 4, y: 4, z: 4 (z_hi: 2, z_lo: 2; z = z_hi * 2 + z_lo), core: 2. Of those that a mesh axis runs over, the one named last changes fastest.
Arguments:
- adjoint_iterate: float32 [8, 64, 256, 256], P('tm', 'space'), may hold values from -6 to 6
- forward_states: float32 [8, 2, 64, 256, 256], P('tm', None, 'space'), may hold values from -6 to 6
- conductivity: float32 [64, 256, 256], P('space'), may hold values from 0.25 to 4
- coarse_rate: float32 [64, 256, 256], P('space'), may hold values from 0.0125 to 4
- terminal_adjoint: float32 [64, 256, 256], P('space'), may hold values from -6 to 6
- smallest_eig: float32 [1], replicated, may hold values from 0.5 to 2
- largest_eig: float32 [1], replicated, may hold values from 50 to 64
Outputs:
- adjoint_next: float32 [8, 64, 256, 256], P('tm', 'space')
- sensitivity: float32 [64, 256, 256], P('space')
All inputs are finite; a program needn't handle non-finite values.
Results may differ from a plain program's by a relative error of at most 0.0001.
Values sent between devices are 32-bit elements; how exact they have to be, the bound alone decides.
No kernel may reach another device: no remote copies, remote signals or barrier semaphores. Data moves between devices by JAX's collectives and lax.ppermute only.
A program may use at most 128 MiB of HBM per device.

v0:
```python
import jax
import jax.numpy as jnp
from jax import lax
from jax.sharding import PartitionSpec as P

SWEEPS = 8


time_step = 1.0
NEIGHBOUR_STEPS = ((1, 0, 0), (-1, 0, 0), (0, 1, 0), (0, -1, 0), (0, 0, 1), (0, 0, -1))


def with_halo(block, sides, width):
    for axis, dim in sides:
        count = lax.axis_size(axis)
        forward = [(i, i + 1) for i in range(count - 1)]
        backward = [(target, source) for source, target in forward]
        low = lax.ppermute(
            lax.slice_in_dim(block, block.shape[dim] - width, None, axis=dim), axis, forward
        )
        high = lax.ppermute(lax.slice_in_dim(block, 0, width, axis=dim), axis, backward)
        block = jnp.concatenate([low, block, high], axis=dim)
    return block


def passed_along(block, axis, distance):
    devices = range(lax.axis_size(axis))
    route = [(i - distance, i) for i in devices if i - distance in devices]
    return lax.ppermute(block, axis, route)


def entering(value, axis, join, neutral):
    count, mine = (lax.axis_size(axis), lax.axis_index(axis))
    pieces = jax.tree.map(lambda part: lax.all_gather(part, axis), value)
    pieces = jax.tree.map(lambda part: part[::-1], pieces)
    mine = count - 1 - mine
    running = jax.tree.map(
        lambda part, zero: jnp.full_like(part, 0) + jnp.asarray(zero, part.dtype), value, neutral
    )

    def lap(position, running):
        longer = join(running, jax.tree.map(lambda part: part[position], pieces))
        return jax.tree.map(lambda new, old: jnp.where(position < mine, new, old), longer, running)

    return lax.fori_loop(0, count - 1, lap, running)


def stencil(field_ext, coef_ext):
    plane_count, row_count, column_count = field_ext.shape
    padded = jnp.pad(field_ext, ((0, 0), (1, 1), (1, 1)))
    coef_pad = jnp.pad(coef_ext, ((0, 0), (1, 1), (1, 1)))
    center = padded[1:-1, 1:-1, 1:-1]
    coef_mid = coef_pad[1:-1, 1:-1, 1:-1]
    total = jnp.zeros_like(center)
    for shift_z, shift_x, shift_y in NEIGHBOUR_STEPS:
        near = padded[
            1 + shift_z : plane_count - 1 + shift_z,
            1 + shift_x : row_count + 1 + shift_x,
            1 + shift_y : column_count + 1 + shift_y,
        ]
        coef_near = coef_pad[
            1 + shift_z : plane_count - 1 + shift_z,
            1 + shift_x : row_count + 1 + shift_x,
            1 + shift_y : column_count + 1 + shift_y,
        ]
        total = total + 0.5 * (coef_mid + coef_near) * (center - near)
    return center + time_step * total


def face_term(adjoint_ext, state_ext):
    plane_count, row_count, column_count = adjoint_ext.shape
    adj_pad = jnp.pad(adjoint_ext, ((0, 0), (1, 1), (1, 1)))
    state_pad = jnp.pad(state_ext, ((0, 0), (1, 1), (1, 1)))
    adj_mid = adj_pad[1:-1, 1:-1, 1:-1]
    state_mid = state_pad[1:-1, 1:-1, 1:-1]
    total = jnp.zeros_like(adj_mid)
    for shift_z, shift_x, shift_y in NEIGHBOUR_STEPS:
        adj_near = adj_pad[
            1 + shift_z : plane_count - 1 + shift_z,
            1 + shift_x : row_count + 1 + shift_x,
            1 + shift_y : column_count + 1 + shift_y,
        ]
        state_near = state_pad[
            1 + shift_z : plane_count - 1 + shift_z,
            1 + shift_x : row_count + 1 + shift_x,
            1 + shift_y : column_count + 1 + shift_y,
        ]
        total = total + (adj_mid - adj_near) * (state_mid - state_near)
    return -time_step * 0.5 * total


def constants(smallest_eig, largest_eig):
    low = smallest_eig[0]
    high = largest_eig[0]
    center = (high + low) / 2.0
    radius = (high - low) / 2.0
    return (center, radius, center / radius)


def solve_single(rhs, coef_wide, smallest_eig, largest_eig):
    center, radius, scaled = constants(smallest_eig, largest_eig)
    coef_ext = coef_wide[1:-1]
    ratio = 1.0 / scaled
    iterate = jnp.zeros_like(rhs)
    residual = rhs
    direction = rhs / center
    for sweep_index in range(SWEEPS):
        iterate = iterate + direction
        extended = with_halo(direction, (("space", 0),), 1)
        residual = residual - stencil(extended, coef_ext)
        ratio_next = 1.0 / (2.0 * scaled - ratio)
        direction = ratio_next * ratio * direction + 2.0 * ratio_next / radius * residual
        ratio = ratio_next
    return iterate + direction


def slab_terms(adjoint_field, state_field):
    both = with_halo(jnp.stack([adjoint_field, state_field]), (("space", 1),), 1)
    return face_term(both[0], both[1])


def combine_maps(earlier, later):
    return (later[0] * earlier[0], later[1] + later[0] * earlier[1])


def per_device(
    adjoint_iterate,
    forward_states,
    conductivity,
    coarse_rate,
    terminal_adjoint,
    smallest_eig,
    largest_eig,
):
    coef_wide = with_halo(conductivity, (("space", 0),), 2)
    slab_index = lax.axis_index("tm")
    slab_total = lax.axis_size("tm")
    is_last = slab_index == slab_total - 1
    shifted = passed_along(adjoint_iterate, "tm", -1)
    late_end = shifted[0] + jnp.where(is_last, terminal_adjoint, 0.0)

    def solve(rhs):
        return solve_single(rhs, coef_wide, smallest_eig, largest_eig)

    late = solve(late_end)
    local_sens = slab_terms(late, forward_states[0, 1])
    early = solve(late)
    local_sens = local_sens + slab_terms(early, forward_states[0, 0])
    decay = jnp.exp(-coarse_rate)
    mismatch = early - adjoint_iterate[0]
    identity = (jnp.ones_like(decay), jnp.zeros_like(mismatch))
    scanned = entering((decay, mismatch), "tm", combine_maps, identity)
    carry_next = scanned[1]
    adjoint_next = (early + decay * carry_next)[None]
    sensitivity = lax.psum(local_sens, "tm")
    return (adjoint_next, sensitivity)


def solution(mesh):
    return jax.shard_map(
        per_device,
        mesh=mesh,
        in_specs=(
            P("tm", "space", None, None),
            P("tm", None, "space", None, None),
            P("space", None, None),
            P("space", None, None),
            P("space", None, None),
            P(),
            P(),
        ),
        out_specs=(P("tm", "space", None, None), P("space", None, None)),
        check_vma=False,
    )
```

profile of v0, /device:TPU:0, one launch (start us, length us, event | category | flops | bytes accessed | tf_op | source)
XLA Modules:
  0.0 559.9 jit_solution(3785033155701249429)
XLA Ops:
  17.7 25.4 %collective-permute-done = f32[1,4,256,256]{3,2,1,0:T(8,128)S(1)} collective-permute-done((f32[1,4,256,256]{3,2,1,0:T(8,128)}, f32[1,4,256,256]{3,2,1,0:T(8,128)S(1)}, u32[]{:S(2)}, u32[]{:S(2)}) %collective-permute-start) | collective-permute-done | bytes 1048608 | tf_op jit(solution)/shard_map/ppermute | solution.py:29
  51.3 4.6 multiply_add_fusion.13
  59.0 6.6 %collective-permute-start.6 = (f32[1,256,256]{2,1,0:T(8,128)}, f32[1,256,256]{2,1,0:T(8,128)}, u32[]{:S(2)}, u32[]{:S(2)}) collective-permute-start(f32[1,256,256]{2,1,0:T(8,128)} %get-tuple-element.203), channel_id=1, source_target_pairs={{0,1},{1,2},{2,3},{3,4},{4,5},{5,6},{6,7},{7,8},{8,9},{9,10},{10,1... | collective-permute-start | bytes 786440 | tf_op jit(solution)/shard_map/ppermute | solution.py:18
  68.7 5.0 multiply_add_fusion.12
  76.8 7.6 %collective-permute-start.8 = (f32[1,256,256]{2,1,0:T(8,128)}, f32[1,256,256]{2,1,0:T(8,128)}, u32[]{:S(2)}, u32[]{:S(2)}) collective-permute-start(f32[1,256,256]{2,1,0:T(8,128)} %get-tuple-element.201), channel_id=1, source_target_pairs={{0,1},{1,2},{2,3},{3,4},{4,5},{5,6},{6,7},{7,8},{8,9},{9,10},{10,1... | collective-permute-start | bytes 786440 | tf_op jit(solution)/shard_map/ppermute | solution.py:18
  93.7 7.3 %collective-permute-start.10 = (f32[1,256,256]{2,1,0:T(8,128)}, f32[1,256,256]{2,1,0:T(8,128)S(1)}, u32[]{:S(2)}, u32[]{:S(2)}) collective-permute-start(f32[1,256,256]{2,1,0:T(8,128)} %get-tuple-element.199), channel_id=1, source_target_pairs={{0,1},{1,2},{2,3},{3,4},{4,5},{5,6},{6,7},{7,8},{8,9},{9,10},{10,1... | collective-permute-start | bytes 786440 | tf_op jit(solution)/shard_map/ppermute | solution.py:18
  102.4 4.3 collective-permute-done.9
  108.8 5.0 multiply_add_fusion.10
  117.0 8.4 %collective-permute-start.12 = (f32[1,256,256]{2,1,0:T(8,128)}, f32[1,256,256]{2,1,0:T(8,128)}, u32[]{:S(2)}, u32[]{:S(2)}) collective-permute-start(f32[1,256,256]{2,1,0:T(8,128)} %get-tuple-element.197), channel_id=1, source_target_pairs={{0,1},{1,2},{2,3},{3,4},{4,5},{5,6},{6,7},{7,8},{8,9},{9,10},{10,1... | collective-permute-start | bytes 786440 | tf_op jit(solution)/shard_map/ppermute | solution.py:18
  127.9 5.0 multiply_add_fusion.9
  136.1 9.8 %collective-permute-start.14 = (f32[1,256,256]{2,1,0:T(8,128)}, f32[1,256,256]{2,1,0:T(8,128)}, u32[]{:S(2)}, u32[]{:S(2)}) collective-permute-start(f32[1,256,256]{2,1,0:T(8,128)} %get-tuple-element.195), channel_id=1, source_target_pairs={{0,1},{1,2},{2,3},{3,4},{4,5},{5,6},{6,7},{7,8},{8,9},{9,10},{10,1... | collective-permute-start | bytes 786440 | tf_op jit(solution)/shard_map/ppermute | solution.py:18
  148.9 5.2 multiply_add_fusion.8
  157.2 8.5 %collective-permute-start.16 = (f32[1,256,256]{2,1,0:T(8,128)}, f32[1,256,256]{2,1,0:T(8,128)}, u32[]{:S(2)}, u32[]{:S(2)}) collective-permute-start(f32[1,256,256]{2,1,0:T(8,128)} %get-tuple-element.193), channel_id=1, source_target_pairs={{0,1},{1,2},{2,3},{3,4},{4,5},{5,6},{6,7},{7,8},{8,9},{9,10},{10,1... | collective-permute-start | bytes 786440 | tf_op jit(solution)/shard_map/ppermute | solution.py:18
  169.3 4.8 multiply_add_fusion.7
  177.1 8.0 %collective-permute-start.18 = (f32[1,256,256]{2,1,0:T(8,128)}, f32[1,256,256]{2,1,0:T(8,128)}, u32[]{:S(2)}, u32[]{:S(2)}) collective-permute-start(f32[1,256,256]{2,1,0:T(8,128)} %get-tuple-element.191), channel_id=1, source_target_pairs={{0,1},{1,2},{2,3},{3,4},{4,5},{5,6},{6,7},{7,8},{8,9},{9,10},{10,1... | collective-permute-start | bytes 786440 | tf_op jit(solution)/shard_map/ppermute | solution.py:18
  188.2 5.8 %broadcast_divide_fusion = (f32[4,256,256]{2,1,0:T(8,128)S(1)}, f32[4,256,256]{2,1,0:T(8,128)S(1)}) fusion(f32[]{:T(128)} %bitcast.1, f32[4,256,256]{2,1,0:T(8,128)} %get-tuple-element.145, f32[4,256,256]{2,1,0:T(8,128)} %copy-done.31, f32[4,256,256]{2,1,0:T(8,128)S(1)} %copy-done.20, f32[6,258,258]{2,1,0:T(8,128)S(1)} %select_maximum_fusion.16, ...), kind=kLoop, calls=%fused_computation.520 | loop fusion | flops 13107200 | bytes 23593016 | tf_op jit(solution)/shard_map/div | solution.py:106
  195.4 13.5 %collective-permute-start.20 = (f32[1,256,256]{2,1,0:T(8,128)S(1)}, f32[1,256,256]{2,1,0:T(8,128)S(1)}, u32[]{:S(2)}, u32[]{:S(2)}) collective-permute-start(f32[1,256,256]{2,1,0:T(8,128)S(1)} %get-tuple-element.189), channel_id=1, source_target_pairs={{0,1},{1,2},{2,3},{3,4},{4,5},{5,6},{6,7},{7,8},{8,9},{9,10},{10,1... | collective-permute-start | bytes 786440 | tf_op jit(solution)/shard_map/ppermute | solution.py:18
  213.5 7.3 %collective-permute-start.22 = (f32[1,256,256]{2,1,0:T(8,128)S(1)}, f32[1,256,256]{2,1,0:T(8,128)S(1)}, u32[]{:S(2)}, u32[]{:S(2)}) collective-permute-start(f32[1,256,256]{2,1,0:T(8,128)S(1)} %get-tuple-element.187), channel_id=1, source_target_pairs={{0,1},{1,2},{2,3},{3,4},{4,5},{5,6},{6,7},{7,8},{8,9},{9,10},{10,1... | collective-permute-start | bytes 786440 | tf_op jit(solution)/shard_map/ppermute | solution.py:18
  225.4 13.7 %collective-permute-start.24 = (f32[1,256,256]{2,1,0:T(8,128)S(1)}, f32[1,256,256]{2,1,0:T(8,128)S(1)}, u32[]{:S(2)}, u32[]{:S(2)}) collective-permute-start(f32[1,256,256]{2,1,0:T(8,128)S(1)} %get-tuple-element.185), channel_id=1, source_target_pairs={{0,1},{1,2},{2,3},{3,4},{4,5},{5,6},{6,7},{7,8},{8,9},{9,10},{10,1... | collective-permute-start | bytes 786440 | tf_op jit(solution)/shard_map/ppermute | solution.py:18
  245.2 12.8 %collective-permute-start.26 = (f32[1,256,256]{2,1,0:T(8,128)S(1)}, f32[1,256,256]{2,1,0:T(8,128)S(1)}, u32[]{:S(2)}, u32[]{:S(2)}) collective-permute-start(f32[1,256,256]{2,1,0:T(8,128)S(1)} %get-tuple-element.183), channel_id=1, source_target_pairs={{0,1},{1,2},{2,3},{3,4},{4,5},{5,6},{6,7},{7,8},{8,9},{9,10},{10,1... | collective-permute-start | bytes 786440 | tf_op jit(solution)/shard_map/ppermute | solution.py:18
  263.3 12.8 %collective-permute-start.28 = (f32[1,256,256]{2,1,0:T(8,128)S(1)}, f32[1,256,256]{2,1,0:T(8,128)S(1)}, u32[]{:S(2)}, u32[]{:S(2)}) collective-permute-start(f32[1,256,256]{2,1,0:T(8,128)S(1)} %get-tuple-element.181), channel_id=1, source_target_pairs={{0,1},{1,2},{2,3},{3,4},{4,5},{5,6},{6,7},{7,8},{8,9},{9,10},{10,1... | collective-permute-start | bytes 786440 | tf_op jit(solution)/shard_map/ppermute | solution.py:18
  281.7 10.3 %collective-permute-start.30 = (f32[1,256,256]{2,1,0:T(8,128)S(1)}, f32[1,256,256]{2,1,0:T(8,128)S(1)}, u32[]{:S(2)}, u32[]{:S(2)}) collective-permute-start(f32[1,256,256]{2,1,0:T(8,128)S(1)} %get-tuple-element.179), channel_id=1, source_target_pairs={{0,1},{1,2},{2,3},{3,4},{4,5},{5,6},{6,7},{7,8},{8,9},{9,10},{10,1... | collective-permute-start | bytes 786440 | tf_op jit(solution)/shard_map/ppermute | solution.py:18
  295.1 4.7 multiply_add_fusion.1
  302.4 7.4 %collective-permute-start.32 = (f32[1,256,256]{2,1,0:T(8,128)S(1)}, f32[1,256,256]{2,1,0:T(8,128)S(1)}, u32[]{:S(2)}, u32[]{:S(2)}) collective-permute-start(f32[1,256,256]{2,1,0:T(8,128)S(1)} %get-tuple-element.177), channel_id=1, source_target_pairs={{0,1},{1,2},{2,3},{3,4},{4,5},{5,6},{6,7},{7,8},{8,9},{9,10},{10,1... | collective-permute-start | bytes 786440 | tf_op jit(solution)/shard_map/ppermute | solution.py:18
  316.2 8.0 %collective-permute-start.34 = (f32[1,256,256]{2,1,0:T(8,128)S(1)}, f32[1,256,256]{2,1,0:T(8,128)S(1)}, u32[]{:S(2)}, u32[]{:S(2)}) collective-permute-start(f32[1,256,256]{2,1,0:T(8,128)S(1)} %get-tuple-element.175), channel_id=1, source_target_pairs={{0,1},{1,2},{2,3},{3,4},{4,5},{5,6},{6,7},{7,8},{8,9},{9,10},{10,1... | collective-permute-start | bytes 786440 | tf_op jit(solution)/shard_map/ppermute | solution.py:18
  335.1 9.0 %collective-permute-start.36 = (f32[2,1,256,256]{3,2,1,0:T(8,128)}, f32[2,1,256,256]{3,2,1,0:T(8,128)}, u32[]{:S(2)}, u32[]{:S(2)}) collective-permute-start(f32[2,1,256,256]{3,2,1,0:T(8,128)} %get-tuple-element.173), channel_id=1, source_target_pairs={{0,1},{1,2},{2,3},{3,4},{4,5},{5,6},{6,7},{7,8},{8,9},{9,10},{10,1... | collective-permute-start | bytes 1572872 | tf_op jit(solution)/shard_map/ppermute | solution.py:18
  356.4 11.4 %fusion.12 = f32[4,256,256]{2,1,0:T(8,128)} fusion(f32[4,256,256]{2,1,0:T(8,128)S(1)} %copy-done.24, f32[6,256,256]{2,1,0:T(8,128)} %get-tuple-element.168, f32[6,256,256]{2,1,0:T(8,128)} %get-tuple-element.167, f32[4,256,256]{2,1,0:T(8,128)S(1)} %copy-done.22, f32[6,256,256]{2,1,0:T(8,128)} %get-tuple-element.166, f32[6,256,256]{2,1,0:T(8,128)} %get-tuple-element.165, ...), kind=kLoop, calls=%fused_computation.73 | loop fusion | flops 16777216 | bytes 17825792 | tf_op jit(solution)/shard_map/add | solution.py:148
  367.9 7.6 %rev.7 = f32[8,4,256,256]{3,2,1,0:T(8,128)} reverse(f32[8,4,256,256]{3,2,1,0:T(8,128)} %bitcast.111), dimensions={0} | reverse | bytes 16777216 | tf_op jit(solution)/shard_map/rev | solution.py:35
  375.5 86.4 %all-gather.5.cloned.1.call-done = f32[32,256,256]{2,1,0:T(8,128)} async-done(((f32[4,256,256]{2,1,0:T(8,128)}), f32[32,256,256]{2,1,0:T(8,128)}) %all-gather.5.cloned.1.call-update) | async-done | bytes 8388624 | tf_op jit(solution)/shard_map/all_gather | solution.py:34
  461.9 7.6 %rev.6 = f32[8,4,256,256]{3,2,1,0:T(8,128)} reverse(f32[8,4,256,256]{3,2,1,0:T(8,128)} %bitcast.112), dimensions={0} | reverse | bytes 16777216 | tf_op jit(solution)/shard_map/rev | solution.py:35
  469.5 17.6 %while.14 = (s32[]{:T(128)}, f32[4,256,256]{2,1,0:T(8,128)S(1)}, s32[]{:T(128)}, f32[8,4,256,256]{3,2,1,0:T(8,128)}, f32[8,4,256,256]{3,2,1,0:T(8,128)}, /*index=5*/s32[]{:T(128)}, s32[]{:T(128)}) while((s32[]{:T(128)}, f32[4,256,256]{2,1,0:T(8,128)S(1)}, s32[]{:T(128)}, f32[8,4,256,256]{3,2,1,0:T(8,128)}, ...), condition=%wide.region_1.2_spmd.clone, body=%wide.region_0.1_spmd.clone.sunk | while | flops 1048580 | bytes 4194405 | solution.py:45
  488.3 62.5 %all-reduce.23.cloned.1.call-done = f32[4,256,256]{2,1,0:T(8,128)} async-done(((f32[4,256,256]{2,1,0:T(8,128)}), f32[4,256,256]{2,1,0:T(8,128)}) %all-reduce.23.cloned.1.call-update) | async-done | bytes 1048592 | tf_op jit(solution)/shard_map/psum | solution.py:155
  (228 shorter events, 146.2 us)
Async XLA Ops:
  7.2 360.7 %all-gather.7.cloned.1.call-start = ((), (), s32[]{:S(2)}) async-start(), calls=%async_computation.2 | async-start | bytes 9437184 | tf_op jit(solution)/shard_map/all_gather | solution.py:34
  7.2 35.8 %collective-permute-start = (f32[1,4,256,256]{3,2,1,0:T(8,128)}, f32[1,4,256,256]{3,2,1,0:T(8,128)S(1)}, u32[]{:S(2)}, u32[]{:S(2)}) collective-permute-start(f32[1,4,256,256]{3,2,1,0:T(8,128)} %param.9), channel_id=1, source_target_pairs={{16,0},{32,16},{48,32},{64,48},{80,64},{96,80},{112,96},{17,1},{33... | collective-permute-start | bytes 3145736 | tf_op jit(solution)/shard_map/ppermute | solution.py:29
  10.9 36.7 %collective-permute-start.1 = (f32[2,256,256]{2,1,0:T(8,128)}, f32[2,256,256]{2,1,0:T(8,128)}, u32[]{:S(2)}, u32[]{:S(2)}) collective-permute-start(f32[2,256,256]{2,1,0:T(8,128)} %get-tuple-element.206), channel_id=1, source_target_pairs={{1,0},{2,1},{3,2},{4,3},{5,4},{6,5},{7,6},{8,7},{9,8},{10,9},{11,1... | collective-permute-start | bytes 1572872 | tf_op jit(solution)/shard_map/ppermute | solution.py:21
  12.3 35.3 %collective-permute-start.3 = (f32[2,256,256]{2,1,0:T(8,128)}, f32[2,256,256]{2,1,0:T(8,128)}, u32[]{:S(2)}, u32[]{:S(2)}) collective-permute-start(f32[2,256,256]{2,1,0:T(8,128)} %get-tuple-element.205), channel_id=1, source_target_pairs={{0,1},{1,2},{2,3},{3,4},{4,5},{5,6},{6,7},{7,8},{8,9},{9,10},{10,1... | collective-permute-start | bytes 1572872 | tf_op jit(solution)/shard_map/ppermute | solution.py:18
  75.6 9.1 %collective-permute-start.7 = (f32[1,256,256]{2,1,0:T(8,128)}, f32[1,256,256]{2,1,0:T(8,128)S(1)}, u32[]{:S(2)}, u32[]{:S(2)}) collective-permute-start(f32[1,256,256]{2,1,0:T(8,128)} %get-tuple-element.202), channel_id=1, source_target_pairs={{1,0},{2,1},{3,2},{4,3},{5,4},{6,5},{7,6},{8,7},{9,8},{10,9},{11,1... | collective-permute-start | bytes 786440 | tf_op jit(solution)/shard_map/ppermute | solution.py:21
  93.7 8.7 %collective-permute-start.10 = (f32[1,256,256]{2,1,0:T(8,128)}, f32[1,256,256]{2,1,0:T(8,128)S(1)}, u32[]{:S(2)}, u32[]{:S(2)}) collective-permute-start(f32[1,256,256]{2,1,0:T(8,128)} %get-tuple-element.199), channel_id=1, source_target_pairs={{0,1},{1,2},{2,3},{3,4},{4,5},{5,6},{6,7},{7,8},{8,9},{9,10},{10,1... | collective-permute-start | bytes 786440 | tf_op jit(solution)/shard_map/ppermute | solution.py:18
  115.7 9.8 %collective-permute-start.11 = (f32[1,256,256]{2,1,0:T(8,128)}, f32[1,256,256]{2,1,0:T(8,128)S(1)}, u32[]{:S(2)}, u32[]{:S(2)}) collective-permute-start(f32[1,256,256]{2,1,0:T(8,128)} %get-tuple-element.198), channel_id=1, source_target_pairs={{1,0},{2,1},{3,2},{4,3},{5,4},{6,5},{7,6},{8,7},{9,8},{10,9},{11,1... | collective-permute-start | bytes 786440 | tf_op jit(solution)/shard_map/ppermute | solution.py:21
  117.0 8.8 %collective-permute-start.12 = (f32[1,256,256]{2,1,0:T(8,128)}, f32[1,256,256]{2,1,0:T(8,128)}, u32[]{:S(2)}, u32[]{:S(2)}) collective-permute-start(f32[1,256,256]{2,1,0:T(8,128)} %get-tuple-element.197), channel_id=1, source_target_pairs={{0,1},{1,2},{2,3},{3,4},{4,5},{5,6},{6,7},{7,8},{8,9},{9,10},{10,1... | collective-permute-start | bytes 786440 | tf_op jit(solution)/shard_map/ppermute | solution.py:18
  134.8 11.2 %collective-permute-start.13 = (f32[1,256,256]{2,1,0:T(8,128)}, f32[1,256,256]{2,1,0:T(8,128)S(1)}, u32[]{:S(2)}, u32[]{:S(2)}) collective-permute-start(f32[1,256,256]{2,1,0:T(8,128)} %get-tuple-element.196), channel_id=1, source_target_pairs={{1,0},{2,1},{3,2},{4,3},{5,4},{6,5},{7,6},{8,7},{9,8},{10,9},{11,1... | collective-permute-start | bytes 786440 | tf_op jit(solution)/shard_map/ppermute | solution.py:21
  136.1 10.5 %collective-permute-start.14 = (f32[1,256,256]{2,1,0:T(8,128)}, f32[1,256,256]{2,1,0:T(8,128)}, u32[]{:S(2)}, u32[]{:S(2)}) collective-permute-start(f32[1,256,256]{2,1,0:T(8,128)} %get-tuple-element.195), channel_id=1, source_target_pairs={{0,1},{1,2},{2,3},{3,4},{4,5},{5,6},{6,7},{7,8},{8,9},{9,10},{10,1... | collective-permute-start | bytes 786440 | tf_op jit(solution)/shard_map/ppermute | solution.py:18
  155.9 11.2 %collective-permute-start.15 = (f32[1,256,256]{2,1,0:T(8,128)}, f32[1,256,256]{2,1,0:T(8,128)S(1)}, u32[]{:S(2)}, u32[]{:S(2)}) collective-permute-start(f32[1,256,256]{2,1,0:T(8,128)} %get-tuple-element.194), channel_id=1, source_target_pairs={{1,0},{2,1},{3,2},{4,3},{5,4},{6,5},{7,6},{8,7},{9,8},{10,9},{11,1... | collective-permute-start | bytes 786440 | tf_op jit(solution)/shard_map/ppermute | solution.py:21
  157.2 9.9 %collective-permute-start.16 = (f32[1,256,256]{2,1,0:T(8,128)}, f32[1,256,256]{2,1,0:T(8,128)}, u32[]{:S(2)}, u32[]{:S(2)}) collective-permute-start(f32[1,256,256]{2,1,0:T(8,128)} %get-tuple-element.193), channel_id=1, source_target_pairs={{0,1},{1,2},{2,3},{3,4},{4,5},{5,6},{6,7},{7,8},{8,9},{9,10},{10,1... | collective-permute-start | bytes 786440 | tf_op jit(solution)/shard_map/ppermute | solution.py:18
  166.9 295.0 %all-gather.5.cloned.1.call-start = ((), (), s32[]{:S(2)}) async-start(), calls=%async_computation.1 | async-start | bytes 9437184 | tf_op jit(solution)/shard_map/all_gather | solution.py:34
  175.8 9.4 %collective-permute-start.17 = (f32[1,256,256]{2,1,0:T(8,128)}, f32[1,256,256]{2,1,0:T(8,128)S(1)}, u32[]{:S(2)}, u32[]{:S(2)}) collective-permute-start(f32[1,256,256]{2,1,0:T(8,128)} %get-tuple-element.192), channel_id=1, source_target_pairs={{1,0},{2,1},{3,2},{4,3},{5,4},{6,5},{7,6},{8,7},{9,8},{10,9},{11,1... | collective-permute-start | bytes 786440 | tf_op jit(solution)/shard_map/ppermute | solution.py:21
  177.1 8.8 %collective-permute-start.18 = (f32[1,256,256]{2,1,0:T(8,128)}, f32[1,256,256]{2,1,0:T(8,128)}, u32[]{:S(2)}, u32[]{:S(2)}) collective-permute-start(f32[1,256,256]{2,1,0:T(8,128)} %get-tuple-element.191), channel_id=1, source_target_pairs={{0,1},{1,2},{2,3},{3,4},{4,5},{5,6},{6,7},{7,8},{8,9},{9,10},{10,1... | collective-permute-start | bytes 786440 | tf_op jit(solution)/shard_map/ppermute | solution.py:18
  194.1 14.8 %collective-permute-start.19 = (f32[1,256,256]{2,1,0:T(8,128)S(1)}, f32[1,256,256]{2,1,0:T(8,128)S(1)}, u32[]{:S(2)}, u32[]{:S(2)}) collective-permute-start(f32[1,256,256]{2,1,0:T(8,128)S(1)} %get-tuple-element.190), channel_id=1, source_target_pairs={{1,0},{2,1},{3,2},{4,3},{5,4},{6,5},{7,6},{8,7},{9,8},{10,9},{11,1... | collective-permute-start | bytes 786440 | tf_op jit(solution)/shard_map/ppermute | solution.py:21
  195.4 14.6 %collective-permute-start.20 = (f32[1,256,256]{2,1,0:T(8,128)S(1)}, f32[1,256,256]{2,1,0:T(8,128)S(1)}, u32[]{:S(2)}, u32[]{:S(2)}) collective-permute-start(f32[1,256,256]{2,1,0:T(8,128)S(1)} %get-tuple-element.189), channel_id=1, source_target_pairs={{0,1},{1,2},{2,3},{3,4},{4,5},{5,6},{6,7},{7,8},{8,9},{9,10},{10,1... | collective-permute-start | bytes 786440 | tf_op jit(solution)/shard_map/ppermute | solution.py:18
  224.1 15.0 %collective-permute-start.23 = (f32[1,256,256]{2,1,0:T(8,128)S(1)}, f32[1,256,256]{2,1,0:T(8,128)S(1)}, u32[]{:S(2)}, u32[]{:S(2)}) collective-permute-start(f32[1,256,256]{2,1,0:T(8,128)S(1)} %get-tuple-element.186), channel_id=1, source_target_pairs={{1,0},{2,1},{3,2},{4,3},{5,4},{6,5},{7,6},{8,7},{9,8},{10,9},{11,1... | collective-permute-start | bytes 786440 | tf_op jit(solution)/shard_map/ppermute | solution.py:21
  225.4 14.8 %collective-permute-start.24 = (f32[1,256,256]{2,1,0:T(8,128)S(1)}, f32[1,256,256]{2,1,0:T(8,128)S(1)}, u32[]{:S(2)}, u32[]{:S(2)}) collective-permute-start(f32[1,256,256]{2,1,0:T(8,128)S(1)} %get-tuple-element.185), channel_id=1, source_target_pairs={{0,1},{1,2},{2,3},{3,4},{4,5},{5,6},{6,7},{7,8},{8,9},{9,10},{10,1... | collective-permute-start | bytes 786440 | tf_op jit(solution)/shard_map/ppermute | solution.py:18
  243.8 14.2 %collective-permute-start.25 = (f32[1,256,256]{2,1,0:T(8,128)S(1)}, f32[1,256,256]{2,1,0:T(8,128)S(1)}, u32[]{:S(2)}, u32[]{:S(2)}) collective-permute-start(f32[1,256,256]{2,1,0:T(8,128)S(1)} %get-tuple-element.184), channel_id=1, source_target_pairs={{1,0},{2,1},{3,2},{4,3},{5,4},{6,5},{7,6},{8,7},{9,8},{10,9},{11,1... | collective-permute-start | bytes 786440 | tf_op jit(solution)/shard_map/ppermute | solution.py:21
  245.2 13.9 %collective-permute-start.26 = (f32[1,256,256]{2,1,0:T(8,128)S(1)}, f32[1,256,256]{2,1,0:T(8,128)S(1)}, u32[]{:S(2)}, u32[]{:S(2)}) collective-permute-start(f32[1,256,256]{2,1,0:T(8,128)S(1)} %get-tuple-element.183), channel_id=1, source_target_pairs={{0,1},{1,2},{2,3},{3,4},{4,5},{5,6},{6,7},{7,8},{8,9},{9,10},{10,1... | collective-permute-start | bytes 786440 | tf_op jit(solution)/shard_map/ppermute | solution.py:18
  262.0 14.1 %collective-permute-start.27 = (f32[1,256,256]{2,1,0:T(8,128)S(1)}, f32[1,256,256]{2,1,0:T(8,128)S(1)}, u32[]{:S(2)}, u32[]{:S(2)}) collective-permute-start(f32[1,256,256]{2,1,0:T(8,128)S(1)} %get-tuple-element.182), channel_id=1, source_target_pairs={{1,0},{2,1},{3,2},{4,3},{5,4},{6,5},{7,6},{8,7},{9,8},{10,9},{11,1... | collective-permute-start | bytes 786440 | tf_op jit(solution)/shard_map/ppermute | solution.py:21
  263.3 13.9 %collective-permute-start.28 = (f32[1,256,256]{2,1,0:T(8,128)S(1)}, f32[1,256,256]{2,1,0:T(8,128)S(1)}, u32[]{:S(2)}, u32[]{:S(2)}) collective-permute-start(f32[1,256,256]{2,1,0:T(8,128)S(1)} %get-tuple-element.181), channel_id=1, source_target_pairs={{0,1},{1,2},{2,3},{3,4},{4,5},{5,6},{6,7},{7,8},{8,9},{9,10},{10,1... | collective-permute-start | bytes 786440 | tf_op jit(solution)/shard_map/ppermute | solution.py:18
  280.4 11.6 %collective-permute-start.29 = (f32[1,256,256]{2,1,0:T(8,128)S(1)}, f32[1,256,256]{2,1,0:T(8,128)S(1)}, u32[]{:S(2)}, u32[]{:S(2)}) collective-permute-start(f32[1,256,256]{2,1,0:T(8,128)S(1)} %get-tuple-element.180), channel_id=1, source_target_pairs={{1,0},{2,1},{3,2},{4,3},{5,4},{6,5},{7,6},{8,7},{9,8},{10,9},{11,1... | collective-permute-start | bytes 786440 | tf_op jit(solution)/shard_map/ppermute | solution.py:21
  281.7 11.4 %collective-permute-start.30 = (f32[1,256,256]{2,1,0:T(8,128)S(1)}, f32[1,256,256]{2,1,0:T(8,128)S(1)}, u32[]{:S(2)}, u32[]{:S(2)}) collective-permute-start(f32[1,256,256]{2,1,0:T(8,128)S(1)} %get-tuple-element.179), channel_id=1, source_target_pairs={{0,1},{1,2},{2,3},{3,4},{4,5},{5,6},{6,7},{7,8},{8,9},{9,10},{10,1... | collective-permute-start | bytes 786440 | tf_op jit(solution)/shard_map/ppermute | solution.py:18
  301.1 8.7 %collective-permute-start.31 = (f32[1,256,256]{2,1,0:T(8,128)S(1)}, f32[1,256,256]{2,1,0:T(8,128)S(1)}, u32[]{:S(2)}, u32[]{:S(2)}) collective-permute-start(f32[1,256,256]{2,1,0:T(8,128)S(1)} %get-tuple-element.178), channel_id=1, source_target_pairs={{1,0},{2,1},{3,2},{4,3},{5,4},{6,5},{7,6},{8,7},{9,8},{10,9},{11,1... | collective-permute-start | bytes 786440 | tf_op jit(solution)/shard_map/ppermute | solution.py:21
  314.8 9.5 %collective-permute-start.33 = (f32[1,256,256]{2,1,0:T(8,128)S(1)}, f32[1,256,256]{2,1,0:T(8,128)S(1)}, u32[]{:S(2)}, u32[]{:S(2)}) collective-permute-start(f32[1,256,256]{2,1,0:T(8,128)S(1)} %get-tuple-element.176), channel_id=1, source_target_pairs={{1,0},{2,1},{3,2},{4,3},{5,4},{6,5},{7,6},{8,7},{9,8},{10,9},{11,1... | collective-permute-start | bytes 786440 | tf_op jit(solution)/shard_map/ppermute | solution.py:21
  316.2 9.2 %collective-permute-start.34 = (f32[1,256,256]{2,1,0:T(8,128)S(1)}, f32[1,256,256]{2,1,0:T(8,128)S(1)}, u32[]{:S(2)}, u32[]{:S(2)}) collective-permute-start(f32[1,256,256]{2,1,0:T(8,128)S(1)} %get-tuple-element.175), channel_id=1, source_target_pairs={{0,1},{1,2},{2,3},{3,4},{4,5},{5,6},{6,7},{7,8},{8,9},{9,10},{10,1... | collective-permute-start | bytes 786440 | tf_op jit(solution)/shard_map/ppermute | solution.py:18
  329.9 221.0 %all-reduce.23.cloned.1.call-start = ((), (), s32[]{:S(2)}) async-start(), calls=%async_computation | async-start | bytes 2097152 | tf_op jit(solution)/shard_map/psum | solution.py:155
  333.7 17.2 %collective-permute-start.35 = (f32[2,1,256,256]{3,2,1,0:T(8,128)}, f32[2,1,256,256]{3,2,1,0:T(8,128)}, u32[]{:S(2)}, u32[]{:S(2)}) collective-permute-start(f32[2,1,256,256]{3,2,1,0:T(8,128)} %get-tuple-element.174), channel_id=1, source_target_pairs={{1,0},{2,1},{3,2},{4,3},{5,4},{6,5},{7,6},{8,7},{9,8},{10,9},{11,1... | collective-permute-start | bytes 1572872 | tf_op jit(solution)/shard_map/ppermute | solution.py:21
  335.1 15.8 %collective-permute-start.36 = (f32[2,1,256,256]{3,2,1,0:T(8,128)}, f32[2,1,256,256]{3,2,1,0:T(8,128)}, u32[]{:S(2)}, u32[]{:S(2)}) collective-permute-start(f32[2,1,256,256]{3,2,1,0:T(8,128)} %get-tuple-element.173), channel_id=1, source_target_pairs={{0,1},{1,2},{2,3},{3,4},{4,5},{5,6},{6,7},{7,8},{8,9},{9,10},{10,1... | collective-permute-start | bytes 1572872 | tf_op jit(solution)/shard_map/ppermute | solution.py:18
  345.3 9.0 %collective-permute-start.37 = (f32[2,1,256,256]{3,2,1,0:T(8,128)S(1)}, f32[2,1,256,256]{3,2,1,0:T(8,128)S(1)}, u32[]{:S(2)}, u32[]{:S(2)}) collective-permute-start(f32[2,1,256,256]{3,2,1,0:T(8,128)S(1)} %get-tuple-element.170), channel_id=1, source_target_pairs={{1,0},{2,1},{3,2},{4,3},{5,4},{6,5},{7,6},{8,7},{9,8},{10,9},{11,1... | collective-permute-start | bytes 1572872 | tf_op jit(solution)/shard_map/ppermute | solution.py:21
  (60 other events, 414.6 us)
Sparse Core Ops, SparseCore 0:
  167.0 140.0 all-gather.6
  330.0 131.8 all-gather.4
  464.4 86.4 all-reduce.22
where the time goes:
time: 569 us; the launch traced here: 560 us
  waiting for transfers between devices  190 us (33%)
  starting transfers between devices  189 us (33%)
  other arithmetic  122 us (21%)
  local copies, waits for them, and re-layouts  41.7 us (7%)
  between operations  17.3 us (3%)
    ppermute x19, starting transfers between devices, with_halo(): lax.ppermute(lax.slice_in_dim(block, block.shape[dim] - width, None, axis...  162 us
    all_gather x2, waiting for transfers between devices, entering(): pieces = jax.tree.map(lambda part: lax.all_gather(part, axis), value)  86.4 us
    psum x1, waiting for transfers between devices, per_device(): sensitivity = lax.psum(local_sens, 'tm')  62.5 us
    add x14, other arithmetic, solve_single(): ratio_next * ratio * direction + 2.0 * ratio_next / radius * residual  50.7 us
    concatenate x19, other arithmetic, with_halo(): block = jnp.concatenate([low, block, high], axis=dim)  28.1 us
    ppermute x1, waiting for transfers between devices, passed_along(): return lax.ppermute(block, axis, route)  25.4 us
    ppermute x19, starting transfers between devices, with_halo(): lax.ppermute(lax.slice_in_dim(block, 0, width, axis=dim), axis, backward)  25 us
    select_n x7, other arithmetic, lap(): jnp.where(position < mine, new, old)  17.5 us
  transfers between devices with their start and end apart: 42, of which 17 were waited for; matrix products, arithmetic and copies ran while one was open for 19% of the time, Pallas kernels for 0%

commit v1 on v0

v1 whole, which is shorter than its diff:
```python
import jax
import jax.numpy as jnp
from jax import lax
from jax.experimental import pallas as pl
from jax.experimental.pallas import tpu as pltpu
from jax.sharding import PartitionSpec as P

SWEEPS = 8
NT = 8
GROUP = 16
CHIPS = 8
PLANES = 4
ROWS = 16
NY = 256
LANES = 128
HALO = 9
EXT = ROWS + 2 * HALO
F32 = jnp.float32
ANY = pl.BlockSpec(memory_space=pl.ANY)
SMEM = pl.BlockSpec(memory_space=pltpu.SMEM)
VMEM = pl.BlockSpec(memory_space=pltpu.VMEM)
DMA = pltpu.SemaphoreType.DMA


def chain_chip(g):
    return g ^ ((g >> 1) & 1)


def chain_place(c):
    return 2 * chain_chip(c >> 1) + (c & 1)


def call(kernel, out_shape, in_specs, out_specs, scratch, megabytes=16, flops=0):
    return pl.pallas_call(
        kernel,
        out_shape=out_shape,
        in_specs=in_specs,
        out_specs=out_specs,
        scratch_shapes=scratch,
        compiler_params=pltpu.CompilerParams(vmem_limit_bytes=megabytes * 1024 * 1024),
        cost_estimate=pl.CostEstimate(flops=flops, bytes_accessed=2**22, transcendentals=0),
    )


def struct(*shape):
    return jax.ShapeDtypeStruct(shape, F32)


def run(todo):
    for copy in todo:
        copy.start()
    for copy in todo:
        copy.wait()


def by_chip(field):
    return field.reshape(PLANES, CHIPS, 2, ROWS, NY)


def pack_first(ids, adjoint, terminal, conductivity, same, other, other_k, sems):
    tm, core = ids[0], ids[2]

    def copies(source):
        source = by_chip(source)
        return [
            pltpu.make_async_copy(source.at[:, :, core], same, sems.at[0]),
            pltpu.make_async_copy(source.at[:, :, 1 - core], other, sems.at[1]),
            pltpu.make_async_copy(
                by_chip(conductivity).at[:, :, 1 - core], other_k, sems.at[2]
            ),
        ]

    @pl.when(tm == 0)
    def _():
        run(copies(terminal))

    @pl.when(tm != 0)
    def _():
        run(copies(adjoint.at[0]))


def pack_states_first(ids, states, rate, other, sems):
    core = ids[2]
    run(
        [
            pltpu.make_async_copy(
                by_chip(field).at[:, :, 1 - core], other.at[at], sems.at[at]
            )
            for at, field in enumerate((states.at[0, 1], states.at[0, 0], rate))
        ]
    )


def pack_conductivity(ids, conductivity, received, *refs):
    outs, sems = refs[:CHIPS], refs[CHIPS]
    chip, core = ids[1], ids[2]
    todo = []
    for step in range(CHIPS):
        place = chain_chip(chip ^ step)
        todo += [
            pltpu.make_async_copy(
                by_chip(conductivity).at[:, place, core], outs[step].at[core], sems.at[0, step]
            ),
            pltpu.make_async_copy(
                received.at[:, place], outs[step].at[1 - core], sems.at[1, step]
            ),
        ]
    run(todo)


def pack_adjoint(ids, same, other, *refs):
    outs, sems = refs[:CHIPS], refs[CHIPS]
    chip, core = ids[1], ids[2]
    todo = []
    for step in range(CHIPS):
        place = chain_chip(chip ^ step)
        todo += [
            pltpu.make_async_copy(same.at[:, place], outs[step].at[core], sems.at[0, step]),
            pltpu.make_async_copy(other.at[:, place], outs[step].at[1 - core], sems.at[1, step]),
        ]
    run(todo)


def pack_states(ids, states, rate, received, *refs):
    outs, sems = refs[:CHIPS], refs[CHIPS]
    chip, core = ids[1], ids[2]
    todo = []
    for step in range(CHIPS):
        place = chain_chip(chip ^ step)
        for at, field in enumerate((states.at[0, 1], states.at[0, 0], rate)):
            todo.append(
                pltpu.make_async_copy(
                    by_chip(field).at[:, place, core], outs[step].at[core, at], sems.at[at, step]
                )
            )
        todo.append(
            pltpu.make_async_copy(
                received.at[:, :, place], outs[step].at[1 - core], sems.at[3, step]
            )
        )
    run(todo)


def fetch_pieces(me, pieces, slots, sems):
    todo = []
    for step, piece in enumerate(pieces):
        every = (slice(None),) * (len(piece.shape) - 1)
        for half in range(2):
            todo.append(
                pltpu.make_async_copy(
                    piece.at[every + (pl.ds(half * LANES, LANES),)],
                    slots.at[half, me ^ step],
                    sems.at[half, step],
                )
            )
    run(todo)


def strided(flat, start, stride):
    return jnp.concatenate(
        [flat[half][pl.ds(start, 8, stride=stride), :] for half in range(2)], axis=1
    )


def halves(slots):
    size = 1
    for extent in slots.shape[1:-1]:
        size *= extent
    return [slots.at[half].reshape(size, LANES) for half in range(2)]


def unpack_field(halo):
    def kernel(ids, *refs):
        pieces = refs[:CHIPS]
        own, up, down, slots, sems = refs[CHIPS:]
        fetch_pieces(ids[1], pieces, slots, sems)
        flat = halves(slots)

        def one_row(row, carry):
            for i in range(8):
                own[row, i] = strided(flat, i * ROWS + row, 8 * ROWS)
            return carry

        lax.fori_loop(0, ROWS, one_row, 0)
        up[...] = own[0:halo]
        down[...] = own[ROWS - halo :]

    return kernel


def unpack_states(ids, *refs):
    pieces = refs[:CHIPS]
    own, decay, up, down, slots, sems = refs[CHIPS:]
    fetch_pieces(ids[1], pieces, slots, sems)
    flat = halves(slots)

    def one_row(row, carry):
        for i in range(8):
            for field in range(3):
                start = (((i // PLANES) * 3 + field) * PLANES + i % PLANES) * ROWS + row
                lines = strided(flat, start, 6 * PLANES * ROWS)
                if field < 2:
                    own[field, row, i] = lines
                else:
                    decay[row, i] = jnp.exp(-lines)
        return carry

    lax.fori_loop(0, ROWS, one_row, 0)
    up[...] = own[:, 0]
    down[...] = own[:, ROWS - 1]


def coefficients(k, kx, ky, kw, kz, diag):
    lane = lax.broadcasted_iota(jnp.int32, (8, NY), 1)
    place = lax.broadcasted_iota(jnp.int32, (8, NY), 0)

    def one_row(e, carry):
        mids = [k[e, i] for i in range(8)]
        last = pltpu.roll(mids[7], 1, 0)
        after = pltpu.roll(mids[0], 7, 0)
        zs = [jnp.where(place == 0, 0.0, 0.5 * (mids[0] + last))]
        zs += [0.5 * (mids[i] + mids[i - 1]) for i in range(1, 8)]
        edge = (lane == 0) | (lane == NY - 1)
        done = []
        for i in range(8):
            mid = mids[i]
            before = jnp.where(lane == 0, 0.0, 0.5 * (mid + pltpu.roll(mid, 1, 1)))
            behind = jnp.where(lane == NY - 1, 0.0, 0.5 * (mid + pltpu.roll(mid, NY - 1, 1)))
            x_low = 0.5 * (mid + k[e - 1, i])
            x_high = 0.5 * (mid + k[e + 1, i])
            extra = jnp.where(edge, 0.5 * mid, 0.0)
            if i == 0:
                extra = extra + jnp.where(place == 0, 0.5 * mid, 0.0)
            if i == 7:
                extra = extra + jnp.where(place == 7, 0.5 * mid, 0.0)
            done.append((x_low, before, behind, 1.0 + extra + (before + behind) + (x_low + x_high)))
        for i in range(8):
            kx[e, i], ky[e, i], kw[e, i], diag[e, i] = done[i]
            kz[e, i] = zs[i]
        return carry

    lax.fori_loop(1, EXT - 1, one_row, 0)
    for i in range(8):
        kx[EXT - 1, i] = 0.5 * (k[EXT - 2, i] + k[EXT - 1, i])


def sweeps(ids, first, weights, d0, d1, r, x, kx, ky, kw, kz, diag):
    at = 2 * chain_chip(ids[1]) + ids[2]
    low = jnp.where(at == 0, HALO, 0)
    high = jnp.where(at == GROUP - 1, HALO + ROWS, EXT)
    start_weight = weights[0]

    def opening(e, carry):
        for i in range(8):
            rhs = d0[e, i]
            r[e, i] = rhs
            begin = rhs * start_weight
            d0[e, i] = begin
            x[e, i] = begin
        return carry

    lax.fori_loop(first, EXT - first, opening, 0)
    zeros = jnp.zeros((8, 8, NY), F32)
    d1[HALO - 1] = zeros
    d1[HALO + ROWS] = zeros

    def one_sweep(step, cur, nxt):
        alpha = weights[1 + 2 * step]
        beta = weights[2 + 2 * step]

        def one_row(e, inner):
            v = [cur[e, i] for i in range(8)]
            head = kz[e, 0] * (v[0] - pltpu.roll(v[7], 1, 0))
            tail = pltpu.roll(head, 7, 0)
            flux = head
            done = []
            for i in range(8):
                mid = v[i]
                flux_next = kz[e, i + 1] * (v[i + 1] - mid) if i < 7 else tail
                total = (
                    diag[e, i] * mid
                    + (flux - flux_next)
                    - kx[e, i] * cur[e - 1, i]
                    - kx[e + 1, i] * cur[e + 1, i]
                    - ky[e, i] * pltpu.roll(mid, 1, 1)
                    - kw[e, i] * pltpu.roll(mid, NY - 1, 1)
                )
                left = r[e, i] - total
                new = alpha * mid + beta * left
                r[e, i] = left
                nxt[e, i] = new
                x[e, i] = x[e, i] + new
                flux = flux_next
            return inner

        begin = jnp.maximum(first + step + 1, low)
        end = jnp.minimum(EXT - first - step - 1, high)

        def some_rows(n, inner):
            for extra in range(4):
                one_row(begin + 4 * n + extra, inner)
            return inner

        full = lax.div(end - begin, 4)
        lax.fori_loop(0, full, some_rows, 0)
        lax.fori_loop(begin + 4 * full, end, one_row, 0)

    def two_sweeps(pair, carry):
        one_sweep(2 * pair, d0, d1)
        one_sweep(2 * pair + 1, d1, d0)
        return carry

    lax.fori_loop(0, SWEEPS // 2, two_sweeps, 0)


FIELD = (EXT, 8, 8, NY)
SOLVE_SCRATCH = [pltpu.VMEM(FIELD, F32) for _ in range(10)] + [DMA((6,)), DMA((3,))]


def solve(halo):
    first = HALO - halo
    last = EXT - first

    def kernel(ids, weights, own_k, above_k, below_k, own, above, below, *refs):
        outs = refs[:-12]
        k, kx, ky, kw, kz, diag, r, x, d0, d1, sems, out_sems = refs[-12:]
        mine = pl.ds(HALO, ROWS)
        fields = [
            pltpu.make_async_copy(above_k, k.at[pl.ds(0, HALO)], sems.at[0]),
            pltpu.make_async_copy(own_k, k.at[mine], sems.at[1]),
            pltpu.make_async_copy(below_k, k.at[pl.ds(HALO + ROWS, HALO)], sems.at[2]),
        ]
        sides = [
            pltpu.make_async_copy(above, d0.at[pl.ds(first, halo)], sems.at[3]),
            pltpu.make_async_copy(own, d0.at[mine], sems.at[4]),
            pltpu.make_async_copy(below, d0.at[pl.ds(HALO + ROWS, halo)], sems.at[5]),
        ]
        for copy in fields + sides:
            copy.start()
        for copy in fields:
            copy.wait()
        coefficients(k, kx, ky, kw, kz, diag)
        for copy in sides:
            copy.wait()
        sweeps(ids, first, weights, d0, d1, r, x, kx, ky, kw, kz, diag)
        if halo == HALO:
            todo = [pltpu.make_async_copy(x.at[pl.ds(HALO - 1, ROWS + 2)], outs[0], out_sems.at[0])]
        else:
            todo = [
                pltpu.make_async_copy(x.at[mine], outs[0], out_sems.at[0]),
                pltpu.make_async_copy(x.at[pl.ds(HALO, HALO)], outs[1], out_sems.at[1]),
                pltpu.make_async_copy(x.at[pl.ds(ROWS, HALO)], outs[2], out_sems.at[2]),
            ]
        run(todo)

    return kernel


def face_rows(w, u, field, out, at, add):
    lane = lax.broadcasted_iota(jnp.int32, (8, NY), 1)
    place = lax.broadcasted_iota(jnp.int32, (8, NY), 0)

    def one_row(row, carry):
        e = row + 1
        vw = [w[e, i] for i in range(8)]
        vu = [u[field, row + 1, i] for i in range(8)]
        back_w = jnp.where(place == 0, 0.0, pltpu.roll(vw[7], 1, 0))
        back_u = jnp.where(place == 0, 0.0, pltpu.roll(vu[7], 1, 0))
        head = (vw[0] - back_w) * (vu[0] - back_u)
        face = head
        for i in range(8):
            if i < 7:
                face_next = (vw[i + 1] - vw[i]) * (vu[i + 1] - vu[i])
            else:
                face_next = jnp.where(place == 7, vw[7] * vu[7], pltpu.roll(head, 7, 0))
            side_w = jnp.where(lane == 0, 0.0, pltpu.roll(vw[i], 1, 1))
            side_u = jnp.where(lane == 0, 0.0, pltpu.roll(vu[i], 1, 1))
            face_y = (vw[i] - side_w) * (vu[i] - side_u)
            far_y = jnp.where(lane == NY - 1, vw[i] * vu[i], pltpu.roll(face_y, NY - 1, 1))
            total = (
                (face + face_next)
                + (face_y + far_y)
                + (vw[i] - w[e - 1, i]) * (vu[i] - u[field, row, i])
                + (vw[i] - w[e + 1, i]) * (vu[i] - u[field, row + 2, i])
            )
            total = -0.5 * total
            for half in range(2):
                part = total[:, half * LANES : (half + 1) * LANES]
                if add:
                    part = out[half, at, row, i] + part
                out[half, at, row, i] = part
            face = face_next
        return carry

    lax.fori_loop(0, ROWS, one_row, 0)


def face_sums(
    ids,
    late,
    late_above,
    late_below,
    early,
    states,
    states_above,
    states_below,
    decay,
    ends,
    *refs,
):
    outs = refs[:NT]
    w, x, u, rate_in, ends_in, pair, parts, sems, out_sems = refs[NT:]
    tm = ids[0]
    inner = pl.ds(1, ROWS)
    todo = [
        pltpu.make_async_copy(late_above.at[HALO - 1], w.at[0], sems.at[0]),
        pltpu.make_async_copy(late, w.at[inner], sems.at[1]),
        pltpu.make_async_copy(late_below.at[0], w.at[ROWS + 1], sems.at[2]),
        pltpu.make_async_copy(states_above, u.at[:, 0], sems.at[3]),
        pltpu.make_async_copy(states, u.at[:, inner], sems.at[4]),
        pltpu.make_async_copy(states_below, u.at[:, ROWS + 1], sems.at[5]),
        pltpu.make_async_copy(early, x, sems.at[6]),
        pltpu.make_async_copy(decay, rate_in, sems.at[7]),
        pltpu.make_async_copy(ends, ends_in, sems.at[8]),
    ]
    run(todo)
    face_rows(w, u, 0, pair, 1, False)
    face_rows(x, u, 1, pair, 1, True)
    keep = jnp.where(tm == NT - 1, 0.0, 1.0)

    def last_row(row, carry):
        for i in range(8):
            value = x[row + 1, i] - keep * (rate_in[row, i] * ends_in[row, i])
            for half in range(2):
                pair[half, 0, row, i] = value[:, half * LANES : (half + 1) * LANES]
        return carry

    lax.fori_loop(0, ROWS, last_row, 0)
    lines = halves(pair)

    def split_row(row, carry):
        for place in range(8):
            for field in range(2):
                start = (field * ROWS + row) * 64 + place
                parts[place, field, row] = strided(lines, start, 8)
        return carry

    lax.fori_loop(0, ROWS, split_row, 0)
    run(
        [
            pltpu.make_async_copy(parts.at[tm ^ step], outs[step], out_sems.at[step])
            for step in range(NT)
        ]
    )


def recur(ids, rate, received, *refs):
    pieces = refs[:NT]
    mine, other, slots, rates, results, sems, out_sems = refs[NT:]
    tm, chip, core = ids[0], ids[1], ids[2]
    place = chain_chip(tm)
    copies = [
        pltpu.make_async_copy(by_chip(rate).at[:, place, core], rates.at[core], out_sems.at[0]),
        pltpu.make_async_copy(received.at[2, :, place], rates.at[1 - core], out_sems.at[1]),
    ]
    for copy in copies:
        copy.start()
    fetch_pieces(chip, pieces, slots, sems)
    for copy in copies:
        copy.wait()
    flat = halves(slots)
    for side in range(2):
        for p in range(8):
            q, plane = p // PLANES, p % PLANES
            rows = pl.ds(8 * side, 8)

            def lines(slab, field):
                start = ((slab * 2 + field) * ROWS + 8 * side) * 8 + p
                return strided(flat, start, 8)

            decay = jnp.exp(-rates[q, plane, rows, :])
            value = lines(NT - 1, 0)
            results[q, NT - 1, plane, rows, :] = value
            for slab in range(NT - 2, -1, -1):
                value = lines(slab, 0) + decay * value
                results[q, slab, plane, rows, :] = value
            summed = lines(0, 1)
            for slab in range(1, NT):
                summed = summed + lines(slab, 1)
            results[q, NT, plane, rows, :] = summed
    run(
        [
            pltpu.make_async_copy(results.at[core], mine, out_sems.at[0]),
            pltpu.make_async_copy(results.at[1 - core], other, out_sems.at[1]),
        ]
    )


def pack_results(ids, mine, received, *refs):
    outs, sems = refs[:NT], refs[NT]
    tm, core = ids[0], ids[2]
    todo = []
    for step in range(NT):
        for field, at in enumerate((tm ^ step, NT)):
            for side, source in ((core, mine), (1 - core, received)):
                rows = pl.ds(pl.multiple_of(ROWS * side, ROWS), ROWS)
                todo.append(
                    pltpu.make_async_copy(
                        source.at[at], outs[step].at[field, :, rows, :], sems.at[len(todo)]
                    )
                )
    run(todo)


def place_results(ids, *refs):
    pieces = refs[:NT]
    adjoint, sensitivity, sems = refs[NT:]
    todo = []
    for step, piece in enumerate(pieces):
        row = pl.multiple_of(chain_chip(ids[0] ^ step) * 2 * ROWS, 2 * ROWS)
        rows = pl.ds(row, 2 * ROWS)
        todo += [
            pltpu.make_async_copy(piece.at[0], adjoint.at[0, :, rows, :], sems.at[0, step]),
            pltpu.make_async_copy(piece.at[1], sensitivity.at[:, rows, :], sems.at[1, step]),
        ]
    run(todo)


def sweep_weights(smallest_eig, largest_eig):
    low, high = smallest_eig[0], largest_eig[0]
    center = (high + low) / 2.0
    radius = (high - low) / 2.0
    scaled = center / radius
    ratio = 1.0 / scaled
    weights = [1.0 / center]
    for _ in range(SWEEPS):
        ratio_next = 1.0 / (2.0 * scaled - ratio)
        weights += [ratio_next * ratio, 2.0 * ratio_next / radius]
        ratio = ratio_next
    return jnp.stack(weights)


def per_device(
    adjoint_iterate,
    forward_states,
    conductivity,
    coarse_rate,
    terminal_adjoint,
    smallest_eig,
    largest_eig,
):
    here = lax.axis_index("space")
    ids = jnp.stack([lax.axis_index("tm"), here // 2, here % 2]).astype(jnp.int32)
    weights = sweep_weights(smallest_eig, largest_eig)
    both = ("tm", "space")
    earlier = [
        [
            (t * GROUP + c, ((t - 1) % NT) * GROUP + (c ^ swap))
            for t in range(NT)
            for c in range(GROUP)
        ]
        for swap in range(2)
    ]
    masks = [[(c, c ^ mask) for c in range(GROUP)] for mask in range(GROUP)]
    forward = [(chain_place(i), chain_place(i + 1)) for i in range(GROUP - 1)]
    backward = [(b, a) for a, b in forward]

    def to_chips(pieces):
        return [pieces[0]] + [
            lax.ppermute(pieces[step], "space", masks[2 * step]) for step in range(1, CHIPS)
        ]

    def along_chain(up, down):
        return lax.ppermute(down, "space", forward), lax.ppermute(up, "space", backward)

    part = (PLANES, CHIPS, ROWS, NY)
    block = (ROWS, 8, 8, NY)
    same, other, other_k = call(
        pack_first, [struct(*part)] * 3, [SMEM] + [ANY] * 3, [VMEM] * 3, [DMA((3,))], 56
    )(ids, adjoint_iterate, terminal_adjoint, conductivity)
    same = lax.ppermute(same, both, earlier[0])
    other = lax.ppermute(other, both, earlier[1])
    other_k = lax.ppermute(other_k, "space", masks[1])

    piece = struct(2, PLANES, ROWS, NY)
    pieces = call(
        pack_conductivity, [piece] * CHIPS, [SMEM, ANY, ANY], [VMEM] * CHIPS, [DMA((2, CHIPS))], 56
    )(ids, conductivity, other_k)

    def unpack(pieces, halo):
        return call(
            unpack_field(halo),
            [struct(*block), struct(halo, 8, 8, NY), struct(halo, 8, 8, NY)],
            [SMEM] + [ANY] * CHIPS,
            [VMEM] * 3,
            [pltpu.VMEM((2, CHIPS, 2, PLANES, ROWS, LANES), F32), DMA((2, CHIPS))],
        )(ids, *pieces)

    own_k, up, down = unpack(to_chips(pieces), HALO)
    above_k, below_k = along_chain(up, down)
    same, other, own_k = lax.optimization_barrier((same, other, own_k))
    pieces = call(
        pack_adjoint, [piece] * CHIPS, [SMEM, ANY, ANY], [VMEM] * CHIPS, [DMA((2, CHIPS))]
    )(ids, same, other)
    ends, up, down = unpack(to_chips(pieces), HALO - 1)
    above, below = along_chain(up, down)

    states, rate, own_k = lax.optimization_barrier((forward_states, coarse_rate, own_k))
    other_states = call(
        pack_states_first, struct(3, *part), [SMEM, ANY, ANY], VMEM, [DMA((3,))], 56
    )(ids, states, rate)
    other_states = lax.ppermute(other_states, "space", masks[1])
    states, rate, ends = lax.optimization_barrier((states, rate, ends))
    pieces = call(
        pack_states,
        [struct(2, 3, PLANES, ROWS, NY)] * CHIPS,
        [SMEM] + [ANY] * 3,
        [VMEM] * CHIPS,
        [DMA((4, CHIPS))],
        56,
    )(ids, states, rate, other_states)
    states, decay, up, down = call(
        unpack_states,
        [struct(2, *block), struct(*block), struct(2, 8, 8, NY), struct(2, 8, 8, NY)],
        [SMEM] + [ANY] * CHIPS,
        [VMEM] * 4,
        [pltpu.VMEM((2, CHIPS, 2, 3, PLANES, ROWS, LANES), F32), DMA((2, CHIPS))],
    )(ids, *to_chips(pieces))
    states_above, states_below = along_chain(up, down)

    late, up, down = call(
        solve(HALO - 1),
        [struct(*block), struct(HALO, 8, 8, NY), struct(HALO, 8, 8, NY)],
        [SMEM] * 2 + [ANY] * 6,
        [ANY] * 3,
        SOLVE_SCRATCH,
        40,
        10**8,
    )(ids, weights, own_k, above_k, below_k, ends, above, below)
    late_above, late_below = along_chain(up, down)
    wide = (ROWS + 2, 8, 8, NY)
    early = call(
        solve(HALO), struct(*wide), [SMEM] * 2 + [ANY] * 6, ANY, SOLVE_SCRATCH, 40, 10**8
    )(ids, weights, own_k, above_k, below_k, late, late_above, late_below)

    pieces = call(
        face_sums,
        [struct(2, ROWS, 8, NY)] * NT,
        [SMEM] + [ANY] * 9,
        [ANY] * NT,
        [
            pltpu.VMEM(wide, F32),
            pltpu.VMEM(wide, F32),
            pltpu.VMEM((2,) + wide, F32),
            pltpu.VMEM(block, F32),
            pltpu.VMEM(block, F32),
            pltpu.VMEM((2, 2, ROWS, 8, 8, LANES), F32),
            pltpu.VMEM((8, 2, ROWS, 8, NY), F32),
            DMA((9,)),
            DMA((NT,)),
        ],
        40,
    )(
        ids,
        late,
        late_above,
        late_below,
        early,
        states,
        states_above,
        states_below,
        decay,
        ends,
    )
    pieces = [
        lax.ppermute(
            pieces[step],
            both,
            [
                (t * GROUP + 2 * g + core, g * GROUP + 2 * (t ^ step) + core)
                for t in range(NT)
                for g in range(CHIPS)
                for core in range(2)
            ],
        )
        for step in range(NT)
    ]
    mine, other = call(
        recur,
        [struct(NT + 1, PLANES, ROWS, NY)] * 2,
        [SMEM] + [ANY] * (NT + 2),
        [ANY] * 2,
        [
            pltpu.VMEM((2, NT, 2, ROWS, 8, LANES), F32),
            pltpu.VMEM((2, PLANES, ROWS, NY), F32),
            pltpu.VMEM((2, NT + 1, PLANES, ROWS, NY), F32),
            DMA((2, NT)),
            DMA((2,)),
        ],
    )(ids, coarse_rate, other_states, *pieces)
    other = lax.ppermute(other, "space", masks[1])
    pieces = call(
        pack_results,
        [struct(2, PLANES, 2 * ROWS, NY)] * NT,
        [SMEM, ANY, ANY],
        [VMEM] * NT,
        [DMA((4 * NT,))],
    )(ids, mine, other)
    pieces = [pieces[0]] + [
        lax.ppermute(pieces[step], "tm", [(t, t ^ step) for t in range(NT)])
        for step in range(1, NT)
    ]
    adjoint_next, sensitivity = call(
        place_results,
        [struct(1, PLANES, NY, NY), struct(PLANES, NY, NY)],
        [SMEM] + [ANY] * NT,
        [VMEM] * 2,
        [DMA((2, NT))],
    )(ids, *pieces)
    return (adjoint_next, sensitivity)


def solution(mesh):
    return jax.shard_map(
        per_device,
        mesh=mesh,
        in_specs=(
            P("tm", "space", None, None),
            P("tm", None, "space", None, None),
            P("space", None, None),
            P("space", None, None),
            P("space", None, None),
            P(),
            P(),
        ),
        out_specs=(P("tm", "space", None, None), P("space", None, None)),
        check_vma=False,
    )
```

time: 569 us -> 305 us (0.54)
  other arithmetic: 122 us -> 0.56 us
  waiting for transfers between devices: 190 us -> 103 us
  starting transfers between devices: 189 us -> 119 us
  Pallas kernels: 0 us -> 67.5 us
  local copies, waits for them, and re-layouts: 41.7 us -> 8.87 us
  between operations: 17.3 us -> 3.31 us
    all_gather x2 -> x0, waiting for transfers between devices: 86.4 us -> none  [entering(): pieces = jax.tree.map(lambda part: lax.all_gather(part, axis), value)]
    ppermute x39 -> x49, starting transfers between devices: 189 us -> 119 us  [the longest x21 43.8 us: to_chips(): lax.ppermute(pieces[step], 'space', masks[2 * step])]
    pallas_call x0 -> x14, Pallas kernels: none -> 67.5 us  [the longest x1 16 us: per_device(): call(solve(HALO), struct(*wide), [SMEM] * 2 + [ANY] * 6, ANY, SOLVE_SCRAT...]
    psum x1 -> x0, waiting for transfers between devices: 62.5 us -> none  [per_device(): sensitivity = lax.psum(local_sens, 'tm')]
    add x15 -> x0, other arithmetic: 62.2 us -> none  [the longest x14 50.7 us: solve_single(): ratio_next * ratio * direction + 2.0 * ratio_next / radius * residual]
    ppermute x39 -> x49, waiting for transfers between devices: 41.1 us -> 103 us  [the longest x21 59.2 us: to_chips(): lax.ppermute(pieces[step], 'space', masks[2 * step])]
    concatenate x19 -> x0, other arithmetic: 28.1 us -> none  [with_halo(): block = jnp.concatenate([low, block, high], axis=dim)]
    select_n x7 -> x0, other arithmetic: 17.5 us -> none  [lap(): jnp.where(position < mine, new, old)]
  transfers between devices with their start and end apart: 42 -> 49, of which waited for: 17 -> 21; matrix products, arithmetic and copies ran while one was open for 19% -> 0% of each run, Pallas kernels for 0% -> 16%
where the time goes in v1:
time: 305 us; the launch traced here: 301 us
  starting transfers between devices  119 us (39%)
  waiting for transfers between devices  103 us (34%)
  Pallas kernels  67.5 us (22%)
  local copies, waits for them, and re-layouts  8.87 us (3%)
  between operations  3.31 us (1%)
    ppermute x21, waiting for transfers between devices, to_chips(): lax.ppermute(pieces[step], 'space', masks[2 * step])  59.2 us
    ppermute x21, starting transfers between devices, to_chips(): lax.ppermute(pieces[step], 'space', masks[2 * step])  43.8 us
    ppermute x8, starting transfers between devices, per_device(): lax.ppermute(pieces[step], both, [(t * GROUP + 2 * g + core, g * GROUP +...  38.5 us
    ppermute x7, waiting for transfers between devices, per_device(): lax.ppermute(pieces[step], 'tm', [(t, t ^ step) for t in range(NT)])  21.3 us
    ppermute x8, waiting for transfers between devices, per_device(): lax.ppermute(pieces[step], both, [(t * GROUP + 2 * g + core, g * GROUP +...  20.1 us
    ppermute x7, starting transfers between devices, per_device(): lax.ppermute(pieces[step], 'tm', [(t, t ^ step) for t in range(NT)])  17.1 us
    pallas_call x1, Pallas kernels, per_device(): call(solve(HALO), struct(*wide), [SMEM] * 2 + [ANY] * 6, ANY, SOLVE_SCRAT...  16 us
    pallas_call x1, Pallas kernels, per_device(): call(solve(HALO - 1), [struct(*block), struct(HALO, 8, 8, NY), struct(HAL...  15.3 us
  transfers between devices with their start and end apart: 49, of which 21 were waited for; matrix products, arithmetic and copies ran while one was open for 0% of the time, Pallas kernels for 16%

profile of v1, /device:TPU:0, one launch (start us, length us, event | category | flops | bytes accessed | tf_op | source)
XLA Modules:
  0.0 301.5 jit_solution(14238052873366296121)
XLA Ops:
  1.2 3.2 %shard_map.86 = (f32[4,8,16,256]{3,2,1,0:T(8,128)}, f32[4,8,16,256]{3,2,1,0:T(8,128)}, f32[4,8,16,256]{3,2,1,0:T(8,128)}) custom-call(s32[3]{0:T(128)} %pad_add_fusion.ids, f32[1,4,256,256]{3,2,1,0:T(8,128)} %adjoint.1, f32[4,256,256]{2,1,0:T(8,128)} %terminal.1, f32[4,256,256]{2,1,0:T(8,128)} %conductivity.3), custom_call_target="tpu_custom_call" | custom-call | bytes 4194304 | tf_op jit(solution)/shard_map/pallas_call | solution.py:578
  4.5 6.5 %collective-permute-start = (f32[4,8,16,256]{3,2,1,0:T(8,128)}, f32[4,8,16,256]{3,2,1,0:T(8,128)S(1)}, u32[]{:S(2)}, u32[]{:S(2)}) collective-permute-start(f32[4,8,16,256]{3,2,1,0:T(8,128)} %get-tuple-element.69), channel_id=1, source_target_pairs={{0,112},{1,113},{2,114},{3,115},{4,116},{5,117},{6,118},{7,119},{8... | collective-permute-start | bytes 1572872 | tf_op jit(solution)/shard_map/ppermute | solution.py:581
  11.9 3.0 %shard_map.87 = (f32[2,4,16,256]{3,2,1,0:T(8,128)}, f32[2,4,16,256]{3,2,1,0:T(8,128)}, f32[2,4,16,256]{3,2,1,0:T(8,128)}, f32[2,4,16,256]{3,2,1,0:T(8,128)}, f32...) custom-call(s32[3]{0:T(128)} %pad_add_fusion.ids, ...), custom_call_target="tpu_custom_call" | custom-call | bytes 4194304 | tf_op jit(solution)/shard_map/pallas_call | solution.py:586
  18.5 21.3 %collective-permute-done.3.refs_1_ = f32[2,4,16,256]{3,2,1,0:T(8,128)S(1)} collective-permute-done((f32[2,4,16,256]{3,2,1,0:T(8,128)}, f32[2,4,16,256]{3,2,1,0:T(8,128)S(1)}, u32[]{:S(2)}, u32[]{:S(2)}) %collective-permute-start.3) | collective-permute-done | bytes 131104 | tf_op jit(solution)/shard_map/ppermute | solution.py:570
  47.0 4.1 %collective-permute-start.9 = (f32[2,4,16,256]{3,2,1,0:T(8,128)}, f32[2,4,16,256]{3,2,1,0:T(8,128)S(1)}, u32[]{:S(2)}, u32[]{:S(2)}) collective-permute-start(f32[2,4,16,256]{3,2,1,0:T(8,128)} %get-tuple-element.79), channel_id=1, source_target_pairs={{0,14},{1,15},{2,12},{3,13},{4,10},{5,11},{6,8},{7,9},{8,6},{9,7},... | collective-permute-start | bytes 393224 | tf_op jit(solution)/shard_map/ppermute | solution.py:570
  53.0 3.1 %collective-permute-done.9.refs_7_ = f32[2,4,16,256]{3,2,1,0:T(8,128)S(1)} collective-permute-done((f32[2,4,16,256]{3,2,1,0:T(8,128)}, f32[2,4,16,256]{3,2,1,0:T(8,128)S(1)}, u32[]{:S(2)}, u32[]{:S(2)}) %collective-permute-start.9) | collective-permute-done | bytes 131104 | tf_op jit(solution)/shard_map/ppermute | solution.py:570
  59.6 3.3 %shard_map.89 = f32[3,4,8,16,256]{4,3,2,1,0:T(8,128)} custom-call(s32[3]{0:T(128)} %pad_add_fusion.ids, f32[1,2,4,256,256]{4,3,2,1,0:T(8,128)} %states.1, f32[4,256,256]{2,1,0:T(8,128)} %rate.3), custom_call_target="tpu_custom_call" | custom-call | bytes 4194304 | tf_op jit(solution)/shard_map/pallas_call | solution.py:609
  84.0 3.2 %collective-permute-done.19.refs_7_ = f32[2,4,16,256]{3,2,1,0:T(8,128)S(1)} collective-permute-done((f32[2,4,16,256]{3,2,1,0:T(8,128)S(1)}, f32[2,4,16,256]{3,2,1,0:T(8,128)S(1)}, u32[]{:S(2)}, u32[]{:S(2)}) %collective-permute-start.19) | collective-permute-done | bytes 131104 | tf_op jit(solution)/shard_map/ppermute | solution.py:570
  93.9 4.5 %shard_map.94 = (f32[2,3,4,16,256]{4,3,2,1,0:T(8,128)}, f32[2,3,4,16,256]{4,3,2,1,0:T(8,128)}, f32[2,3,4,16,256]{4,3,2,1,0:T(8,128)}, f32[2,3,4,16,256]{4,3,2,1,...) custom-call(s32[3]{0:T(128)} %pad_add_fusion.ids, ...), custom_call_target="tpu_custom_call" | custom-call | bytes 4194304 | tf_op jit(solution)/shard_map/pallas_call | solution.py:614
  98.5 3.5 %collective-permute-start.24 = (f32[2,3,4,16,256]{4,3,2,1,0:T(8,128)}, f32[2,3,4,16,256]{4,3,2,1,0:T(8,128)S(1)}, u32[]{:S(2)}, u32[]{:S(2)}) collective-permute-start(f32[2,3,4,16,256]{4,3,2,1,0:T(8,128)} %get-tuple-element.107), channel_id=1, source_target_pairs={{0,2},{1,3},{2,0},{3,1},{4,6},{5,7},{6,4},{7,5},{8,10},{9,11},{10,... | collective-permute-start | bytes 1179656 | tf_op jit(solution)/shard_map/ppermute | solution.py:570
  111.9 15.3 %shard_map.92 = (f32[16,8,8,256]{3,2,1,0:T(8,128)S(1)}, f32[9,8,8,256]{3,2,1,0:T(8,128)S(1)}, f32[9,8,8,256]{3,2,1,0:T(8,128)S(1)}) custom-call(s32[3]{0:T(128)S(1)} %copy-done.14, f32[17]{0:T(128)S(1)} %stack.87.weights, f32[16,8,8,256]{3,2,1,0:T(8,128)S(1)} %copy-done.4, f32[9,8,8,256]{3,2,1,0:T(8,128)S(1)} %collective-permute-done.11.above_k, ...), custom_call_target="tpu_custom_call" | custom-call | flops 100000000 | bytes 4194304 | tf_op jit(solution)/shard_map/pallas_call | solution.py:631
  130.9 7.2 %collective-permute-start.28 = (f32[2,3,4,16,256]{4,3,2,1,0:T(8,128)S(1)}, f32[2,3,4,16,256]{4,3,2,1,0:T(8,128)S(1)}, u32[]{:S(2)}, u32[]{:S(2)}) collective-permute-start(f32[2,3,4,16,256]{4,3,2,1,0:T(8,128)S(1)} %copy-done.18), channel_id=1, source_target_pairs={{0,10},{1,11},{2,8},{3,9},{4,14},{5,15},{6,12},{7,13},{8,2},{9,3},... | collective-permute-start | bytes 1179656 | tf_op jit(solution)/shard_map/ppermute | solution.py:570
  140.9 7.4 %collective-permute-done.28.refs_5_ = f32[2,3,4,16,256]{4,3,2,1,0:T(8,128)S(1)} collective-permute-done((f32[2,3,4,16,256]{4,3,2,1,0:T(8,128)S(1)}, f32[2,3,4,16,256]{4,3,2,1,0:T(8,128)S(1)}, u32[]{:S(2)}, u32[]{:S(2)}) %collective-permute-start.28) | collective-permute-done | bytes 393248 | tf_op jit(solution)/shard_map/ppermute | solution.py:570
  148.3 7.3 %collective-permute-done.29.refs_6_ = f32[2,3,4,16,256]{4,3,2,1,0:T(8,128)S(1)} collective-permute-done((f32[2,3,4,16,256]{4,3,2,1,0:T(8,128)S(1)}, f32[2,3,4,16,256]{4,3,2,1,0:T(8,128)S(1)}, u32[]{:S(2)}, u32[]{:S(2)}) %collective-permute-start.29) | collective-permute-done | bytes 393248 | tf_op jit(solution)/shard_map/ppermute | solution.py:570
  155.6 10.3 %collective-permute-done.30.refs_7_ = f32[2,3,4,16,256]{4,3,2,1,0:T(8,128)S(1)} collective-permute-done((f32[2,3,4,16,256]{4,3,2,1,0:T(8,128)S(1)}, f32[2,3,4,16,256]{4,3,2,1,0:T(8,128)S(1)}, u32[]{:S(2)}, u32[]{:S(2)}) %collective-permute-start.30) | collective-permute-done | bytes 393248 | tf_op jit(solution)/shard_map/ppermute | solution.py:570
  165.9 3.1 %shard_map.95 = (f32[2,16,8,8,256]{4,3,2,1,0:T(8,128)S(1)}, f32[16,8,8,256]{3,2,1,0:T(8,128)S(1)}, f32[2,8,8,256]{3,2,1,0:T(8,128)S(1)}, f32[2,8,8,256]{3,2,1,0:T(8,128)S(1)}) custom-call(s32[3]{0:T(128)S(1)} %copy-done.14, f32[2,3,4,16,256]{4,3,2,1,0:T(8,128)S(1)} %copy-done.10, f32[2,3,4,16,256]{4,3,2,1,0:T(8,128)S(1)} %collective-permute-done.24.refs_1_, ...), custom_call_target="tpu_custom_call" | custom-call | bytes 4194304 | tf_op jit(solution)/shard_map/pallas_call | solution.py:622
  172.1 16.0 %shard_map.93.early = f32[18,8,8,256]{3,2,1,0:T(8,128)S(1)} custom-call(s32[3]{0:T(128)S(1)} %copy-done.14, f32[17]{0:T(128)S(1)} %stack.87.weights, f32[16,8,8,256]{3,2,1,0:T(8,128)S(1)} %copy-done.4, f32[9,8,8,256]{3,2,1,0:T(8,128)S(1)} %collective-permute-done.11.above_k, f32[9,8,8,256]{3,2,1,0:T(8,128)S(1)} %copy-done.7, ...), custom_call_target="tpu_custom_call" | custom-call | flops 100000000 | bytes 4194304 | tf_op jit(solution)/shard_map/pallas_call | solution.py:642
  188.1 8.2 %shard_map.96 = (f32[2,16,8,256]{3,2,1,0:T(8,128)S(1)}, f32[2,16,8,256]{3,2,1,0:T(8,128)S(1)}, f32[2,16,8,256]{3,2,1,0:T(8,128)S(1)}, f32[2,16,8,256]{3,2,1,0:T(...) custom-call(s32[3]{0:T(128)S(1)} %copy-done.14, ...), custom_call_target="tpu_custom_call" | custom-call | bytes 4194304 | tf_op jit(solution)/shard_map/pallas_call | solution.py:646
  197.1 5.5 %collective-permute-start.34 = (f32[2,16,8,256]{3,2,1,0:T(8,128)S(1)}, f32[2,16,8,256]{3,2,1,0:T(8,128)S(1)}, u32[]{:S(2)}, u32[]{:S(2)}) collective-permute-start(f32[2,16,8,256]{3,2,1,0:T(8,128)S(1)} %get-tuple-element.119), channel_id=1, source_target_pairs={{0,2},{1,3},{2,18},{3,19},{4,34},{5,35},{6,50},{7,51},{8,66},{9,67... | collective-permute-start | bytes 786440 | tf_op jit(solution)/shard_map/ppermute | solution.py:676
  205.1 5.8 %collective-permute-start.36 = (f32[2,16,8,256]{3,2,1,0:T(8,128)S(1)}, f32[2,16,8,256]{3,2,1,0:T(8,128)S(1)}, u32[]{:S(2)}, u32[]{:S(2)}) collective-permute-start(f32[2,16,8,256]{3,2,1,0:T(8,128)S(1)} %get-tuple-element.121), channel_id=1, source_target_pairs={{0,6},{1,7},{2,22},{3,23},{4,38},{5,39},{6,54},{7,55},{8,70},{9,71... | collective-permute-start | bytes 786440 | tf_op jit(solution)/shard_map/ppermute | solution.py:676
  210.9 8.9 %collective-permute-start.37 = (f32[2,16,8,256]{3,2,1,0:T(8,128)S(1)}, f32[2,16,8,256]{3,2,1,0:T(8,128)S(1)}, u32[]{:S(2)}, u32[]{:S(2)}) collective-permute-start(f32[2,16,8,256]{3,2,1,0:T(8,128)S(1)} %get-tuple-element.122), channel_id=1, source_target_pairs={{0,8},{1,9},{2,24},{3,25},{4,40},{5,41},{6,56},{7,57},{8,72},{9,73... | collective-permute-start | bytes 786440 | tf_op jit(solution)/shard_map/ppermute | solution.py:676
  219.8 5.1 %collective-permute-start.38 = (f32[2,16,8,256]{3,2,1,0:T(8,128)S(1)}, f32[2,16,8,256]{3,2,1,0:T(8,128)S(1)}, u32[]{:S(2)}, u32[]{:S(2)}) collective-permute-start(f32[2,16,8,256]{3,2,1,0:T(8,128)S(1)} %get-tuple-element.123), channel_id=1, source_target_pairs={{0,10},{1,11},{2,26},{3,27},{4,42},{5,43},{6,58},{7,59},{8,74},{9,... | collective-permute-start | bytes 786440 | tf_op jit(solution)/shard_map/ppermute | solution.py:676
  224.9 10.0 %collective-permute-start.39 = (f32[2,16,8,256]{3,2,1,0:T(8,128)S(1)}, f32[2,16,8,256]{3,2,1,0:T(8,128)S(1)}, u32[]{:S(2)}, u32[]{:S(2)}) collective-permute-start(f32[2,16,8,256]{3,2,1,0:T(8,128)S(1)} %get-tuple-element.124), channel_id=1, source_target_pairs={{0,12},{1,13},{2,28},{3,29},{4,44},{5,45},{6,60},{7,61},{8,76},{9,... | collective-permute-start | bytes 786440 | tf_op jit(solution)/shard_map/ppermute | solution.py:676
  234.9 3.3 %collective-permute-done.38.refs_5_ = f32[2,16,8,256]{3,2,1,0:T(8,128)S(1)} collective-permute-done((f32[2,16,8,256]{3,2,1,0:T(8,128)S(1)}, f32[2,16,8,256]{3,2,1,0:T(8,128)S(1)}, u32[]{:S(2)}, u32[]{:S(2)}) %collective-permute-start.38) | collective-permute-done | bytes 262176 | tf_op jit(solution)/shard_map/ppermute | solution.py:676
  238.2 13.1 %collective-permute-done.39.refs_6_ = f32[2,16,8,256]{3,2,1,0:T(8,128)S(1)} collective-permute-done((f32[2,16,8,256]{3,2,1,0:T(8,128)S(1)}, f32[2,16,8,256]{3,2,1,0:T(8,128)S(1)}, u32[]{:S(2)}, u32[]{:S(2)}) %collective-permute-start.39) | collective-permute-done | bytes 262176 | tf_op jit(solution)/shard_map/ppermute | solution.py:676
  251.3 3.6 %collective-permute-done.40.refs_7_ = f32[2,16,8,256]{3,2,1,0:T(8,128)S(1)} collective-permute-done((f32[2,16,8,256]{3,2,1,0:T(8,128)S(1)}, f32[2,16,8,256]{3,2,1,0:T(8,128)S(1)}, u32[]{:S(2)}, u32[]{:S(2)}) %collective-permute-start.40) | collective-permute-done | bytes 262176 | tf_op jit(solution)/shard_map/ppermute | solution.py:676
  260.7 4.4 %collective-permute-start.43 = (f32[2,4,32,256]{3,2,1,0:T(8,128)S(1)}, f32[2,4,32,256]{3,2,1,0:T(8,128)S(1)}, u32[]{:S(2)}, u32[]{:S(2)}) collective-permute-start(f32[2,4,32,256]{3,2,1,0:T(8,128)S(1)} %get-tuple-element.130), channel_id=1, source_target_pairs={{0,32},{16,48},{32,0},{48,16},{64,96},{80,112},{96,64},{112,80},{1... | collective-permute-start | bytes 786440 | tf_op jit(solution)/shard_map/ppermute | solution.py:710
  267.3 3.1 %collective-permute-start.45 = (f32[2,4,32,256]{3,2,1,0:T(8,128)S(1)}, f32[2,4,32,256]{3,2,1,0:T(8,128)S(1)}, u32[]{:S(2)}, u32[]{:S(2)}) collective-permute-start(f32[2,4,32,256]{3,2,1,0:T(8,128)S(1)} %get-tuple-element.132), channel_id=1, source_target_pairs={{0,64},{16,80},{32,96},{48,112},{64,0},{80,16},{96,32},{112,48},{1... | collective-permute-start | bytes 786440 | tf_op jit(solution)/shard_map/ppermute | solution.py:710
  271.0 4.2 %collective-permute-start.47 = (f32[2,4,32,256]{3,2,1,0:T(8,128)S(1)}, f32[2,4,32,256]{3,2,1,0:T(8,128)S(1)}, u32[]{:S(2)}, u32[]{:S(2)}) collective-permute-start(f32[2,4,32,256]{3,2,1,0:T(8,128)S(1)} %get-tuple-element.134), channel_id=1, source_target_pairs={{0,96},{16,112},{32,64},{48,80},{64,32},{80,48},{96,0},{112,16},{1... | collective-permute-start | bytes 786440 | tf_op jit(solution)/shard_map/ppermute | solution.py:710
  280.1 5.1 %collective-permute-done.45.refs_4_ = f32[2,4,32,256]{3,2,1,0:T(8,128)S(1)} collective-permute-done((f32[2,4,32,256]{3,2,1,0:T(8,128)S(1)}, f32[2,4,32,256]{3,2,1,0:T(8,128)S(1)}, u32[]{:S(2)}, u32[]{:S(2)}) %collective-permute-start.45) | collective-permute-done | bytes 262176 | tf_op jit(solution)/shard_map/ppermute | solution.py:710
  285.2 7.7 %collective-permute-done.46.refs_5_ = f32[2,4,32,256]{3,2,1,0:T(8,128)S(1)} collective-permute-done((f32[2,4,32,256]{3,2,1,0:T(8,128)S(1)}, f32[2,4,32,256]{3,2,1,0:T(8,128)S(1)}, u32[]{:S(2)}, u32[]{:S(2)}) %collective-permute-start.46) | collective-permute-done | bytes 262176 | tf_op jit(solution)/shard_map/ppermute | solution.py:710
  293.7 4.9 %collective-permute-done.48.refs_7_ = f32[2,4,32,256]{3,2,1,0:T(8,128)S(1)} collective-permute-done((f32[2,4,32,256]{3,2,1,0:T(8,128)S(1)}, f32[2,4,32,256]{3,2,1,0:T(8,128)S(1)}, u32[]{:S(2)}, u32[]{:S(2)}) %collective-permute-start.48) | collective-permute-done | bytes 262176 | tf_op jit(solution)/shard_map/ppermute | solution.py:710
  (120 shorter events, 82.8 us)
Async XLA Ops:
  4.5 55.1 %collective-permute-start = (f32[4,8,16,256]{3,2,1,0:T(8,128)}, f32[4,8,16,256]{3,2,1,0:T(8,128)S(1)}, u32[]{:S(2)}, u32[]{:S(2)}) collective-permute-start(f32[4,8,16,256]{3,2,1,0:T(8,128)} %get-tuple-element.69), channel_id=1, source_target_pairs={{0,112},{1,113},{2,114},{3,115},{4,116},{5,117},{6,118},{7,119},{8... | collective-permute-start | bytes 1572872 | tf_op jit(solution)/shard_map/ppermute | solution.py:581
  11.0 48.6 %collective-permute-start.1 = (f32[4,8,16,256]{3,2,1,0:T(8,128)}, f32[4,8,16,256]{3,2,1,0:T(8,128)S(1)}, u32[]{:S(2)}, u32[]{:S(2)}) collective-permute-start(f32[4,8,16,256]{3,2,1,0:T(8,128)} %get-tuple-element.70), channel_id=1, source_target_pairs={{0,113},{1,112},{2,115},{3,114},{4,117},{5,116},{6,119},{7,118},{8... | collective-permute-start | bytes 1572872 | tf_op jit(solution)/shard_map/ppermute | solution.py:582
  14.9 24.9 %collective-permute-start.3 = (f32[2,4,16,256]{3,2,1,0:T(8,128)}, f32[2,4,16,256]{3,2,1,0:T(8,128)S(1)}, u32[]{:S(2)}, u32[]{:S(2)}) collective-permute-start(f32[2,4,16,256]{3,2,1,0:T(8,128)} %get-tuple-element.73), channel_id=1, source_target_pairs={{0,2},{1,3},{2,0},{3,1},{4,6},{5,7},{6,4},{7,5},{8,10},{9,11},{10,... | collective-permute-start | bytes 393224 | tf_op jit(solution)/shard_map/ppermute | solution.py:570
  16.2 26.5 %collective-permute-start.4 = (f32[2,4,16,256]{3,2,1,0:T(8,128)}, f32[2,4,16,256]{3,2,1,0:T(8,128)S(1)}, u32[]{:S(2)}, u32[]{:S(2)}) collective-permute-start(f32[2,4,16,256]{3,2,1,0:T(8,128)} %get-tuple-element.74), channel_id=1, source_target_pairs={{0,4},{1,5},{2,6},{3,7},{4,0},{5,1},{6,2},{7,3},{8,12},{9,13},{10,... | collective-permute-start | bytes 393224 | tf_op jit(solution)/shard_map/ppermute | solution.py:570
  17.7 26.0 %collective-permute-start.5 = (f32[2,4,16,256]{3,2,1,0:T(8,128)}, f32[2,4,16,256]{3,2,1,0:T(8,128)S(1)}, u32[]{:S(2)}, u32[]{:S(2)}) collective-permute-start(f32[2,4,16,256]{3,2,1,0:T(8,128)} %get-tuple-element.75), channel_id=1, source_target_pairs={{0,6},{1,7},{2,4},{3,5},{4,2},{5,3},{6,0},{7,1},{8,14},{9,15},{10,... | collective-permute-start | bytes 393224 | tf_op jit(solution)/shard_map/ppermute | solution.py:570
  62.9 29.9 %collective-permute-start.10 = (f32[3,4,8,16,256]{4,3,2,1,0:T(8,128)}, f32[3,4,8,16,256]{4,3,2,1,0:T(8,128)S(1)}, u32[]{:S(2)}, u32[]{:S(2)}) collective-permute-start(f32[3,4,8,16,256]{4,3,2,1,0:T(8,128)} %shard_map.89), channel_id=1, source_target_pairs={{0,1},{1,0},{2,3},{3,2},{4,5},{5,4},{6,7},{7,6},{8,9},{9,8},{10,11... | collective-permute-start | bytes 4718600 | tf_op jit(solution)/shard_map/ppermute | solution.py:612
  79.1 22.9 %collective-permute-start.11 = (f32[9,8,8,256]{3,2,1,0:T(8,128)S(1)}, f32[9,8,8,256]{3,2,1,0:T(8,128)S(1)}, u32[]{:S(2)}, u32[]{:S(2)}) collective-permute-start(f32[9,8,8,256]{3,2,1,0:T(8,128)S(1)} %get-tuple-element.85), channel_id=1, source_target_pairs={{0,1},{1,2},{2,3},{3,6},{6,7},{7,4},{4,5},{5,8},{8,9},{9,10},{10,1... | collective-permute-start | bytes 1769480 | tf_op jit(solution)/shard_map/ppermute | solution.py:574
  81.6 20.4 %collective-permute-start.12 = (f32[9,8,8,256]{3,2,1,0:T(8,128)S(1)}, f32[9,8,8,256]{3,2,1,0:T(8,128)S(1)}, u32[]{:S(2)}, u32[]{:S(2)}) collective-permute-start(f32[9,8,8,256]{3,2,1,0:T(8,128)S(1)} %get-tuple-element.86), channel_id=1, source_target_pairs={{1,0},{2,1},{3,2},{6,3},{7,6},{4,7},{5,4},{8,5},{9,8},{10,9},{11,1... | collective-permute-start | bytes 1769480 | tf_op jit(solution)/shard_map/ppermute | solution.py:574
  91.5 17.1 %collective-permute-start.21 = (f32[8,8,8,256]{3,2,1,0:T(8,128)}, f32[8,8,8,256]{3,2,1,0:T(8,128)}, u32[]{:S(2)}, u32[]{:S(2)}) collective-permute-start(f32[8,8,8,256]{3,2,1,0:T(8,128)} %get-tuple-element.100), channel_id=1, source_target_pairs={{1,0},{2,1},{3,2},{6,3},{7,6},{4,7},{5,4},{8,5},{9,8},{10,9},{11,1... | collective-permute-start | bytes 1572872 | tf_op jit(solution)/shard_map/ppermute | solution.py:574
  98.5 31.1 %collective-permute-start.24 = (f32[2,3,4,16,256]{4,3,2,1,0:T(8,128)}, f32[2,3,4,16,256]{4,3,2,1,0:T(8,128)S(1)}, u32[]{:S(2)}, u32[]{:S(2)}) collective-permute-start(f32[2,3,4,16,256]{4,3,2,1,0:T(8,128)} %get-tuple-element.107), channel_id=1, source_target_pairs={{0,2},{1,3},{2,0},{3,1},{4,6},{5,7},{6,4},{7,5},{8,10},{9,11},{10,... | collective-permute-start | bytes 1179656 | tf_op jit(solution)/shard_map/ppermute | solution.py:570
  102.0 28.9 %collective-permute-start.25 = (f32[2,3,4,16,256]{4,3,2,1,0:T(8,128)}, f32[2,3,4,16,256]{4,3,2,1,0:T(8,128)S(1)}, u32[]{:S(2)}, u32[]{:S(2)}) collective-permute-start(f32[2,3,4,16,256]{4,3,2,1,0:T(8,128)} %get-tuple-element.108), channel_id=1, source_target_pairs={{0,4},{1,5},{2,6},{3,7},{4,0},{5,1},{6,2},{7,3},{8,12},{9,13},{10,... | collective-permute-start | bytes 1179656 | tf_op jit(solution)/shard_map/ppermute | solution.py:570
  102.8 35.3 %collective-permute-start.26 = (f32[2,3,4,16,256]{4,3,2,1,0:T(8,128)}, f32[2,3,4,16,256]{4,3,2,1,0:T(8,128)S(1)}, u32[]{:S(2)}, u32[]{:S(2)}) collective-permute-start(f32[2,3,4,16,256]{4,3,2,1,0:T(8,128)} %get-tuple-element.109), channel_id=1, source_target_pairs={{0,6},{1,7},{2,4},{3,5},{4,2},{5,3},{6,0},{7,1},{8,14},{9,15},{10,... | collective-permute-start | bytes 1179656 | tf_op jit(solution)/shard_map/ppermute | solution.py:570
  105.2 33.7 %collective-permute-start.27 = (f32[2,3,4,16,256]{4,3,2,1,0:T(8,128)}, f32[2,3,4,16,256]{4,3,2,1,0:T(8,128)S(1)}, u32[]{:S(2)}, u32[]{:S(2)}) collective-permute-start(f32[2,3,4,16,256]{4,3,2,1,0:T(8,128)} %get-tuple-element.110), channel_id=1, source_target_pairs={{0,8},{1,9},{2,10},{3,11},{4,12},{5,13},{6,14},{7,15},{8,0},{9,1},... | collective-permute-start | bytes 1179656 | tf_op jit(solution)/shard_map/ppermute | solution.py:570
  127.2 44.9 %collective-permute-start.22 = (f32[9,8,8,256]{3,2,1,0:T(8,128)S(1)}, f32[9,8,8,256]{3,2,1,0:T(8,128)S(1)}, u32[]{:S(2)}, u32[]{:S(2)}) collective-permute-start(f32[9,8,8,256]{3,2,1,0:T(8,128)S(1)} %get-tuple-element.102), channel_id=1, source_target_pairs={{0,1},{1,2},{2,3},{3,6},{6,7},{7,4},{4,5},{5,8},{8,9},{9,10},{10,1... | collective-permute-start | bytes 1769480 | tf_op jit(solution)/shard_map/ppermute | solution.py:574
  129.6 42.5 %collective-permute-start.23 = (f32[9,8,8,256]{3,2,1,0:T(8,128)S(1)}, f32[9,8,8,256]{3,2,1,0:T(8,128)S(1)}, u32[]{:S(2)}, u32[]{:S(2)}) collective-permute-start(f32[9,8,8,256]{3,2,1,0:T(8,128)S(1)} %get-tuple-element.103), channel_id=1, source_target_pairs={{1,0},{2,1},{3,2},{6,3},{7,6},{4,7},{5,4},{8,5},{9,8},{10,9},{11,1... | collective-permute-start | bytes 1769480 | tf_op jit(solution)/shard_map/ppermute | solution.py:574
  130.9 17.4 %collective-permute-start.28 = (f32[2,3,4,16,256]{4,3,2,1,0:T(8,128)S(1)}, f32[2,3,4,16,256]{4,3,2,1,0:T(8,128)S(1)}, u32[]{:S(2)}, u32[]{:S(2)}) collective-permute-start(f32[2,3,4,16,256]{4,3,2,1,0:T(8,128)S(1)} %copy-done.18), channel_id=1, source_target_pairs={{0,10},{1,11},{2,8},{3,9},{4,14},{5,15},{6,12},{7,13},{8,2},{9,3},... | collective-permute-start | bytes 1179656 | tf_op jit(solution)/shard_map/ppermute | solution.py:570
  138.1 17.5 %collective-permute-start.29 = (f32[2,3,4,16,256]{4,3,2,1,0:T(8,128)S(1)}, f32[2,3,4,16,256]{4,3,2,1,0:T(8,128)S(1)}, u32[]{:S(2)}, u32[]{:S(2)}) collective-permute-start(f32[2,3,4,16,256]{4,3,2,1,0:T(8,128)S(1)} %copy-done.17), channel_id=1, source_target_pairs={{0,12},{1,13},{2,14},{3,15},{4,8},{5,9},{6,10},{7,11},{8,4},{9,5},... | collective-permute-start | bytes 1179656 | tf_op jit(solution)/shard_map/ppermute | solution.py:570
  138.8 27.0 %collective-permute-start.30 = (f32[2,3,4,16,256]{4,3,2,1,0:T(8,128)S(1)}, f32[2,3,4,16,256]{4,3,2,1,0:T(8,128)S(1)}, u32[]{:S(2)}, u32[]{:S(2)}) collective-permute-start(f32[2,3,4,16,256]{4,3,2,1,0:T(8,128)S(1)} %copy-done.16), channel_id=1, source_target_pairs={{0,14},{1,15},{2,12},{3,13},{4,10},{5,11},{6,8},{7,9},{8,6},{9,7},... | collective-permute-start | bytes 1179656 | tf_op jit(solution)/shard_map/ppermute | solution.py:570
  169.0 19.0 %collective-permute-start.31 = (f32[2,8,8,256]{3,2,1,0:T(8,128)S(1)}, f32[2,8,8,256]{3,2,1,0:T(8,128)S(1)}, u32[]{:S(2)}, u32[]{:S(2)}) collective-permute-start(f32[2,8,8,256]{3,2,1,0:T(8,128)S(1)} %get-tuple-element.115), channel_id=1, source_target_pairs={{0,1},{1,2},{2,3},{3,6},{6,7},{7,4},{4,5},{5,8},{8,9},{9,10},{10,1... | collective-permute-start | bytes 393224 | tf_op jit(solution)/shard_map/ppermute | solution.py:574
  170.6 17.5 %collective-permute-start.32 = (f32[2,8,8,256]{3,2,1,0:T(8,128)S(1)}, f32[2,8,8,256]{3,2,1,0:T(8,128)S(1)}, u32[]{:S(2)}, u32[]{:S(2)}) collective-permute-start(f32[2,8,8,256]{3,2,1,0:T(8,128)S(1)} %get-tuple-element.116), channel_id=1, source_target_pairs={{1,0},{2,1},{3,2},{6,3},{7,6},{4,7},{5,4},{8,5},{9,8},{10,9},{11,1... | collective-permute-start | bytes 393224 | tf_op jit(solution)/shard_map/ppermute | solution.py:574
  196.4 23.4 %collective-permute-start.33 = (f32[2,16,8,256]{3,2,1,0:T(8,128)S(1)}, f32[2,16,8,256]{3,2,1,0:T(8,128)S(1)}, u32[]{:S(2)}, u32[]{:S(2)}) collective-permute-start(f32[2,16,8,256]{3,2,1,0:T(8,128)S(1)} %get-tuple-element.118), channel_id=1, source_target_pairs={{0,0},{1,1},{2,16},{3,17},{4,32},{5,33},{6,48},{7,49},{8,64},{9,65... | collective-permute-start | bytes 786440 | tf_op jit(solution)/shard_map/ppermute | solution.py:676
  197.1 27.8 %collective-permute-start.34 = (f32[2,16,8,256]{3,2,1,0:T(8,128)S(1)}, f32[2,16,8,256]{3,2,1,0:T(8,128)S(1)}, u32[]{:S(2)}, u32[]{:S(2)}) collective-permute-start(f32[2,16,8,256]{3,2,1,0:T(8,128)S(1)} %get-tuple-element.119), channel_id=1, source_target_pairs={{0,2},{1,3},{2,18},{3,19},{4,34},{5,35},{6,50},{7,51},{8,66},{9,67... | collective-permute-start | bytes 786440 | tf_op jit(solution)/shard_map/ppermute | solution.py:676
  202.6 32.3 %collective-permute-start.35 = (f32[2,16,8,256]{3,2,1,0:T(8,128)S(1)}, f32[2,16,8,256]{3,2,1,0:T(8,128)S(1)}, u32[]{:S(2)}, u32[]{:S(2)}) collective-permute-start(f32[2,16,8,256]{3,2,1,0:T(8,128)S(1)} %get-tuple-element.120), channel_id=1, source_target_pairs={{0,4},{1,5},{2,20},{3,21},{4,36},{5,37},{6,52},{7,53},{8,68},{9,69... | collective-permute-start | bytes 786440 | tf_op jit(solution)/shard_map/ppermute | solution.py:676
  205.1 29.8 %collective-permute-start.36 = (f32[2,16,8,256]{3,2,1,0:T(8,128)S(1)}, f32[2,16,8,256]{3,2,1,0:T(8,128)S(1)}, u32[]{:S(2)}, u32[]{:S(2)}) collective-permute-start(f32[2,16,8,256]{3,2,1,0:T(8,128)S(1)} %get-tuple-element.121), channel_id=1, source_target_pairs={{0,6},{1,7},{2,22},{3,23},{4,38},{5,39},{6,54},{7,55},{8,70},{9,71... | collective-permute-start | bytes 786440 | tf_op jit(solution)/shard_map/ppermute | solution.py:676
  210.9 24.0 %collective-permute-start.37 = (f32[2,16,8,256]{3,2,1,0:T(8,128)S(1)}, f32[2,16,8,256]{3,2,1,0:T(8,128)S(1)}, u32[]{:S(2)}, u32[]{:S(2)}) collective-permute-start(f32[2,16,8,256]{3,2,1,0:T(8,128)S(1)} %get-tuple-element.122), channel_id=1, source_target_pairs={{0,8},{1,9},{2,24},{3,25},{4,40},{5,41},{6,56},{7,57},{8,72},{9,73... | collective-permute-start | bytes 786440 | tf_op jit(solution)/shard_map/ppermute | solution.py:676
  219.8 18.4 %collective-permute-start.38 = (f32[2,16,8,256]{3,2,1,0:T(8,128)S(1)}, f32[2,16,8,256]{3,2,1,0:T(8,128)S(1)}, u32[]{:S(2)}, u32[]{:S(2)}) collective-permute-start(f32[2,16,8,256]{3,2,1,0:T(8,128)S(1)} %get-tuple-element.123), channel_id=1, source_target_pairs={{0,10},{1,11},{2,26},{3,27},{4,42},{5,43},{6,58},{7,59},{8,74},{9,... | collective-permute-start | bytes 786440 | tf_op jit(solution)/shard_map/ppermute | solution.py:676
  224.9 26.4 %collective-permute-start.39 = (f32[2,16,8,256]{3,2,1,0:T(8,128)S(1)}, f32[2,16,8,256]{3,2,1,0:T(8,128)S(1)}, u32[]{:S(2)}, u32[]{:S(2)}) collective-permute-start(f32[2,16,8,256]{3,2,1,0:T(8,128)S(1)} %get-tuple-element.124), channel_id=1, source_target_pairs={{0,12},{1,13},{2,28},{3,29},{4,44},{5,45},{6,60},{7,61},{8,76},{9,... | collective-permute-start | bytes 786440 | tf_op jit(solution)/shard_map/ppermute | solution.py:676
  234.9 20.1 %collective-permute-start.40 = (f32[2,16,8,256]{3,2,1,0:T(8,128)S(1)}, f32[2,16,8,256]{3,2,1,0:T(8,128)S(1)}, u32[]{:S(2)}, u32[]{:S(2)}) collective-permute-start(f32[2,16,8,256]{3,2,1,0:T(8,128)S(1)} %get-tuple-element.125), channel_id=1, source_target_pairs={{0,14},{1,15},{2,30},{3,31},{4,46},{5,47},{6,62},{7,63},{8,78},{9,... | collective-permute-start | bytes 786440 | tf_op jit(solution)/shard_map/ppermute | solution.py:676
  267.3 17.8 %collective-permute-start.45 = (f32[2,4,32,256]{3,2,1,0:T(8,128)S(1)}, f32[2,4,32,256]{3,2,1,0:T(8,128)S(1)}, u32[]{:S(2)}, u32[]{:S(2)}) collective-permute-start(f32[2,4,32,256]{3,2,1,0:T(8,128)S(1)} %get-tuple-element.132), channel_id=1, source_target_pairs={{0,64},{16,80},{32,96},{48,112},{64,0},{80,16},{96,32},{112,48},{1... | collective-permute-start | bytes 786440 | tf_op jit(solution)/shard_map/ppermute | solution.py:710
  270.5 22.4 %collective-permute-start.46 = (f32[2,4,32,256]{3,2,1,0:T(8,128)S(1)}, f32[2,4,32,256]{3,2,1,0:T(8,128)S(1)}, u32[]{:S(2)}, u32[]{:S(2)}) collective-permute-start(f32[2,4,32,256]{3,2,1,0:T(8,128)S(1)} %get-tuple-element.133), channel_id=1, source_target_pairs={{0,80},{16,64},{32,112},{48,96},{64,16},{80,0},{96,48},{112,32},{1... | collective-permute-start | bytes 786440 | tf_op jit(solution)/shard_map/ppermute | solution.py:710
  271.0 22.6 %collective-permute-start.47 = (f32[2,4,32,256]{3,2,1,0:T(8,128)S(1)}, f32[2,4,32,256]{3,2,1,0:T(8,128)S(1)}, u32[]{:S(2)}, u32[]{:S(2)}) collective-permute-start(f32[2,4,32,256]{3,2,1,0:T(8,128)S(1)} %get-tuple-element.134), channel_id=1, source_target_pairs={{0,96},{16,112},{32,64},{48,80},{64,32},{80,48},{96,0},{112,16},{1... | collective-permute-start | bytes 786440 | tf_op jit(solution)/shard_map/ppermute | solution.py:710
  275.3 23.3 %collective-permute-start.48 = (f32[2,4,32,256]{3,2,1,0:T(8,128)S(1)}, f32[2,4,32,256]{3,2,1,0:T(8,128)S(1)}, u32[]{:S(2)}, u32[]{:S(2)}) collective-permute-start(f32[2,4,32,256]{3,2,1,0:T(8,128)S(1)} %get-tuple-element.135), channel_id=1, source_target_pairs={{0,112},{16,96},{32,80},{48,64},{64,48},{80,32},{96,16},{112,0},{1... | collective-permute-start | bytes 786440 | tf_op jit(solution)/shard_map/ppermute | solution.py:710
  (36 other events, 512.3 us)

commit v2 on v1

v2 whole, which is shorter than its diff:
```python
import jax
import jax.numpy as jnp
from jax import lax
from jax.experimental import pallas as pl
from jax.experimental.pallas import tpu as pltpu
from jax.sharding import PartitionSpec as P

SWEEPS = 8
NT = 8
GROUP = 16
CHIPS = 8
PLANES = 4
ROWS = 16
NY = 256
LANES = 128
HALO = 9
UNROLL = 8
EXT = ROWS + 2 * HALO
F32 = jnp.float32
ANY = pl.BlockSpec(memory_space=pl.ANY)
SMEM = pl.BlockSpec(memory_space=pltpu.SMEM)
VMEM = pl.BlockSpec(memory_space=pltpu.VMEM)
DMA = pltpu.SemaphoreType.DMA


def chain_chip(g):
    return g ^ ((g >> 1) & 1)


def chain_place(c):
    return 2 * chain_chip(c >> 1) + (c & 1)


def call(kernel, out_shape, in_specs, out_specs, scratch, megabytes=24):
    return pl.pallas_call(
        kernel,
        out_shape=out_shape,
        in_specs=in_specs,
        out_specs=out_specs,
        scratch_shapes=scratch,
        compiler_params=pltpu.CompilerParams(vmem_limit_bytes=megabytes * 1024 * 1024),
    )


def struct(*shape):
    return jax.ShapeDtypeStruct(shape, F32)


def run(todo):
    for copy in todo:
        copy.start()
    for copy in todo:
        copy.wait()


def by_chip(field):
    return field.reshape(PLANES, CHIPS, 2, ROWS, NY)


def pack_field(field, out, sems):
    run(
        [
            pltpu.make_async_copy(
                field.at[:, pl.ds(chain_place(c) * ROWS, ROWS), :], out.at[c], sems.at[c]
            )
            for c in range(GROUP)
        ]
    )


DEPTH = 3 * PLANES * ROWS + 16
STEPS = (0, 1, 2, 6, 5, 3, 7, 4)


def state_copies(states, rate, edges, place, core, target, sems):
    rows = pl.ds(pl.multiple_of((2 * place + core) * ROWS, ROWS), ROWS)
    todo = [
        pltpu.make_async_copy(
            field.at[plane, rows, :],
            target.at[pl.ds((at * PLANES + plane) * ROWS, ROWS)],
            sems.at[at * PLANES + plane],
        )
        for at, field in enumerate((states.at[0, 1], states.at[0, 0], rate))
        for plane in range(PLANES)
    ]
    todo.append(
        pltpu.make_async_copy(
            edges.at[2 * place + core],
            target.at[pl.ds(DEPTH - 16, 16)],
            sems.at[3 * PLANES],
        )
    )
    return todo


def pack_states_first(ids, states, rate, edges, out, sems):
    todo = []
    for place in range(CHIPS):
        todo += state_copies(
            states, rate, edges, place, 1 - ids[2], out.at[place], sems.at[place]
        )
    run(todo)


def pack_states(ids, states, rate, edges, received, *refs):
    outs, sems, more = refs[:CHIPS], refs[CHIPS], refs[CHIPS + 1]
    chip, core = ids[1], ids[2]
    todo = []
    for step in range(CHIPS):
        place = chain_chip(chip ^ STEPS[step])
        todo += state_copies(
            states, rate, edges, place, core, outs[step].at[core], sems.at[step]
        )
        todo.append(
            pltpu.make_async_copy(received.at[place], outs[step].at[1 - core], more.at[step])
        )
    run(todo)


def edge_rows(states):
    blocks = states[0].reshape(2, PLANES, GROUP, ROWS, NY)
    zero = jnp.zeros((2, PLANES, 1, NY), F32)
    before = jnp.concatenate([zero, blocks[:, :, :-1, ROWS - 1]], axis=2)
    after = jnp.concatenate([blocks[:, :, 1:, 0], zero], axis=2)
    edges = jnp.stack([before[::-1], after[::-1]], axis=1)
    return edges.transpose(3, 0, 1, 2, 4).reshape(GROUP, 16, NY)


def fetch_pieces(chip, pieces, slots, sems):
    todo = []
    for step, piece in enumerate(pieces):
        for half in range(2):
            todo.append(
                pltpu.make_async_copy(
                    piece.at[:, :, pl.ds(half * LANES, LANES)],
                    slots.at[half, pl.ds(2 * (chip ^ STEPS[step]), 2)],
                    sems.at[half, step],
                )
            )
    run(todo)


def strided(flat, start, stride):
    return jnp.concatenate(
        [flat[half][pl.ds(start, 8, stride=stride), :] for half in range(2)], axis=1
    )


def halves(slots):
    size = 1
    for extent in slots.shape[1:-1]:
        size *= extent
    return [slots.at[half].reshape(size, LANES) for half in range(2)]


def fetch_halves(received, slots, sems):
    every = (slice(None),) * (len(received.shape) - 1)
    run(
        [
            pltpu.make_async_copy(
                received.at[every + (pl.ds(half * LANES, LANES),)], slots.at[half], sems.at[half]
            )
            for half in range(2)
        ]
    )


def unpack_field(halo):
    def kernel(received, own, up, down, slots, sems):
        fetch_halves(received, slots, sems)
        flat = halves(slots)

        def one_row(row, carry):
            for i in range(8):
                own[row, i] = strided(flat, i * ROWS + row, 8 * ROWS)
            return carry

        lax.fori_loop(0, ROWS, one_row, 0)
        up[...] = own[0:halo]
        down[...] = own[ROWS - halo :]

    return kernel


def lines_of(slots):
    flat = halves(slots)

    def lines(i, line):
        return strided(flat, (i // PLANES) * slots.shape[2] + line, 2 * slots.shape[2])

    return lines


def unpack_states(ids, *refs):
    pieces = refs[:CHIPS]
    own, decay, slots, sems = refs[CHIPS:]
    fetch_pieces(ids[1], pieces, slots, sems)
    lines = lines_of(slots)

    def one_row(row, carry):
        for i in range(8):
            for field in range(2):
                own[field, row + 1, i] = lines(i, (field * PLANES + i % PLANES) * ROWS + row)
            decay[row, i] = jnp.exp(-lines(i, (2 * PLANES + i % PLANES) * ROWS + row))
        return carry

    lax.fori_loop(0, ROWS, one_row, 0)
    for i in range(8):
        for field in range(2):
            for side in range(2):
                line = 3 * PLANES * ROWS + (field * 2 + side) * PLANES + i % PLANES
                own[field, side * (ROWS + 1), i] = lines(i, line)


def coefficients(weights, k, kx, ky, kw, kz, diag):
    scale = weights[0]
    half = 0.5 * scale
    rest = weights[1] - scale
    lane = lax.broadcasted_iota(jnp.int32, (8, NY), 1)
    place = lax.broadcasted_iota(jnp.int32, (8, NY), 0)

    def one_row(e, carry):
        mids = [k[e, i] for i in range(8)]
        last = pltpu.roll(mids[7], 1, 0)
        kz[e, 0] = jnp.where(place == 0, 0.0, half * (mids[0] + last))
        for i in range(8):
            mid = mids[i]
            if i:
                kz[e, i] = half * (mid + mids[i - 1])
            before = jnp.where(lane == 0, 0.0, half * (mid + pltpu.roll(mid, 1, 1)))
            behind = jnp.where(lane == NY - 1, 0.0, half * (mid + pltpu.roll(mid, NY - 1, 1)))
            x_low = half * (mid + k[e - 1, i])
            x_high = half * (mid + k[e + 1, i])
            own = half * mid
            extra = jnp.where((lane == 0) | (lane == NY - 1), own, 0.0)
            if i == 0:
                extra = extra + jnp.where(place == 0, own, 0.0)
            if i == 7:
                extra = extra + jnp.where(place == 7, own, 0.0)
            kx[e, i] = x_low
            ky[e, i] = before
            kw[e, i] = behind
            diag[e, i] = rest - extra - (before + behind) - (x_low + x_high)
        return carry

    def two_rows(n, carry):
        one_row(2 * n + 1, carry)
        one_row(2 * n + 2, carry)
        return carry

    lax.fori_loop(0, EXT // 2 - 1, two_rows, 0)
    for i in range(8):
        kx[EXT - 1, i] = half * (k[EXT - 2, i] + k[EXT - 1, i])


def sweeps(ids, first, weights, rhs, d0, d1, kx, ky, kw, kz, diag):
    at = 2 * chain_chip(ids[1]) + ids[2]
    low = jnp.where(at == 0, HALO, 0)
    high = jnp.where(at == GROUP - 1, HALO + ROWS, EXT)
    start_weight = weights[2]
    zeros = jnp.zeros((8, NY), F32)

    def opening(e, carry):
        for i in range(8):
            d0[e, i] = start_weight * rhs[e, i]
            d1[e, i] = zeros
        return carry

    lax.fori_loop(first, EXT - first, opening, 0)

    def one_sweep(step, cur, nxt):
        share = weights[3 + 2 * step]
        weight = weights[4 + 2 * step]

        def one_row(e, inner):
            v = [cur[e, i] for i in range(8)]
            head = kz[e, 0] * (v[0] - pltpu.roll(v[7], 1, 0))
            tail = pltpu.roll(head, 7, 0)
            flux = head
            for i in range(8):
                mid = v[i]
                flux_next = kz[e, i + 1] * (v[i + 1] - mid) if i < 7 else tail
                total = (
                    diag[e, i] * mid
                    + (flux_next - flux)
                    + kx[e, i] * cur[e - 1, i]
                    + kx[e + 1, i] * cur[e + 1, i]
                    + ky[e, i] * pltpu.roll(mid, 1, 1)
                    + kw[e, i] * pltpu.roll(mid, NY - 1, 1)
                )
                nxt[e, i] = share * total + (weight * rhs[e, i] - nxt[e, i])
                flux = flux_next
            return inner

        begin = jnp.maximum(first + step + 1, low)
        end = jnp.minimum(EXT - first - step - 1, high)

        def some_rows(n, inner):
            for extra in range(UNROLL):
                one_row(begin + UNROLL * n + extra, inner)
            return inner

        full = lax.div(end - begin, UNROLL)
        lax.fori_loop(0, full, some_rows, 0)
        rest = begin + UNROLL * full
        pairs = lax.div(end - rest, 2)

        def two_rows(n, inner):
            one_row(rest + 2 * n, inner)
            one_row(rest + 2 * n + 1, inner)
            return inner

        lax.fori_loop(0, pairs, two_rows, 0)
        lax.fori_loop(rest + 2 * pairs, end, one_row, 0)

    def two_sweeps(pair, carry):
        one_sweep(2 * pair, d0, d1)
        one_sweep(2 * pair + 1, d1, d0)
        return carry

    lax.fori_loop(0, SWEEPS // 2, two_sweeps, 0)


FIELD = (EXT, 8, 8, NY)
SOLVE_SCRATCH = [pltpu.VMEM(FIELD, F32) for _ in range(9)] + [DMA((6,)), DMA((3,))]


def solve(halo):
    first = HALO - halo
    last = EXT - first

    def kernel(ids, weights, own_k, above_k, below_k, own, above, below, *refs):
        outs = refs[:-11]
        k, kx, ky, kw, kz, diag, rhs, d0, d1, sems, out_sems = refs[-11:]
        mine = pl.ds(HALO, ROWS)
        fields = [
            pltpu.make_async_copy(above_k, k.at[pl.ds(0, HALO)], sems.at[0]),
            pltpu.make_async_copy(own_k, k.at[mine], sems.at[1]),
            pltpu.make_async_copy(below_k, k.at[pl.ds(HALO + ROWS, HALO)], sems.at[2]),
        ]
        sides = [
            pltpu.make_async_copy(above, rhs.at[pl.ds(first, halo)], sems.at[3]),
            pltpu.make_async_copy(own, rhs.at[mine], sems.at[4]),
            pltpu.make_async_copy(below, rhs.at[pl.ds(HALO + ROWS, halo)], sems.at[5]),
        ]
        for copy in fields + sides:
            copy.start()
        for copy in fields:
            copy.wait()
        coefficients(weights, k, kx, ky, kw, kz, diag)
        for copy in sides:
            copy.wait()
        sweeps(ids, first, weights, rhs, d0, d1, kx, ky, kw, kz, diag)
        if halo == HALO:
            todo = [pltpu.make_async_copy(d0.at[pl.ds(HALO - 1, ROWS + 2)], outs[0], out_sems.at[0])]
        else:
            todo = [
                pltpu.make_async_copy(d0.at[mine], outs[0], out_sems.at[0]),
                pltpu.make_async_copy(d0.at[pl.ds(HALO, HALO)], outs[1], out_sems.at[1]),
                pltpu.make_async_copy(d0.at[pl.ds(ROWS, HALO)], outs[2], out_sems.at[2]),
            ]
        run(todo)

    return kernel


def face_rows(w, u, field, out, add):
    lane = lax.broadcasted_iota(jnp.int32, (8, NY), 1)
    place = lax.broadcasted_iota(jnp.int32, (8, NY), 0)

    def one_row(row, carry):
        e = row + 1
        vw = [w[e, i] for i in range(8)]
        vu = [u[field, row + 1, i] for i in range(8)]
        back_w = jnp.where(place == 0, 0.0, pltpu.roll(vw[7], 1, 0))
        back_u = jnp.where(place == 0, 0.0, pltpu.roll(vu[7], 1, 0))
        head = (vw[0] - back_w) * (vu[0] - back_u)
        face = head
        for i in range(8):
            if i < 7:
                face_next = (vw[i + 1] - vw[i]) * (vu[i + 1] - vu[i])
            else:
                face_next = jnp.where(place == 7, vw[7] * vu[7], pltpu.roll(head, 7, 0))
            side_w = jnp.where(lane == 0, 0.0, pltpu.roll(vw[i], 1, 1))
            side_u = jnp.where(lane == 0, 0.0, pltpu.roll(vu[i], 1, 1))
            face_y = (vw[i] - side_w) * (vu[i] - side_u)
            far_y = jnp.where(lane == NY - 1, vw[i] * vu[i], pltpu.roll(face_y, NY - 1, 1))
            total = (
                (face + face_next)
                + (face_y + far_y)
                + (vw[i] - w[e - 1, i]) * (vu[i] - u[field, row, i])
                + (vw[i] - w[e + 1, i]) * (vu[i] - u[field, row + 2, i])
            )
            total = -0.5 * total
            if add:
                total = out[lax.rem(row, 8), 1, lax.div(row, 8), i] + total
            out[lax.rem(row, 8), 1, lax.div(row, 8), i] = total
            face = face_next
        return carry

    lax.fori_loop(0, ROWS, one_row, 0)


def face_sums(
    ids,
    late,
    late_above,
    late_below,
    early,
    states,
    decay,
    ends,
    *refs,
):
    out, w, x, u, rate_in, ends_in, sems = refs
    tm = ids[0]
    inner = pl.ds(1, ROWS)
    todo = [
        pltpu.make_async_copy(late_above.at[HALO - 1], w.at[0], sems.at[0]),
        pltpu.make_async_copy(late, w.at[inner], sems.at[1]),
        pltpu.make_async_copy(late_below.at[0], w.at[ROWS + 1], sems.at[2]),
        pltpu.make_async_copy(states, u, sems.at[3]),
        pltpu.make_async_copy(early, x, sems.at[4]),
        pltpu.make_async_copy(decay, rate_in, sems.at[5]),
        pltpu.make_async_copy(ends, ends_in, sems.at[6]),
    ]
    run(todo)
    face_rows(w, u, 0, out, False)
    face_rows(x, u, 1, out, True)
    keep = jnp.where(tm == NT - 1, 0.0, 1.0)

    def last_row(row, carry):
        for i in range(8):
            value = x[row + 1, i] - keep * (rate_in[row, i] * ends_in[row, i])
            out[lax.rem(row, 8), 0, lax.div(row, 8), i] = value
        return carry

    lax.fori_loop(0, ROWS, last_row, 0)


def recur(ids, decay, received, out, rates, lines, total, sems):
    copies = [
        pltpu.make_async_copy(decay.at[ids[0] + 8 * r], rates.at[r], sems.at[r])
        for r in range(2)
    ]
    run(copies)

    def split(value, target, index):
        for half in range(2):
            target[(half,) + index] = value[:, half * LANES : (half + 1) * LANES]

    def one_plane(i, carry):
        for r in range(2):
            rate = rates[r, i]
            value = received[NT - 1, 0, r, i]
            split(value, lines, (NT - 1, i, r))
            for slab in range(NT - 2, -1, -1):
                value = received[slab, 0, r, i] + rate * value
                split(value, lines, (slab, i, r))
            summed = received[0, 1, r, i]
            for slab in range(1, NT):
                summed = summed + received[slab, 1, r, i]
            split(summed, total, (i, r))
        return carry

    lax.fori_loop(0, 8, one_plane, 0)
    flat, flat_total = halves(lines), halves(total)
    for s in range(GROUP):
        start = (s % 2) * 64 + s // 2
        summed = strided(flat_total, start, 8)

        def one_slab(slab, carry):
            out[slab * GROUP + s, 0] = strided(flat, slab * 128 + start, 8)
            out[slab * GROUP + s, 1] = summed
            return carry

        lax.fori_loop(0, NT, one_slab, 0)


def place_results(received, adjoint, sensitivity, slots, sems):
    fetch_halves(received, slots, sems)
    flat = halves(slots)
    for c in range(GROUP):
        for r in range(2):
            rows = pl.ds(chain_place(c) * ROWS + 8 * r, 8)
            for plane in range(PLANES):
                start = c * 16 + 2 * plane + r
                adjoint[0, plane, rows, :] = strided(flat, start, 256)
                sensitivity[plane, rows, :] = strided(flat, start + 8, 256)


def sweep_weights(smallest_eig, largest_eig):
    low, high = smallest_eig[0], largest_eig[0]
    center = (high + low) / 2.0
    radius = (high - low) / 2.0
    sigma = center / radius
    second = [1.0, 2.0 * sigma]
    for _ in range(SWEEPS):
        second.append(2.0 * sigma * second[-1] - second[-2])
    norm = radius * 0.5 * (second[SWEEPS + 1] - second[SWEEPS - 1])
    parts = [2.0 * second[SWEEPS - k] / norm for k in range(SWEEPS + 1)]
    weights = [2.0 / radius, 2.0 * sigma, parts[SWEEPS]]
    for k in range(SWEEPS - 1, -1, -1):
        weights += [jnp.float32(1.0 if k else 0.5), parts[k] * (1.0 if k else 0.5)]
    return jnp.stack(weights)


def per_device(
    adjoint_iterate,
    forward_states,
    conductivity,
    coarse_rate,
    terminal_adjoint,
    smallest_eig,
    largest_eig,
):
    here = lax.axis_index("space")
    ids = jnp.stack([lax.axis_index("tm"), here // 2, here % 2]).astype(jnp.int32)
    weights = sweep_weights(smallest_eig, largest_eig)
    masks = [[(c, c ^ mask) for c in range(GROUP)] for mask in range(GROUP)]
    forward = [(chain_place(i), chain_place(i + 1)) for i in range(GROUP - 1)]
    backward = [(b, a) for a, b in forward]

    def to_chips(pieces, steps):
        return [
            lax.ppermute(piece, "space", masks[2 * step]) for piece, step in zip(pieces, steps)
        ]

    def along_chain(up, down):
        return lax.ppermute(down, "space", forward), lax.ppermute(up, "space", backward)

    block = (ROWS, 8, 8, NY)
    def spread(field):
        return call(pack_field, struct(GROUP, PLANES, ROWS, NY), [ANY], VMEM, [DMA((GROUP,))], 56)(
            field
        )

    def unpack(received, halo):
        return call(
            unpack_field(halo),
            [struct(*block), struct(halo, 8, 8, NY), struct(halo, 8, 8, NY)],
            [ANY],
            [VMEM] * 3,
            [pltpu.VMEM((2, GROUP, PLANES, ROWS, LANES), F32), DMA((2,))],
        )(received)

    first = jnp.where(lax.axis_index("tm") == 0, terminal_adjoint, adjoint_iterate[0])
    ends = lax.ppermute(first, "tm", [(t, (t - 1) % NT) for t in range(NT)])
    edges = edge_rows(forward_states)
    other = call(
        pack_states_first,
        struct(CHIPS, DEPTH, NY),
        [SMEM] + [ANY] * 3,
        VMEM,
        [DMA((CHIPS, 3 * PLANES + 1))],
        56,
    )(ids, forward_states, coarse_rate, edges)
    received = lax.all_to_all(spread(conductivity), "space", 0, 0)
    received, other = lax.optimization_barrier((received, other))
    own_k, up, down = unpack(received, HALO)
    above_k, below_k = along_chain(up, down)
    other = lax.ppermute(other, "space", masks[1])
    ends, own_k = lax.optimization_barrier((ends, own_k))
    received = lax.all_to_all(spread(ends), "space", 0, 0)
    pieces = call(
        pack_states,
        [struct(2, DEPTH, NY)] * CHIPS,
        [SMEM] + [ANY] * 4,
        [VMEM] * CHIPS,
        [DMA((CHIPS, 3 * PLANES + 1)), DMA((CHIPS,))],
        56,
    )(ids, forward_states, coarse_rate, edges, other)
    received, pieces = lax.optimization_barrier((received, list(pieces)))
    ends, up, down = unpack(received, HALO - 1)
    above, below = along_chain(up, down)
    pieces[1:5] = to_chips(pieces[1:5], STEPS[1:5])

    late, up, down = call(
        solve(HALO - 1),
        [struct(*block), struct(HALO, 8, 8, NY), struct(HALO, 8, 8, NY)],
        [SMEM] * 2 + [ANY] * 6,
        [ANY] * 3,
        SOLVE_SCRATCH,
        56,
    )(ids, weights, own_k, above_k, below_k, ends, above, below)
    pieces[1:5], late, up, down = lax.optimization_barrier((pieces[1:5], late, up, down))
    late_above, late_below = along_chain(up, down)
    pieces[5:], late_above, late_below = lax.optimization_barrier(
        (pieces[5:], late_above, late_below)
    )
    pieces[5:] = to_chips(pieces[5:], STEPS[5:])
    wide = (ROWS + 2, 8, 8, NY)
    early = call(
        solve(HALO), struct(*wide), [SMEM] * 2 + [ANY] * 6, ANY, SOLVE_SCRATCH, 56
    )(ids, weights, own_k, above_k, below_k, late, late_above, late_below)

    pieces, early = lax.optimization_barrier((pieces, early))
    states, decay = call(
        unpack_states,
        [struct(2, *wide), struct(*block)],
        [SMEM] + [ANY] * CHIPS,
        [VMEM] * 2,
        [pltpu.VMEM((2, GROUP, DEPTH, LANES), F32), DMA((2, CHIPS))],
    )(ids, *pieces)
    parts = call(
        face_sums,
        struct(NT, 2, 2, 8, 8, NY),
        [SMEM] + [ANY] * 7,
        VMEM,
        [
            pltpu.VMEM(wide, F32),
            pltpu.VMEM(wide, F32),
            pltpu.VMEM((2,) + wide, F32),
            pltpu.VMEM(block, F32),
            pltpu.VMEM(block, F32),
            DMA((7,)),
        ],
        40,
    )(
        ids,
        late,
        late_above,
        late_below,
        early,
        states,
        decay,
        ends,
    )
    parts = lax.all_to_all(parts, "tm", 0, 0)
    results = call(
        recur,
        struct(NT * GROUP, 2, 8, NY),
        [SMEM, ANY, VMEM],
        VMEM,
        [
            pltpu.VMEM((2, 8, 8, NY), F32),
            pltpu.VMEM((2, NT, 8, 2, 8, LANES), F32),
            pltpu.VMEM((2, 8, 2, 8, LANES), F32),
            DMA((2,)),
        ],
    )(ids, decay, parts)
    results = lax.all_to_all(results, ("tm", "space"), 0, 0)
    adjoint_next, sensitivity = call(
        place_results,
        [struct(1, PLANES, NY, NY), struct(PLANES, NY, NY)],
        [ANY],
        [VMEM] * 2,
        [pltpu.VMEM((2, NT * GROUP, 2, 8, LANES), F32), DMA((2,))],
    )(results)
    return (adjoint_next, sensitivity)


def solution(mesh):
    return jax.shard_map(
        per_device,
        mesh=mesh,
        in_specs=(
            P("tm", "space", None, None),
            P("tm", None, "space", None, None),
            P("space", None, None),
            P("space", None, None),
            P("space", None, None),
            P(),
            P(),
        ),
        out_specs=(P("tm", "space", None, None), P("space", None, None)),
        check_vma=False,
    )
```

time: 305 us -> 237 us (0.78)
  starting transfers between devices: 119 us -> 50.3 us
  blocking collectives: 0 us -> 67.1 us
  waiting for transfers between devices: 103 us -> 45.1 us
  Pallas kernels: 67.5 us -> 60.4 us
    ppermute x40 -> x8, starting transfers between devices: 106 us -> 27.8 us  [the longest x7 21.7 us: to_chips(): lax.ppermute(piece, 'space', masks[2 * step])]
    ppermute x40 -> x8, waiting for transfers between devices: 101 us -> 30.9 us  [the longest x1 18.4 us: per_device(): ends = lax.ppermute(first, 'tm', [(t, (t - 1) % NT) for t in range(NT)])]
    all_to_all x0 -> x2, blocking collectives: none -> 67.1 us  [the longest x1 34.1 us: per_device(): results = lax.all_to_all(results, ('tm', 'space'), 0, 0)]
    all_to_all x0 -> x2, waiting for transfers between devices: none -> 11.4 us  [the longest x1 7.44 us: per_device(): received = lax.all_to_all(spread(ends), 'space', 0, 0)]
    all_to_all x0 -> x2, starting transfers between devices: none -> 10.7 us  [the longest x1 5.85 us: per_device(): received = lax.all_to_all(spread(conductivity), 'space', 0, 0)]
    unnamed x38 -> x30, local copies, waits for them, and re-layouts: 8.78 us -> 4.89 us
    pallas_call x9 -> x7, Pallas kernels: 29.6 us -> 26.9 us  [the longest x1 7.31 us: per_device(): call(face_sums, struct(NT, 2, 2, 8, 8, NY), [SMEM] + [ANY] * 7, VMEM, [pl...]
    ppermute x4 -> x3, starting transfers between devices: 7.16 us -> 7.94 us  [along_chain(): lax.ppermute(down, 'space', forward)]
  transfers between devices with their start and end apart: 49 -> 17, of which waited for: 21 -> 7; matrix products, arithmetic and copies ran while one was open for 0% -> 2% of each run, Pallas kernels for 16% -> 18%
where the time goes in v2:
time: 237 us; the launch traced here: 236 us
  blocking collectives  67.1 us (28%)
  Pallas kernels  60.4 us (25%)
  starting transfers between devices  50.3 us (21%)
  waiting for transfers between devices  45.1 us (19%)
  local copies, waits for them, and re-layouts  8.19 us (3%)
  between operations  2.79 us (1%)
    all_to_all x1, blocking collectives, per_device(): results = lax.all_to_all(results, ('tm', 'space'), 0, 0)  34.1 us
    all_to_all x1, blocking collectives, per_device(): parts = lax.all_to_all(parts, 'tm', 0, 0)  33.1 us
    ppermute x7, starting transfers between devices, to_chips(): lax.ppermute(piece, 'space', masks[2 * step])  21.7 us
    ppermute x1, waiting for transfers between devices, per_device(): ends = lax.ppermute(first, 'tm', [(t, (t - 1) % NT) for t in range(NT)])  18.4 us
    pallas_call x1, Pallas kernels, per_device(): call(solve(HALO), struct(*wide), [SMEM] * 2 + [ANY] * 6, ANY, SOLVE_SCRAT...  14.6 us
    pallas_call x1, Pallas kernels, per_device(): call(solve(HALO - 1), [struct(*block), struct(HALO, 8, 8, NY), struct(HAL...  14.5 us
    ppermute x7, waiting for transfers between devices, to_chips(): lax.ppermute(piece, 'space', masks[2 * step])  12.5 us
    ppermute x3, starting transfers between devices, along_chain(): lax.ppermute(down, 'space', forward)  7.94 us
  transfers between devices with their start and end apart: 17, of which 7 were waited for; matrix products, arithmetic and copies ran while one was open for 2% of the time, Pallas kernels for 18%

profile of v2, /device:TPU:0, one launch (start us, length us, event | category | flops | bytes accessed | tf_op | source)
XLA Modules:
  0.0 235.7 jit_solution(13405361304040440097)
XLA Ops:
  0.6 2.5 %shard_map.86 = f32[16,4,16,256]{3,2,1,0:T(8,128)} custom-call(f32[4,256,256]{2,1,0:T(8,128)} %field.1), custom_call_target="tpu_custom_call" | custom-call | tf_op jit(solution)/shard_map/pallas_call | solution.py:534
  3.1 5.9 %all-to-all-start = ((f32[16,4,16,256]{3,2,1,0:T(8,128)}), f32[16,4,16,256]{3,2,1,0:T(8,128)S(1)}, u32[]{:S(2)}, u32[]{:S(2)}) async-start(f32[16,4,16,256]{3,2,1,0:T(8,128)} %shard_map.86), calls=%async_computation | async-start | bytes 2097152 | tf_op jit(solution)/shard_map/all_to_all | solution.py:558
  10.1 6.0 %collective-permute-start = (f32[4,256,256]{2,1,0:T(8,128)}, f32[4,256,256]{2,1,0:T(8,128)}, u32[]{:S(2)}, u32[]{:S(2)}) collective-permute-start(f32[4,256,256]{2,1,0:T(8,128)} %bitcast_select_fusion), channel_id=1, source_target_pairs={{0,112},{16,0},{32,16},{48,32},{64,48},{80,64},{96,80},{112,96},{1... | collective-permute-start | bytes 3145736 | tf_op jit(solution)/shard_map/ppermute | solution.py:548
  16.2 1.7 fusion
  19.5 4.2 %shard_map.87 = f32[8,208,256]{2,1,0:T(8,128)} custom-call(s32[3]{0:T(128)} %pad_add_fusion.ids, f32[1,2,4,256,256]{4,3,2,1,0:T(8,128)} %states.3, f32[4,256,256]{2,1,0:T(8,128)} %rate.3, f32[16,16,256]{2,1,0:T(8,128)} %reshape.25.edges), custom_call_target="tpu_custom_call" | custom-call | tf_op jit(solution)/shard_map/pallas_call | solution.py:550
  23.7 3.9 %all-to-all-done.received = f32[16,4,16,256]{3,2,1,0:T(8,128)S(1)} async-done(((f32[16,4,16,256]{3,2,1,0:T(8,128)}), f32[16,4,16,256]{3,2,1,0:T(8,128)S(1)}, u32[]{:S(2)}, u32[]{:S(2)}) %all-to-all-start) | async-done | bytes 1048608 | tf_op jit(solution)/shard_map/all_to_all | solution.py:558
  29.5 18.4 %collective-permute-done.field = f32[4,256,256]{2,1,0:T(8,128)} collective-permute-done((f32[4,256,256]{2,1,0:T(8,128)}, f32[4,256,256]{2,1,0:T(8,128)}, u32[]{:S(2)}, u32[]{:S(2)}) %collective-permute-start) | collective-permute-done | bytes 1048608 | tf_op jit(solution)/shard_map/ppermute | solution.py:548
  47.9 2.3 shard_map.89
  50.2 4.9 %all-to-all-start.1 = ((f32[16,4,16,256]{3,2,1,0:T(8,128)}), f32[16,4,16,256]{3,2,1,0:T(8,128)S(1)}, u32[]{:S(2)}, u32[]{:S(2)}) async-start(f32[16,4,16,256]{3,2,1,0:T(8,128)} %shard_map.89), calls=%async_computation.1 | async-start | bytes 2097152 | tf_op jit(solution)/shard_map/all_to_all | solution.py:564
  55.1 2.3 collective-permute-start.6
  57.4 1.3 collective-permute-start.7
  58.7 5.4 %shard_map.90 = (f32[2,208,256]{2,1,0:T(8,128)}, f32[2,208,256]{2,1,0:T(8,128)}, f32[2,208,256]{2,1,0:T(8,128)}, f32[2,208,256]{2,1,0:T(8,128)}, f32[2,208,256]{...) custom-call(s32[3]{0:T(128)} %pad_add_fusion.ids, ...), custom_call_target="tpu_custom_call" | custom-call | tf_op jit(solution)/shard_map/pallas_call | solution.py:565
  64.2 7.4 %all-to-all-done.1.received = f32[16,4,16,256]{3,2,1,0:T(8,128)S(1)} async-done(((f32[16,4,16,256]{3,2,1,0:T(8,128)}), f32[16,4,16,256]{3,2,1,0:T(8,128)S(1)}, u32[]{:S(2)}, u32[]{:S(2)}) %all-to-all-start.1) | async-done | bytes 1048608 | tf_op jit(solution)/shard_map/all_to_all | solution.py:564
  73.4 1.5 collective-permute-start.8
  74.9 1.3 collective-permute-start.9
  76.2 3.3 %collective-permute-start.2 = (f32[2,208,256]{2,1,0:T(8,128)}, f32[2,208,256]{2,1,0:T(8,128)S(1)}, u32[]{:S(2)}, u32[]{:S(2)}) collective-permute-start(f32[2,208,256]{2,1,0:T(8,128)} %get-tuple-element.68), channel_id=1, source_target_pairs={{0,2},{1,3},{2,0},{3,1},{4,6},{5,7},{6,4},{7,5},{8,10},{9,11},{10,... | collective-permute-start | bytes 1277960 | tf_op jit(solution)/shard_map/ppermute | solution.py:526
  79.7 2.4 %collective-permute-start.4 = (f32[2,208,256]{2,1,0:T(8,128)}, f32[2,208,256]{2,1,0:T(8,128)S(1)}, u32[]{:S(2)}, u32[]{:S(2)}) collective-permute-start(f32[2,208,256]{2,1,0:T(8,128)} %get-tuple-element.70), channel_id=1, source_target_pairs={{0,12},{1,13},{2,14},{3,15},{4,8},{5,9},{6,10},{7,11},{8,4},{9,5},... | collective-permute-start | bytes 1277960 | tf_op jit(solution)/shard_map/ppermute | solution.py:526
  82.9 4.7 %collective-permute-start.5 = (f32[2,208,256]{2,1,0:T(8,128)}, f32[2,208,256]{2,1,0:T(8,128)S(1)}, u32[]{:S(2)}, u32[]{:S(2)}) collective-permute-start(f32[2,208,256]{2,1,0:T(8,128)} %get-tuple-element.71), channel_id=1, source_target_pairs={{0,10},{1,11},{2,8},{3,9},{4,14},{5,15},{6,12},{7,13},{8,2},{9,3},... | collective-permute-start | bytes 1277960 | tf_op jit(solution)/shard_map/ppermute | solution.py:526
  90.1 14.5 %shard_map.92 = (f32[16,8,8,256]{3,2,1,0:T(8,128)}, f32[9,8,8,256]{3,2,1,0:T(8,128)}, f32[9,8,8,256]{3,2,1,0:T(8,128)}) custom-call(s32[3]{0:T(128)} %pad_add_fusion.ids, f32[19]{0:T(128)} %stack.69.weights, f32[16,8,8,256]{3,2,1,0:T(8,128)} %copy-done.3, f32[9,8,8,256]{3,2,1,0:T(8,128)} %copy-done.11, f32[9,8,8,256]{3,2,1,0:T(8,128)} %collective-permute-done.7.below_k, ...), custom_call_target="tpu_custom_call" | custom-call | tf_op jit(solution)/shard_map/pallas_call | solution.py:578
  104.7 4.1 %collective-permute-start.10 = (f32[9,8,8,256]{3,2,1,0:T(8,128)}, f32[9,8,8,256]{3,2,1,0:T(8,128)S(1)}, u32[]{:S(2)}, u32[]{:S(2)}) collective-permute-start(f32[9,8,8,256]{3,2,1,0:T(8,128)} %get-tuple-element.89), channel_id=1, source_target_pairs={{0,1},{1,2},{2,3},{3,6},{6,7},{7,4},{4,5},{5,8},{8,9},{9,10},{10,1... | collective-permute-start | bytes 1769480 | tf_op jit(solution)/shard_map/ppermute | solution.py:530
  110.5 2.3 collective-permute-done.11.below.late_below
  112.9 7.5 %collective-permute-start.12 = (f32[2,208,256]{2,1,0:T(8,128)}, f32[2,208,256]{2,1,0:T(8,128)S(1)}, u32[]{:S(2)}, u32[]{:S(2)}) collective-permute-start(f32[2,208,256]{2,1,0:T(8,128)} %get-tuple-element.91), channel_id=1, source_target_pairs={{0,6},{1,7},{2,4},{3,5},{4,2},{5,3},{6,0},{7,1},{8,14},{9,15},{10,... | collective-permute-start | bytes 1277960 | tf_op jit(solution)/shard_map/ppermute | solution.py:526
  120.4 3.7 %collective-permute-start.13 = (f32[2,208,256]{2,1,0:T(8,128)}, f32[2,208,256]{2,1,0:T(8,128)S(1)}, u32[]{:S(2)}, u32[]{:S(2)}) collective-permute-start(f32[2,208,256]{2,1,0:T(8,128)} %get-tuple-element.92), channel_id=1, source_target_pairs={{0,14},{1,15},{2,12},{3,13},{4,10},{5,11},{6,8},{7,9},{8,6},{9,7},... | collective-permute-start | bytes 1277960 | tf_op jit(solution)/shard_map/ppermute | solution.py:526
  124.1 14.6 %shard_map.93.early = f32[18,8,8,256]{3,2,1,0:T(8,128)} custom-call(s32[3]{0:T(128)} %pad_add_fusion.ids, f32[19]{0:T(128)} %stack.69.weights, f32[16,8,8,256]{3,2,1,0:T(8,128)} %copy-done.3, f32[9,8,8,256]{3,2,1,0:T(8,128)} %copy-done.11, f32[9,8,8,256]{3,2,1,0:T(8,128)} %collective-permute-done.7.below_k, f32[16,8,8,256]{3,2,1,0:T(8,128)} %get-tuple-element.94.own.late, ...), custom_call_target="tpu_custom_call" | custom-call | tf_op jit(solution)/shard_map/pallas_call | solution.py:593
  138.7 8.3 %collective-permute-done.13.refs_6_ = f32[2,208,256]{2,1,0:T(8,128)S(1)} collective-permute-done((f32[2,208,256]{2,1,0:T(8,128)}, f32[2,208,256]{2,1,0:T(8,128)S(1)}, u32[]{:S(2)}, u32[]{:S(2)}) %collective-permute-start.13) | collective-permute-done | bytes 426016 | tf_op jit(solution)/shard_map/ppermute | solution.py:526
  147.0 4.2 %collective-permute-done.14.refs_7_ = f32[2,208,256]{2,1,0:T(8,128)S(1)} collective-permute-done((f32[2,208,256]{2,1,0:T(8,128)}, f32[2,208,256]{2,1,0:T(8,128)S(1)}, u32[]{:S(2)}, u32[]{:S(2)}) %collective-permute-start.14) | collective-permute-done | bytes 426016 | tf_op jit(solution)/shard_map/ppermute | solution.py:526
  151.2 3.4 %shard_map.94 = (f32[2,18,8,8,256]{4,3,2,1,0:T(8,128)S(1)}, f32[16,8,8,256]{3,2,1,0:T(8,128)S(1)}) custom-call(s32[3]{0:T(128)S(1)} %copy-done.10, f32[2,208,256]{2,1,0:T(8,128)S(1)} %copy-done.9, f32[2,208,256]{2,1,0:T(8,128)S(1)} %collective-permute-done.2.refs_1_, f32[2,208,256]{2,1,0:T(8,128)S(1)} %collective-permute-done.3.refs_2_, ...), custom_call_target="tpu_custom_call" | custom-call | tf_op jit(solution)/shard_map/pallas_call | solution.py:598
  156.7 7.3 %shard_map.95 = f32[8,2,2,8,8,256]{5,4,3,2,1,0:T(8,128)S(1)} custom-call(s32[3]{0:T(128)S(1)} %copy-done.10, f32[16,8,8,256]{3,2,1,0:T(8,128)S(1)} %copy-done.4, f32[9,8,8,256]{3,2,1,0:T(8,128)S(1)} %copy-done.6, f32[9,8,8,256]{3,2,1,0:T(8,128)S(1)} %copy-done.8, f32[18,8,8,256]{3,2,1,0:T(8,128)S(1)} %copy-done, ...), custom_call_target="tpu_custom_call" | custom-call | tf_op jit(solution)/shard_map/pallas_call | solution.py:605
  164.1 33.1 %all_to_all.20.received = f32[8,2,2,8,8,256]{5,4,3,2,1,0:T(8,128)S(1)} all-to-all(f32[8,2,2,8,8,256]{5,4,3,2,1,0:T(8,128)S(1)} %shard_map.95), channel_id=1, replica_groups=mesh['tm'=8,'space'=16] {'tm'}, dimensions={0} | all-to-all | bytes 4194304 | tf_op jit(solution)/shard_map/all_to_all | solution.py:629
  197.1 1.8 shard_map.96
  198.9 34.1 %all_to_all.21.received = f32[128,2,8,256]{3,2,1,0:T(8,128)S(1)} all-to-all(f32[128,2,8,256]{3,2,1,0:T(8,128)S(1)} %shard_map.96), channel_id=1, replica_groups=mesh['tm'=8,'space'=16] {'tm','space'}, dimensions={0} | all-to-all | bytes 4194304 | tf_op jit(solution)/shard_map/all_to_all | solution.py:642
  233.0 2.7 %shard_map.97 = (f32[1,4,256,256]{3,2,1,0:T(8,128)}, f32[4,256,256]{2,1,0:T(8,128)}) custom-call(f32[128,2,8,256]{3,2,1,0:T(8,128)S(1)} %all_to_all.21.received), custom_call_target="tpu_custom_call" | custom-call | tf_op jit(solution)/shard_map/pallas_call | solution.py:643
  (57 shorter events, 12.0 us)
Async XLA Ops:
  0.6 8.4 %copy-start.12 = (f32[4,256,256]{2,1,0:T(8,128)S(1)}, f32[4,256,256]{2,1,0:T(8,128)}, u32[]{:S(2)}) copy-start(f32[4,256,256]{2,1,0:T(8,128)} %param.11) | copy-start | bytes 3145732
  0.6 8.4 %copy-start.13 = (f32[1,4,256,256]{3,2,1,0:T(8,128)S(1)}, f32[1,4,256,256]{3,2,1,0:T(8,128)}, u32[]{:S(2)}) copy-start(f32[1,4,256,256]{3,2,1,0:T(8,128)} %param.7) | copy-start | bytes 3145732
  3.1 24.5 %all-to-all-start = ((f32[16,4,16,256]{3,2,1,0:T(8,128)}), f32[16,4,16,256]{3,2,1,0:T(8,128)S(1)}, u32[]{:S(2)}, u32[]{:S(2)}) async-start(f32[16,4,16,256]{3,2,1,0:T(8,128)} %shard_map.86), calls=%async_computation | async-start | bytes 2097152 | tf_op jit(solution)/shard_map/all_to_all | solution.py:558
  10.1 37.7 %collective-permute-start = (f32[4,256,256]{2,1,0:T(8,128)}, f32[4,256,256]{2,1,0:T(8,128)}, u32[]{:S(2)}, u32[]{:S(2)}) collective-permute-start(f32[4,256,256]{2,1,0:T(8,128)} %bitcast_select_fusion), channel_id=1, source_target_pairs={{0,112},{16,0},{32,16},{48,32},{64,48},{80,64},{96,80},{112,96},{1... | collective-permute-start | bytes 3145736 | tf_op jit(solution)/shard_map/ppermute | solution.py:548
  27.7 31.1 %collective-permute-start.1 = (f32[8,208,256]{2,1,0:T(8,128)}, f32[8,208,256]{2,1,0:T(8,128)}, u32[]{:S(2)}, u32[]{:S(2)}) collective-permute-start(f32[8,208,256]{2,1,0:T(8,128)} %shard_map.87), channel_id=1, source_target_pairs={{0,1},{1,0},{2,3},{3,2},{4,5},{5,4},{6,7},{7,6},{8,9},{9,8},{10,11... | collective-permute-start | bytes 5111816 | tf_op jit(solution)/shard_map/ppermute | solution.py:562
  28.5 1.0 copy-start.3
  50.2 21.4 %all-to-all-start.1 = ((f32[16,4,16,256]{3,2,1,0:T(8,128)}), f32[16,4,16,256]{3,2,1,0:T(8,128)S(1)}, u32[]{:S(2)}, u32[]{:S(2)}) async-start(f32[16,4,16,256]{3,2,1,0:T(8,128)} %shard_map.89), calls=%async_computation.1 | async-start | bytes 2097152 | tf_op jit(solution)/shard_map/all_to_all | solution.py:564
  55.1 24.4 %collective-permute-start.6 = (f32[9,8,8,256]{3,2,1,0:T(8,128)S(1)}, f32[9,8,8,256]{3,2,1,0:T(8,128)S(1)}, u32[]{:S(2)}, u32[]{:S(2)}) collective-permute-start(f32[9,8,8,256]{3,2,1,0:T(8,128)S(1)} %get-tuple-element.73), channel_id=1, source_target_pairs={{0,1},{1,2},{2,3},{3,6},{6,7},{7,4},{4,5},{5,8},{8,9},{9,10},{10,1... | collective-permute-start | bytes 1769480 | tf_op jit(solution)/shard_map/ppermute | solution.py:530
  57.4 22.3 %collective-permute-start.7 = (f32[9,8,8,256]{3,2,1,0:T(8,128)S(1)}, f32[9,8,8,256]{3,2,1,0:T(8,128)}, u32[]{:S(2)}, u32[]{:S(2)}) collective-permute-start(f32[9,8,8,256]{3,2,1,0:T(8,128)S(1)} %get-tuple-element.74), channel_id=1, source_target_pairs={{1,0},{2,1},{3,2},{6,3},{7,6},{4,7},{5,4},{8,5},{9,8},{10,9},{11,1... | collective-permute-start | bytes 1769480 | tf_op jit(solution)/shard_map/ppermute | solution.py:530
  72.5 1.0 copy-start.1
  73.4 8.7 %collective-permute-start.8 = (f32[8,8,8,256]{3,2,1,0:T(8,128)S(1)}, f32[8,8,8,256]{3,2,1,0:T(8,128)S(1)}, u32[]{:S(2)}, u32[]{:S(2)}) collective-permute-start(f32[8,8,8,256]{3,2,1,0:T(8,128)S(1)} %get-tuple-element.77), channel_id=1, source_target_pairs={{0,1},{1,2},{2,3},{3,6},{6,7},{7,4},{4,5},{5,8},{8,9},{9,10},{10,1... | collective-permute-start | bytes 1572872 | tf_op jit(solution)/shard_map/ppermute | solution.py:530
  74.9 15.1 %collective-permute-start.9 = (f32[8,8,8,256]{3,2,1,0:T(8,128)S(1)}, f32[8,8,8,256]{3,2,1,0:T(8,128)}, u32[]{:S(2)}, u32[]{:S(2)}) collective-permute-start(f32[8,8,8,256]{3,2,1,0:T(8,128)S(1)} %get-tuple-element.78), channel_id=1, source_target_pairs={{1,0},{2,1},{3,2},{6,3},{7,6},{4,7},{5,4},{8,5},{9,8},{10,9},{11,1... | collective-permute-start | bytes 1572872 | tf_op jit(solution)/shard_map/ppermute | solution.py:530
  76.2 28.4 %collective-permute-start.2 = (f32[2,208,256]{2,1,0:T(8,128)}, f32[2,208,256]{2,1,0:T(8,128)S(1)}, u32[]{:S(2)}, u32[]{:S(2)}) collective-permute-start(f32[2,208,256]{2,1,0:T(8,128)} %get-tuple-element.68), channel_id=1, source_target_pairs={{0,2},{1,3},{2,0},{3,1},{4,6},{5,7},{6,4},{7,5},{8,10},{9,11},{10,... | collective-permute-start | bytes 1277960 | tf_op jit(solution)/shard_map/ppermute | solution.py:526
  79.5 10.6 %copy-start.11 = (f32[9,8,8,256]{3,2,1,0:T(8,128)}, f32[9,8,8,256]{3,2,1,0:T(8,128)S(1)}, u32[]{:S(2)}) copy-start(f32[9,8,8,256]{3,2,1,0:T(8,128)S(1)} %collective-permute-done.6.above_k) | copy-start | bytes 1769476
  79.5 25.1 %collective-permute-start.3 = (f32[2,208,256]{2,1,0:T(8,128)}, f32[2,208,256]{2,1,0:T(8,128)S(1)}, u32[]{:S(2)}, u32[]{:S(2)}) collective-permute-start(f32[2,208,256]{2,1,0:T(8,128)} %get-tuple-element.69), channel_id=1, source_target_pairs={{0,4},{1,5},{2,6},{3,7},{4,0},{5,1},{6,2},{7,3},{8,12},{9,13},{10,... | collective-permute-start | bytes 1277960 | tf_op jit(solution)/shard_map/ppermute | solution.py:526
  79.7 24.9 %collective-permute-start.4 = (f32[2,208,256]{2,1,0:T(8,128)}, f32[2,208,256]{2,1,0:T(8,128)S(1)}, u32[]{:S(2)}, u32[]{:S(2)}) collective-permute-start(f32[2,208,256]{2,1,0:T(8,128)} %get-tuple-element.70), channel_id=1, source_target_pairs={{0,12},{1,13},{2,14},{3,15},{4,8},{5,9},{6,10},{7,11},{8,4},{9,5},... | collective-permute-start | bytes 1277960 | tf_op jit(solution)/shard_map/ppermute | solution.py:526
  82.1 0.8 copy-start.14
  82.9 21.7 %collective-permute-start.5 = (f32[2,208,256]{2,1,0:T(8,128)}, f32[2,208,256]{2,1,0:T(8,128)S(1)}, u32[]{:S(2)}, u32[]{:S(2)}) collective-permute-start(f32[2,208,256]{2,1,0:T(8,128)} %get-tuple-element.71), channel_id=1, source_target_pairs={{0,10},{1,11},{2,8},{3,9},{4,14},{5,15},{6,12},{7,13},{8,2},{9,3},... | collective-permute-start | bytes 1277960 | tf_op jit(solution)/shard_map/ppermute | solution.py:526
  104.6 46.6 %copy-start.9 = (f32[2,208,256]{2,1,0:T(8,128)S(1)}, f32[2,208,256]{2,1,0:T(8,128)}, u32[]{:S(2)}) copy-start(f32[2,208,256]{2,1,0:T(8,128)} %get-tuple-element.97.refs_0_) | copy-start | bytes 1277956
  104.6 46.5 %copy-start.10 = (s32[3]{0:T(128)S(1)}, s32[3]{0:T(128)}, u32[]{:S(2)}) copy-start(s32[3]{0:T(128)} %pad_add_fusion.ids) | copy-start | bytes 40
  104.7 5.9 %collective-permute-start.10 = (f32[9,8,8,256]{3,2,1,0:T(8,128)}, f32[9,8,8,256]{3,2,1,0:T(8,128)S(1)}, u32[]{:S(2)}, u32[]{:S(2)}) collective-permute-start(f32[9,8,8,256]{3,2,1,0:T(8,128)} %get-tuple-element.89), channel_id=1, source_target_pairs={{0,1},{1,2},{2,3},{3,6},{6,7},{7,4},{4,5},{5,8},{8,9},{9,10},{10,1... | collective-permute-start | bytes 1769480 | tf_op jit(solution)/shard_map/ppermute | solution.py:530
  108.8 4.1 %collective-permute-start.11 = (f32[9,8,8,256]{3,2,1,0:T(8,128)}, f32[9,8,8,256]{3,2,1,0:T(8,128)S(1)}, u32[]{:S(2)}, u32[]{:S(2)}) collective-permute-start(f32[9,8,8,256]{3,2,1,0:T(8,128)} %get-tuple-element.90), channel_id=1, source_target_pairs={{1,0},{2,1},{3,2},{6,3},{7,6},{4,7},{5,4},{8,5},{9,8},{10,9},{11,1... | collective-permute-start | bytes 1769480 | tf_op jit(solution)/shard_map/ppermute | solution.py:530
  110.5 13.5 %copy-start.5 = (f32[9,8,8,256]{3,2,1,0:T(8,128)}, f32[9,8,8,256]{3,2,1,0:T(8,128)S(1)}, u32[]{:S(2)}) copy-start(f32[9,8,8,256]{3,2,1,0:T(8,128)S(1)} %collective-permute-done.10.above.late_above) | copy-start | bytes 1769476
  112.9 11.2 %copy-start.7 = (f32[9,8,8,256]{3,2,1,0:T(8,128)}, f32[9,8,8,256]{3,2,1,0:T(8,128)S(1)}, u32[]{:S(2)}) copy-start(f32[9,8,8,256]{3,2,1,0:T(8,128)S(1)} %collective-permute-done.11.below.late_below) | copy-start | bytes 1769476
  112.9 25.9 %collective-permute-start.12 = (f32[2,208,256]{2,1,0:T(8,128)}, f32[2,208,256]{2,1,0:T(8,128)S(1)}, u32[]{:S(2)}, u32[]{:S(2)}) collective-permute-start(f32[2,208,256]{2,1,0:T(8,128)} %get-tuple-element.91), channel_id=1, source_target_pairs={{0,6},{1,7},{2,4},{3,5},{4,2},{5,3},{6,0},{7,1},{8,14},{9,15},{10,... | collective-permute-start | bytes 1277960 | tf_op jit(solution)/shard_map/ppermute | solution.py:526
  120.4 26.6 %collective-permute-start.13 = (f32[2,208,256]{2,1,0:T(8,128)}, f32[2,208,256]{2,1,0:T(8,128)S(1)}, u32[]{:S(2)}, u32[]{:S(2)}) collective-permute-start(f32[2,208,256]{2,1,0:T(8,128)} %get-tuple-element.92), channel_id=1, source_target_pairs={{0,14},{1,15},{2,12},{3,13},{4,10},{5,11},{6,8},{7,9},{8,6},{9,7},... | collective-permute-start | bytes 1277960 | tf_op jit(solution)/shard_map/ppermute | solution.py:526
  124.1 27.1 %collective-permute-start.14 = (f32[2,208,256]{2,1,0:T(8,128)}, f32[2,208,256]{2,1,0:T(8,128)S(1)}, u32[]{:S(2)}, u32[]{:S(2)}) collective-permute-start(f32[2,208,256]{2,1,0:T(8,128)} %get-tuple-element.93), channel_id=1, source_target_pairs={{0,8},{1,9},{2,10},{3,11},{4,12},{5,13},{6,14},{7,15},{8,0},{9,1},... | collective-permute-start | bytes 1277960 | tf_op jit(solution)/shard_map/ppermute | solution.py:526
  138.7 15.9 %copy-start = (f32[18,8,8,256]{3,2,1,0:T(8,128)S(1)}, f32[18,8,8,256]{3,2,1,0:T(8,128)}, u32[]{:S(2)}) copy-start(f32[18,8,8,256]{3,2,1,0:T(8,128)} %shard_map.93.early) | copy-start | bytes 3538948
  138.7 15.9 %copy-start.2 = (f32[16,8,8,256]{3,2,1,0:T(8,128)S(1)}, f32[16,8,8,256]{3,2,1,0:T(8,128)}, u32[]{:S(2)}) copy-start(f32[16,8,8,256]{3,2,1,0:T(8,128)} %copy-done.1) | copy-start | bytes 3145732
  138.7 15.9 %copy-start.4 = (f32[16,8,8,256]{3,2,1,0:T(8,128)S(1)}, f32[16,8,8,256]{3,2,1,0:T(8,128)}, u32[]{:S(2)}) copy-start(f32[16,8,8,256]{3,2,1,0:T(8,128)} %get-tuple-element.94.own.late) | copy-start | bytes 3145732
  154.6 1.1 copy-start.6
  155.7 1.1 copy-start.8

commit v3 on v2

--- a/solution.py
+++ b/solution.py
@@ -555,13 +555,14 @@
         [DMA((CHIPS, 3 * PLANES + 1))],
         56,
     )(ids, forward_states, coarse_rate, edges)
+    conductivity, other = lax.optimization_barrier((conductivity, other))
     received = lax.all_to_all(spread(conductivity), "space", 0, 0)
-    received, other = lax.optimization_barrier((received, other))
+    sent = spread(ends)
+    received, sent = lax.optimization_barrier((received, sent))
     own_k, up, down = unpack(received, HALO)
     above_k, below_k = along_chain(up, down)
     other = lax.ppermute(other, "space", masks[1])
-    ends, own_k = lax.optimization_barrier((ends, own_k))
-    received = lax.all_to_all(spread(ends), "space", 0, 0)
+    received = lax.all_to_all(sent, "space", 0, 0)
     pieces = call(
         pack_states,
         [struct(2, DEPTH, NY)] * CHIPS,

time: 237 us -> 233 us (0.983)
  waiting for transfers between devices: 45.1 us -> 22.6 us
  starting transfers between devices: 50.3 us -> 58.9 us
  blocking collectives: 67.1 us -> 74.2 us
    all_to_all x1, blocking collectives: 34.1 us -> 46.6 us  [per_device(): results = lax.all_to_all(results, ('tm', 'space'), 0, 0)]
    ppermute x7, waiting for transfers between devices: 12.5 us -> 0.02 us  [to_chips(): lax.ppermute(piece, 'space', masks[2 * step])]
    ppermute x7, starting transfers between devices: 21.7 us -> 29.3 us  [to_chips(): lax.ppermute(piece, 'space', masks[2 * step])]
    all_to_all x1, blocking collectives: 33.1 us -> 27.6 us  [per_device(): parts = lax.all_to_all(parts, 'tm', 0, 0)]
    all_to_all x1, waiting for transfers between devices: 3.93 us -> 0.22 us  [per_device(): received = lax.all_to_all(spread(conductivity), 'space', 0, 0)]
    ppermute x1, waiting for transfers between devices: 18.4 us -> 14.8 us  [per_device(): ends = lax.ppermute(first, 'tm', [(t, (t - 1) % NT) for t in range(NT)])]
    all_to_all x1, waiting for transfers between devices: 7.44 us -> 4.77 us  [per_device(): received = lax.all_to_all(sent, 'space', 0, 0)]
    unnamed x30 -> x32, local copies, waits for them, and re-layouts: 4.89 us -> 5.89 us
  transfers between devices with their start and end apart: 17 -> 17, of which waited for: 7 -> 5; matrix products, arithmetic and copies ran while one was open for 2% -> 2% of each run, Pallas kernels for 18% -> 20%
where the time goes in v3:
time: 233 us; the launch traced here: 231 us
  blocking collectives  74.2 us (32%)
  Pallas kernels  61.3 us (26%)
  starting transfers between devices  58.9 us (25%)
  waiting for transfers between devices  22.6 us (10%)
  local copies, waits for them, and re-layouts  9.15 us (4%)
  between operations  2.8 us (1%)
  other arithmetic  2.36 us (1%)
    all_to_all x1, blocking collectives, per_device(): results = lax.all_to_all(results, ('tm', 'space'), 0, 0)  46.6 us
    ppermute x7, starting transfers between devices, to_chips(): lax.ppermute(piece, 'space', masks[2 * step])  29.3 us
    all_to_all x1, blocking collectives, per_device(): parts = lax.all_to_all(parts, 'tm', 0, 0)  27.6 us
    ppermute x1, waiting for transfers between devices, per_device(): ends = lax.ppermute(first, 'tm', [(t, (t - 1) % NT) for t in range(NT)])  14.8 us
    pallas_call x1, Pallas kernels, per_device(): call(solve(HALO - 1), [struct(*block), struct(HALO, 8, 8, NY), struct(HAL...  14.7 us
    pallas_call x1, Pallas kernels, per_device(): call(solve(HALO), struct(*wide), [SMEM] * 2 + [ANY] * 6, ANY, SOLVE_SCRAT...  14.6 us
    ppermute x3, starting transfers between devices, along_chain(): lax.ppermute(down, 'space', forward)  8.75 us
    pallas_call x1, Pallas kernels, per_device(): call(face_sums, struct(NT, 2, 2, 8, 8, NY), [SMEM] + [ANY] * 7, VMEM, [pl...  7.34 us
  transfers between devices with their start and end apart: 17, of which 5 were waited for; matrix products, arithmetic and copies ran while one was open for 2% of the time, Pallas kernels for 20%

profile of v3, /device:TPU:0, one launch (start us, length us, event | category | flops | bytes accessed | tf_op | source)
XLA Modules:
  0.0 231.3 jit_solution(2265928122096707567)
XLA Ops:
  0.6 1.7 bitcast_select_fusion
  2.3 6.2 %collective-permute-start = (f32[4,256,256]{2,1,0:T(8,128)S(1)}, f32[4,256,256]{2,1,0:T(8,128)S(1)}, u32[]{:S(2)}, u32[]{:S(2)}) collective-permute-start(f32[4,256,256]{2,1,0:T(8,128)S(1)} %bitcast_select_fusion), channel_id=1, source_target_pairs={{0,112},{16,0},{32,16},{48,32},{64,48},{80,64},{96,80},{112,96},{1... | collective-permute-start | bytes 3145736 | tf_op jit(solution)/shard_map/ppermute | solution.py:548
  8.5 1.7 fusion
  11.8 4.2 %shard_map.86 = f32[8,208,256]{2,1,0:T(8,128)} custom-call(s32[3]{0:T(128)} %pad_add_fusion.ids, f32[1,2,4,256,256]{4,3,2,1,0:T(8,128)} %states.3, f32[4,256,256]{2,1,0:T(8,128)} %rate.3, f32[16,16,256]{2,1,0:T(8,128)} %reshape.25.edges), custom_call_target="tpu_custom_call" | custom-call | tf_op jit(solution)/shard_map/pallas_call | solution.py:550
  16.0 2.4 %shard_map.87 = f32[16,4,16,256]{3,2,1,0:T(8,128)} custom-call(f32[4,256,256]{2,1,0:T(8,128)} %field), custom_call_target="tpu_custom_call" | custom-call | tf_op jit(solution)/shard_map/pallas_call | solution.py:534
  18.4 4.9 %all-to-all-start = ((f32[16,4,16,256]{3,2,1,0:T(8,128)}), f32[16,4,16,256]{3,2,1,0:T(8,128)S(1)}, u32[]{:S(2)}, u32[]{:S(2)}) async-start(f32[16,4,16,256]{3,2,1,0:T(8,128)} %shard_map.87), calls=%async_computation | async-start | bytes 2097152 | tf_op jit(solution)/shard_map/all_to_all | solution.py:559
  23.7 14.8 %collective-permute-done.field = f32[4,256,256]{2,1,0:T(8,128)S(1)} collective-permute-done((f32[4,256,256]{2,1,0:T(8,128)S(1)}, f32[4,256,256]{2,1,0:T(8,128)S(1)}, u32[]{:S(2)}, u32[]{:S(2)}) %collective-permute-start) | collective-permute-done | bytes 1048608 | tf_op jit(solution)/shard_map/ppermute | solution.py:548
  39.4 2.4 %shard_map.88 = f32[16,4,16,256]{3,2,1,0:T(8,128)} custom-call(f32[4,256,256]{2,1,0:T(8,128)} %copy-done.11), custom_call_target="tpu_custom_call" | custom-call | tf_op jit(solution)/shard_map/pallas_call | solution.py:534
  42.0 5.6 %all-to-all-start.1 = ((f32[16,4,16,256]{3,2,1,0:T(8,128)}), f32[16,4,16,256]{3,2,1,0:T(8,128)S(1)}, u32[]{:S(2)}, u32[]{:S(2)}) async-start(f32[16,4,16,256]{3,2,1,0:T(8,128)} %shard_map.88), calls=%async_computation.1 | async-start | bytes 2097152 | tf_op jit(solution)/shard_map/all_to_all | solution.py:565
  49.4 3.1 %collective-permute-start.6 = (f32[9,8,8,256]{3,2,1,0:T(8,128)S(1)}, f32[9,8,8,256]{3,2,1,0:T(8,128)}, u32[]{:S(2)}, u32[]{:S(2)}) collective-permute-start(f32[9,8,8,256]{3,2,1,0:T(8,128)S(1)} %get-tuple-element.73), channel_id=1, source_target_pairs={{0,1},{1,2},{2,3},{3,6},{6,7},{7,4},{4,5},{5,8},{8,9},{9,10},{10,1... | collective-permute-start | bytes 1769480 | tf_op jit(solution)/shard_map/ppermute | solution.py:530
  52.5 1.3 collective-permute-start.7
  53.8 5.5 %shard_map.89 = (f32[2,208,256]{2,1,0:T(8,128)}, f32[2,208,256]{2,1,0:T(8,128)}, f32[2,208,256]{2,1,0:T(8,128)}, f32[2,208,256]{2,1,0:T(8,128)}, f32[2,208,256]{...) custom-call(s32[3]{0:T(128)} %pad_add_fusion.ids, ...), custom_call_target="tpu_custom_call" | custom-call | tf_op jit(solution)/shard_map/pallas_call | solution.py:566
  59.4 4.8 %all-to-all-done.1.received = f32[16,4,16,256]{3,2,1,0:T(8,128)S(1)} async-done(((f32[16,4,16,256]{3,2,1,0:T(8,128)}), f32[16,4,16,256]{3,2,1,0:T(8,128)S(1)}, u32[]{:S(2)}, u32[]{:S(2)}) %all-to-all-start.1) | async-done | bytes 1048608 | tf_op jit(solution)/shard_map/all_to_all | solution.py:565
  64.1 1.6 shard_map.91
  66.7 1.5 collective-permute-start.8
  68.2 1.3 collective-permute-start.9
  69.5 3.3 %collective-permute-start.2 = (f32[2,208,256]{2,1,0:T(8,128)}, f32[2,208,256]{2,1,0:T(8,128)S(1)}, u32[]{:S(2)}, u32[]{:S(2)}) collective-permute-start(f32[2,208,256]{2,1,0:T(8,128)} %get-tuple-element.67), channel_id=1, source_target_pairs={{0,2},{1,3},{2,0},{3,1},{4,6},{5,7},{6,4},{7,5},{8,10},{9,11},{10,... | collective-permute-start | bytes 1277960 | tf_op jit(solution)/shard_map/ppermute | solution.py:526
  73.0 2.4 %collective-permute-start.4 = (f32[2,208,256]{2,1,0:T(8,128)}, f32[2,208,256]{2,1,0:T(8,128)S(1)}, u32[]{:S(2)}, u32[]{:S(2)}) collective-permute-start(f32[2,208,256]{2,1,0:T(8,128)} %get-tuple-element.69), channel_id=1, source_target_pairs={{0,12},{1,13},{2,14},{3,15},{4,8},{5,9},{6,10},{7,11},{8,4},{9,5},... | collective-permute-start | bytes 1277960 | tf_op jit(solution)/shard_map/ppermute | solution.py:526
  76.2 4.7 %collective-permute-start.5 = (f32[2,208,256]{2,1,0:T(8,128)}, f32[2,208,256]{2,1,0:T(8,128)S(1)}, u32[]{:S(2)}, u32[]{:S(2)}) collective-permute-start(f32[2,208,256]{2,1,0:T(8,128)} %get-tuple-element.70), channel_id=1, source_target_pairs={{0,10},{1,11},{2,8},{3,9},{4,14},{5,15},{6,12},{7,13},{8,2},{9,3},... | collective-permute-start | bytes 1277960 | tf_op jit(solution)/shard_map/ppermute | solution.py:526
  83.3 14.7 %shard_map.92 = (f32[16,8,8,256]{3,2,1,0:T(8,128)}, f32[9,8,8,256]{3,2,1,0:T(8,128)}, f32[9,8,8,256]{3,2,1,0:T(8,128)}) custom-call(s32[3]{0:T(128)} %pad_add_fusion.ids, f32[19]{0:T(128)} %stack.69.weights, f32[16,8,8,256]{3,2,1,0:T(8,128)} %copy-done.3, f32[9,8,8,256]{3,2,1,0:T(8,128)} %collective-permute-done.6.above_k, ...), custom_call_target="tpu_custom_call" | custom-call | tf_op jit(solution)/shard_map/pallas_call | solution.py:579
  98.1 4.1 %collective-permute-start.10 = (f32[9,8,8,256]{3,2,1,0:T(8,128)}, f32[9,8,8,256]{3,2,1,0:T(8,128)S(1)}, u32[]{:S(2)}, u32[]{:S(2)}) collective-permute-start(f32[9,8,8,256]{3,2,1,0:T(8,128)} %get-tuple-element.89), channel_id=1, source_target_pairs={{0,1},{1,2},{2,3},{3,6},{6,7},{7,4},{4,5},{5,8},{8,9},{9,10},{10,1... | collective-permute-start | bytes 1769480 | tf_op jit(solution)/shard_map/ppermute | solution.py:530
  102.2 1.3 collective-permute-start.11
  104.0 2.3 %collective-permute-done.11.below.late_below = f32[9,8,8,256]{3,2,1,0:T(8,128)S(1)} collective-permute-done((f32[9,8,8,256]{3,2,1,0:T(8,128)}, f32[9,8,8,256]{3,2,1,0:T(8,128)S(1)}, u32[]{:S(2)}, u32[]{:S(2)}) %collective-permute-start.11) | collective-permute-done | bytes 589856 | tf_op jit(solution)/shard_map/ppermute | solution.py:530
  106.3 7.5 %collective-permute-start.12 = (f32[2,208,256]{2,1,0:T(8,128)S(1)}, f32[2,208,256]{2,1,0:T(8,128)S(1)}, u32[]{:S(2)}, u32[]{:S(2)}) collective-permute-start(f32[2,208,256]{2,1,0:T(8,128)S(1)} %copy-done.15), channel_id=1, source_target_pairs={{0,6},{1,7},{2,4},{3,5},{4,2},{5,3},{6,0},{7,1},{8,14},{9,15},{10,... | collective-permute-start | bytes 1277960 | tf_op jit(solution)/shard_map/ppermute | solution.py:526
  113.8 11.2 %collective-permute-start.13 = (f32[2,208,256]{2,1,0:T(8,128)S(1)}, f32[2,208,256]{2,1,0:T(8,128)S(1)}, u32[]{:S(2)}, u32[]{:S(2)}) collective-permute-start(f32[2,208,256]{2,1,0:T(8,128)S(1)} %copy-done.14), channel_id=1, source_target_pairs={{0,14},{1,15},{2,12},{3,13},{4,10},{5,11},{6,8},{7,9},{8,6},{9,7},... | collective-permute-start | bytes 1277960 | tf_op jit(solution)/shard_map/ppermute | solution.py:526
  125.1 14.6 %shard_map.93.early = f32[18,8,8,256]{3,2,1,0:T(8,128)} custom-call(s32[3]{0:T(128)} %pad_add_fusion.ids, f32[19]{0:T(128)} %stack.69.weights, f32[16,8,8,256]{3,2,1,0:T(8,128)} %copy-done.3, f32[9,8,8,256]{3,2,1,0:T(8,128)} %collective-permute-done.6.above_k, f32[9,8,8,256]{3,2,1,0:T(8,128)} %collective-permute-done.7.below_k, ...), custom_call_target="tpu_custom_call" | custom-call | tf_op jit(solution)/shard_map/pallas_call | solution.py:594
  139.7 3.4 %shard_map.94 = (f32[2,18,8,8,256]{4,3,2,1,0:T(8,128)S(1)}, f32[16,8,8,256]{3,2,1,0:T(8,128)S(1)}) custom-call(s32[3]{0:T(128)S(1)} %copy-done.10, f32[2,208,256]{2,1,0:T(8,128)S(1)} %copy-done.9, f32[2,208,256]{2,1,0:T(8,128)S(1)} %collective-permute-done.2.refs_1_, f32[2,208,256]{2,1,0:T(8,128)S(1)} %collective-permute-done.3.refs_2_, ...), custom_call_target="tpu_custom_call" | custom-call | tf_op jit(solution)/shard_map/pallas_call | solution.py:599
  145.3 7.3 %shard_map.95 = f32[8,2,2,8,8,256]{5,4,3,2,1,0:T(8,128)S(1)} custom-call(s32[3]{0:T(128)S(1)} %copy-done.10, f32[16,8,8,256]{3,2,1,0:T(8,128)S(1)} %copy-done.4, f32[9,8,8,256]{3,2,1,0:T(8,128)S(1)} %copy-done.6, f32[9,8,8,256]{3,2,1,0:T(8,128)S(1)} %copy-done.8, f32[18,8,8,256]{3,2,1,0:T(8,128)S(1)} %copy-done, ...), custom_call_target="tpu_custom_call" | custom-call | tf_op jit(solution)/shard_map/pallas_call | solution.py:606
  152.6 27.6 %all_to_all.20.received = f32[8,2,2,8,8,256]{5,4,3,2,1,0:T(8,128)S(1)} all-to-all(f32[8,2,2,8,8,256]{5,4,3,2,1,0:T(8,128)S(1)} %shard_map.95), channel_id=1, replica_groups=mesh['tm'=8,'space'=16] {'tm'}, dimensions={0} | all-to-all | bytes 4194304 | tf_op jit(solution)/shard_map/all_to_all | solution.py:630
  180.2 1.8 shard_map.96
  182.0 46.6 %all_to_all.21.received = f32[128,2,8,256]{3,2,1,0:T(8,128)S(1)} all-to-all(f32[128,2,8,256]{3,2,1,0:T(8,128)S(1)} %shard_map.96), channel_id=1, replica_groups=mesh['tm'=8,'space'=16] {'tm','space'}, dimensions={0} | all-to-all | bytes 4194304 | tf_op jit(solution)/shard_map/all_to_all | solution.py:643
  228.6 2.7 %shard_map.97 = (f32[1,4,256,256]{3,2,1,0:T(8,128)}, f32[4,256,256]{2,1,0:T(8,128)}) custom-call(f32[128,2,8,256]{3,2,1,0:T(8,128)S(1)} %all_to_all.21.received), custom_call_target="tpu_custom_call" | custom-call | tf_op jit(solution)/shard_map/pallas_call | solution.py:644
  (59 shorter events, 10.3 us)
Async XLA Ops:
  2.3 36.1 %collective-permute-start = (f32[4,256,256]{2,1,0:T(8,128)S(1)}, f32[4,256,256]{2,1,0:T(8,128)S(1)}, u32[]{:S(2)}, u32[]{:S(2)}) collective-permute-start(f32[4,256,256]{2,1,0:T(8,128)S(1)} %bitcast_select_fusion), channel_id=1, source_target_pairs={{0,112},{16,0},{32,16},{48,32},{64,48},{80,64},{96,80},{112,96},{1... | collective-permute-start | bytes 3145736 | tf_op jit(solution)/shard_map/ppermute | solution.py:548
  18.4 23.6 %all-to-all-start = ((f32[16,4,16,256]{3,2,1,0:T(8,128)}), f32[16,4,16,256]{3,2,1,0:T(8,128)S(1)}, u32[]{:S(2)}, u32[]{:S(2)}) async-start(f32[16,4,16,256]{3,2,1,0:T(8,128)} %shard_map.87), calls=%async_computation | async-start | bytes 2097152 | tf_op jit(solution)/shard_map/all_to_all | solution.py:559
  23.3 30.6 %collective-permute-start.1 = (f32[8,208,256]{2,1,0:T(8,128)}, f32[8,208,256]{2,1,0:T(8,128)}, u32[]{:S(2)}, u32[]{:S(2)}) collective-permute-start(f32[8,208,256]{2,1,0:T(8,128)} %shard_map.86), channel_id=1, source_target_pairs={{0,1},{1,0},{2,3},{3,2},{4,5},{5,4},{6,7},{7,6},{8,9},{9,8},{10,11... | collective-permute-start | bytes 5111816 | tf_op jit(solution)/shard_map/ppermute | solution.py:564
  38.5 1.0 copy-start.11
  42.0 22.1 %all-to-all-start.1 = ((f32[16,4,16,256]{3,2,1,0:T(8,128)}), f32[16,4,16,256]{3,2,1,0:T(8,128)S(1)}, u32[]{:S(2)}, u32[]{:S(2)}) async-start(f32[16,4,16,256]{3,2,1,0:T(8,128)} %shard_map.88), calls=%async_computation.1 | async-start | bytes 2097152 | tf_op jit(solution)/shard_map/all_to_all | solution.py:565
  48.4 1.0 copy-start.3
  49.4 23.4 %collective-permute-start.6 = (f32[9,8,8,256]{3,2,1,0:T(8,128)S(1)}, f32[9,8,8,256]{3,2,1,0:T(8,128)}, u32[]{:S(2)}, u32[]{:S(2)}) collective-permute-start(f32[9,8,8,256]{3,2,1,0:T(8,128)S(1)} %get-tuple-element.73), channel_id=1, source_target_pairs={{0,1},{1,2},{2,3},{3,6},{6,7},{7,4},{4,5},{5,8},{8,9},{9,10},{10,1... | collective-permute-start | bytes 1769480 | tf_op jit(solution)/shard_map/ppermute | solution.py:530
  52.5 20.5 %collective-permute-start.7 = (f32[9,8,8,256]{3,2,1,0:T(8,128)S(1)}, f32[9,8,8,256]{3,2,1,0:T(8,128)}, u32[]{:S(2)}, u32[]{:S(2)}) collective-permute-start(f32[9,8,8,256]{3,2,1,0:T(8,128)S(1)} %get-tuple-element.74), channel_id=1, source_target_pairs={{1,0},{2,1},{3,2},{6,3},{7,6},{4,7},{5,4},{8,5},{9,8},{10,9},{11,1... | collective-permute-start | bytes 1769480 | tf_op jit(solution)/shard_map/ppermute | solution.py:530
  65.7 1.0 copy-start.1
  66.7 8.7 %collective-permute-start.8 = (f32[8,8,8,256]{3,2,1,0:T(8,128)S(1)}, f32[8,8,8,256]{3,2,1,0:T(8,128)S(1)}, u32[]{:S(2)}, u32[]{:S(2)}) collective-permute-start(f32[8,8,8,256]{3,2,1,0:T(8,128)S(1)} %get-tuple-element.77), channel_id=1, source_target_pairs={{0,1},{1,2},{2,3},{3,6},{6,7},{7,4},{4,5},{5,8},{8,9},{9,10},{10,1... | collective-permute-start | bytes 1572872 | tf_op jit(solution)/shard_map/ppermute | solution.py:530
  68.2 15.1 %collective-permute-start.9 = (f32[8,8,8,256]{3,2,1,0:T(8,128)}, f32[8,8,8,256]{3,2,1,0:T(8,128)}, u32[]{:S(2)}, u32[]{:S(2)}) collective-permute-start(f32[8,8,8,256]{3,2,1,0:T(8,128)} %get-tuple-element.78), channel_id=1, source_target_pairs={{1,0},{2,1},{3,2},{6,3},{7,6},{4,7},{5,4},{8,5},{9,8},{10,9},{11,1... | collective-permute-start | bytes 1572872 | tf_op jit(solution)/shard_map/ppermute | solution.py:530
  69.5 28.5 %collective-permute-start.2 = (f32[2,208,256]{2,1,0:T(8,128)}, f32[2,208,256]{2,1,0:T(8,128)S(1)}, u32[]{:S(2)}, u32[]{:S(2)}) collective-permute-start(f32[2,208,256]{2,1,0:T(8,128)} %get-tuple-element.67), channel_id=1, source_target_pairs={{0,2},{1,3},{2,0},{3,1},{4,6},{5,7},{6,4},{7,5},{8,10},{9,11},{10,... | collective-permute-start | bytes 1277960 | tf_op jit(solution)/shard_map/ppermute | solution.py:526
  72.8 25.2 %collective-permute-start.3 = (f32[2,208,256]{2,1,0:T(8,128)}, f32[2,208,256]{2,1,0:T(8,128)S(1)}, u32[]{:S(2)}, u32[]{:S(2)}) collective-permute-start(f32[2,208,256]{2,1,0:T(8,128)} %get-tuple-element.68), channel_id=1, source_target_pairs={{0,4},{1,5},{2,6},{3,7},{4,0},{5,1},{6,2},{7,3},{8,12},{9,13},{10,... | collective-permute-start | bytes 1277960 | tf_op jit(solution)/shard_map/ppermute | solution.py:526
  73.0 25.0 %collective-permute-start.4 = (f32[2,208,256]{2,1,0:T(8,128)}, f32[2,208,256]{2,1,0:T(8,128)S(1)}, u32[]{:S(2)}, u32[]{:S(2)}) collective-permute-start(f32[2,208,256]{2,1,0:T(8,128)} %get-tuple-element.69), channel_id=1, source_target_pairs={{0,12},{1,13},{2,14},{3,15},{4,8},{5,9},{6,10},{7,11},{8,4},{9,5},... | collective-permute-start | bytes 1277960 | tf_op jit(solution)/shard_map/ppermute | solution.py:526
  76.2 21.8 %collective-permute-start.5 = (f32[2,208,256]{2,1,0:T(8,128)}, f32[2,208,256]{2,1,0:T(8,128)S(1)}, u32[]{:S(2)}, u32[]{:S(2)}) collective-permute-start(f32[2,208,256]{2,1,0:T(8,128)} %get-tuple-element.70), channel_id=1, source_target_pairs={{0,10},{1,11},{2,8},{3,9},{4,14},{5,15},{6,12},{7,13},{8,2},{9,3},... | collective-permute-start | bytes 1277960 | tf_op jit(solution)/shard_map/ppermute | solution.py:526
  83.3 23.0 %copy-start.15 = (f32[2,208,256]{2,1,0:T(8,128)S(1)}, f32[2,208,256]{2,1,0:T(8,128)}, u32[]{:S(2)}) copy-start(f32[2,208,256]{2,1,0:T(8,128)} %get-tuple-element.91) | copy-start | bytes 1277956
  83.3 30.5 %copy-start.14 = (f32[2,208,256]{2,1,0:T(8,128)S(1)}, f32[2,208,256]{2,1,0:T(8,128)}, u32[]{:S(2)}) copy-start(f32[2,208,256]{2,1,0:T(8,128)} %get-tuple-element.92) | copy-start | bytes 1277956
  83.3 41.7 %copy-start.13 = (f32[2,208,256]{2,1,0:T(8,128)S(1)}, f32[2,208,256]{2,1,0:T(8,128)}, u32[]{:S(2)}) copy-start(f32[2,208,256]{2,1,0:T(8,128)} %get-tuple-element.93) | copy-start | bytes 1277956
  98.0 41.7 %copy-start.9 = (f32[2,208,256]{2,1,0:T(8,128)S(1)}, f32[2,208,256]{2,1,0:T(8,128)}, u32[]{:S(2)}) copy-start(f32[2,208,256]{2,1,0:T(8,128)} %get-tuple-element.97.refs_0_) | copy-start | bytes 1277956
  98.1 41.7 %copy-start.10 = (s32[3]{0:T(128)S(1)}, s32[3]{0:T(128)}, u32[]{:S(2)}) copy-start(s32[3]{0:T(128)} %pad_add_fusion.ids) | copy-start | bytes 40
  98.1 5.9 %collective-permute-start.10 = (f32[9,8,8,256]{3,2,1,0:T(8,128)}, f32[9,8,8,256]{3,2,1,0:T(8,128)S(1)}, u32[]{:S(2)}, u32[]{:S(2)}) collective-permute-start(f32[9,8,8,256]{3,2,1,0:T(8,128)} %get-tuple-element.89), channel_id=1, source_target_pairs={{0,1},{1,2},{2,3},{3,6},{6,7},{7,4},{4,5},{5,8},{8,9},{9,10},{10,1... | collective-permute-start | bytes 1769480 | tf_op jit(solution)/shard_map/ppermute | solution.py:530
  102.2 4.1 %collective-permute-start.11 = (f32[9,8,8,256]{3,2,1,0:T(8,128)}, f32[9,8,8,256]{3,2,1,0:T(8,128)S(1)}, u32[]{:S(2)}, u32[]{:S(2)}) collective-permute-start(f32[9,8,8,256]{3,2,1,0:T(8,128)} %get-tuple-element.90), channel_id=1, source_target_pairs={{1,0},{2,1},{3,2},{6,3},{7,6},{4,7},{5,4},{8,5},{9,8},{10,9},{11,1... | collective-permute-start | bytes 1769480 | tf_op jit(solution)/shard_map/ppermute | solution.py:530
  104.0 21.1 %copy-start.5 = (f32[9,8,8,256]{3,2,1,0:T(8,128)}, f32[9,8,8,256]{3,2,1,0:T(8,128)S(1)}, u32[]{:S(2)}) copy-start(f32[9,8,8,256]{3,2,1,0:T(8,128)S(1)} %collective-permute-done.10.above.late_above) | copy-start | bytes 1769476
  106.3 18.8 %copy-start.7 = (f32[9,8,8,256]{3,2,1,0:T(8,128)}, f32[9,8,8,256]{3,2,1,0:T(8,128)S(1)}, u32[]{:S(2)}) copy-start(f32[9,8,8,256]{3,2,1,0:T(8,128)S(1)} %collective-permute-done.11.below.late_below) | copy-start | bytes 1769476
  106.3 33.4 %collective-permute-start.12 = (f32[2,208,256]{2,1,0:T(8,128)S(1)}, f32[2,208,256]{2,1,0:T(8,128)S(1)}, u32[]{:S(2)}, u32[]{:S(2)}) collective-permute-start(f32[2,208,256]{2,1,0:T(8,128)S(1)} %copy-done.15), channel_id=1, source_target_pairs={{0,6},{1,7},{2,4},{3,5},{4,2},{5,3},{6,0},{7,1},{8,14},{9,15},{10,... | collective-permute-start | bytes 1277960 | tf_op jit(solution)/shard_map/ppermute | solution.py:526
  113.8 25.9 %collective-permute-start.13 = (f32[2,208,256]{2,1,0:T(8,128)S(1)}, f32[2,208,256]{2,1,0:T(8,128)S(1)}, u32[]{:S(2)}, u32[]{:S(2)}) collective-permute-start(f32[2,208,256]{2,1,0:T(8,128)S(1)} %copy-done.14), channel_id=1, source_target_pairs={{0,14},{1,15},{2,12},{3,13},{4,10},{5,11},{6,8},{7,9},{8,6},{9,7},... | collective-permute-start | bytes 1277960 | tf_op jit(solution)/shard_map/ppermute | solution.py:526
  125.0 14.6 %collective-permute-start.14 = (f32[2,208,256]{2,1,0:T(8,128)S(1)}, f32[2,208,256]{2,1,0:T(8,128)S(1)}, u32[]{:S(2)}, u32[]{:S(2)}) collective-permute-start(f32[2,208,256]{2,1,0:T(8,128)S(1)} %copy-done.13), channel_id=1, source_target_pairs={{0,8},{1,9},{2,10},{3,11},{4,12},{5,13},{6,14},{7,15},{8,0},{9,1},... | collective-permute-start | bytes 1277960 | tf_op jit(solution)/shard_map/ppermute | solution.py:526
  139.6 3.5 %copy-start = (f32[18,8,8,256]{3,2,1,0:T(8,128)S(1)}, f32[18,8,8,256]{3,2,1,0:T(8,128)}, u32[]{:S(2)}) copy-start(f32[18,8,8,256]{3,2,1,0:T(8,128)} %shard_map.93.early) | copy-start | bytes 3538948
  139.6 3.5 %copy-start.2 = (f32[16,8,8,256]{3,2,1,0:T(8,128)S(1)}, f32[16,8,8,256]{3,2,1,0:T(8,128)}, u32[]{:S(2)}) copy-start(f32[16,8,8,256]{3,2,1,0:T(8,128)} %copy-done.1) | copy-start | bytes 3145732
  139.7 3.5 %copy-start.4 = (f32[16,8,8,256]{3,2,1,0:T(8,128)S(1)}, f32[16,8,8,256]{3,2,1,0:T(8,128)}, u32[]{:S(2)}) copy-start(f32[16,8,8,256]{3,2,1,0:T(8,128)} %get-tuple-element.94.own.late) | copy-start | bytes 3145732
  143.2 1.1 copy-start.6
  144.2 1.1 copy-start.8
  (1 other events, 0.8 us)

commit v4 on v3

--- a/solution.py
+++ b/solution.py
@@ -69,7 +69,7 @@
 
 
 DEPTH = 3 * PLANES * ROWS + 16
-STEPS = (0, 1, 2, 6, 5, 3, 7, 4)
+STEPS = (0, 2, 6, 4, 1, 5, 3, 7)
 
 
 def state_copies(states, rate, edges, place, core, target, sems):

time: 233 us -> 248 us (1.064)
  waiting for transfers between devices: 22.6 us -> 30.4 us
  starting transfers between devices: 58.9 us -> 64.4 us
    all_to_all x1, blocking collectives: 27.6 us -> 35.5 us  [per_device(): parts = lax.all_to_all(parts, 'tm', 0, 0)]
    ppermute x7, waiting for transfers between devices: 0.02 us -> 7.86 us  [to_chips(): lax.ppermute(piece, 'space', masks[2 * step])]
    all_to_all x1, blocking collectives: 46.6 us -> 40.4 us  [per_device(): results = lax.all_to_all(results, ('tm', 'space'), 0, 0)]
    ppermute x7, starting transfers between devices: 29.3 us -> 35.4 us  [to_chips(): lax.ppermute(piece, 'space', masks[2 * step])]
  transfers between devices with their start and end apart: 17 -> 17, of which waited for: 5 -> 6; matrix products, arithmetic and copies ran while one was open for 2% -> 2% of each run, Pallas kernels for 20% -> 19%
where the time goes in v4:
time: 248 us; the launch traced here: 246 us
  blocking collectives  75.9 us (31%)
  starting transfers between devices  64.4 us (26%)
  Pallas kernels  61.2 us (25%)
  waiting for transfers between devices  30.4 us (12%)
  local copies, waits for them, and re-layouts  9.15 us (4%)
  between operations  2.77 us (1%)
    all_to_all x1, blocking collectives, per_device(): results = lax.all_to_all(results, ('tm', 'space'), 0, 0)  40.4 us
    all_to_all x1, blocking collectives, per_device(): parts = lax.all_to_all(parts, 'tm', 0, 0)  35.5 us
    ppermute x7, starting transfers between devices, to_chips(): lax.ppermute(piece, 'space', masks[2 * step])  35.4 us
    ppermute x1, waiting for transfers between devices, per_device(): ends = lax.ppermute(first, 'tm', [(t, (t - 1) % NT) for t in range(NT)])  14.8 us
    pallas_call x1, Pallas kernels, per_device(): call(solve(HALO - 1), [struct(*block), struct(HALO, 8, 8, NY), struct(HAL...  14.7 us
    pallas_call x1, Pallas kernels, per_device(): call(solve(HALO), struct(*wide), [SMEM] * 2 + [ANY] * 6, ANY, SOLVE_SCRAT...  14.6 us
    ppermute x3, starting transfers between devices, along_chain(): lax.ppermute(down, 'space', forward)  8.2 us
    ppermute x7, waiting for transfers between devices, to_chips(): lax.ppermute(piece, 'space', masks[2 * step])  7.86 us
  transfers between devices with their start and end apart: 17, of which 6 were waited for; matrix products, arithmetic and copies ran while one was open for 2% of the time, Pallas kernels for 19%

profile of v4, /device:TPU:0, one launch (start us, length us, event | category | flops | bytes accessed | tf_op | source)
XLA Modules:
  0.0 246.3 jit_solution(15266754573270754833)
XLA Ops:
  0.6 1.7 bitcast_select_fusion
  2.3 6.2 %collective-permute-start = (f32[4,256,256]{2,1,0:T(8,128)S(1)}, f32[4,256,256]{2,1,0:T(8,128)S(1)}, u32[]{:S(2)}, u32[]{:S(2)}) collective-permute-start(f32[4,256,256]{2,1,0:T(8,128)S(1)} %bitcast_select_fusion), channel_id=1, source_target_pairs={{0,112},{16,0},{32,16},{48,32},{64,48},{80,64},{96,80},{112,96},{1... | collective-permute-start | bytes 3145736 | tf_op jit(solution)/shard_map/ppermute | solution.py:548
  8.5 1.7 fusion
  11.8 4.2 %shard_map.86 = f32[8,208,256]{2,1,0:T(8,128)} custom-call(s32[3]{0:T(128)} %pad_add_fusion.ids, f32[1,2,4,256,256]{4,3,2,1,0:T(8,128)} %states.3, f32[4,256,256]{2,1,0:T(8,128)} %rate.3, f32[16,16,256]{2,1,0:T(8,128)} %reshape.25.edges), custom_call_target="tpu_custom_call" | custom-call | tf_op jit(solution)/shard_map/pallas_call | solution.py:550
  16.0 2.4 shard_map.87
  18.4 4.9 %all-to-all-start = ((f32[16,4,16,256]{3,2,1,0:T(8,128)}), f32[16,4,16,256]{3,2,1,0:T(8,128)S(1)}, u32[]{:S(2)}, u32[]{:S(2)}) async-start(f32[16,4,16,256]{3,2,1,0:T(8,128)} %shard_map.87), calls=%async_computation | async-start | bytes 2097152 | tf_op jit(solution)/shard_map/all_to_all | solution.py:559
  23.7 14.8 %collective-permute-done.field = f32[4,256,256]{2,1,0:T(8,128)S(1)} collective-permute-done((f32[4,256,256]{2,1,0:T(8,128)S(1)}, f32[4,256,256]{2,1,0:T(8,128)S(1)}, u32[]{:S(2)}, u32[]{:S(2)}) %collective-permute-start) | collective-permute-done | bytes 1048608 | tf_op jit(solution)/shard_map/ppermute | solution.py:548
  39.4 2.4 shard_map.88
  42.0 5.6 %all-to-all-start.1 = ((f32[16,4,16,256]{3,2,1,0:T(8,128)}), f32[16,4,16,256]{3,2,1,0:T(8,128)S(1)}, u32[]{:S(2)}, u32[]{:S(2)}) async-start(f32[16,4,16,256]{3,2,1,0:T(8,128)} %shard_map.88), calls=%async_computation.1 | async-start | bytes 2097152 | tf_op jit(solution)/shard_map/all_to_all | solution.py:565
  49.4 3.1 %collective-permute-start.6 = (f32[9,8,8,256]{3,2,1,0:T(8,128)S(1)}, f32[9,8,8,256]{3,2,1,0:T(8,128)}, u32[]{:S(2)}, u32[]{:S(2)}) collective-permute-start(f32[9,8,8,256]{3,2,1,0:T(8,128)S(1)} %get-tuple-element.73), channel_id=1, source_target_pairs={{0,1},{1,2},{2,3},{3,6},{6,7},{7,4},{4,5},{5,8},{8,9},{9,10},{10,1... | collective-permute-start | bytes 1769480 | tf_op jit(solution)/shard_map/ppermute | solution.py:530
  53.8 5.5 %shard_map.89 = (f32[2,208,256]{2,1,0:T(8,128)}, f32[2,208,256]{2,1,0:T(8,128)}, f32[2,208,256]{2,1,0:T(8,128)}, f32[2,208,256]{2,1,0:T(8,128)}, f32[2,208,256]{...) custom-call(s32[3]{0:T(128)} %pad_add_fusion.ids, ...), custom_call_target="tpu_custom_call" | custom-call | tf_op jit(solution)/shard_map/pallas_call | solution.py:566
  59.4 4.8 %all-to-all-done.1.received = f32[16,4,16,256]{3,2,1,0:T(8,128)S(1)} async-done(((f32[16,4,16,256]{3,2,1,0:T(8,128)}), f32[16,4,16,256]{3,2,1,0:T(8,128)S(1)}, u32[]{:S(2)}, u32[]{:S(2)}) %all-to-all-start.1) | async-done | bytes 1048608 | tf_op jit(solution)/shard_map/all_to_all | solution.py:565
  64.1 1.6 shard_map.91
  66.7 1.5 collective-permute-start.8
  68.2 1.3 collective-permute-start.9
  69.5 2.7 %collective-permute-start.2 = (f32[2,208,256]{2,1,0:T(8,128)}, f32[2,208,256]{2,1,0:T(8,128)S(1)}, u32[]{:S(2)}, u32[]{:S(2)}) collective-permute-start(f32[2,208,256]{2,1,0:T(8,128)} %get-tuple-element.67), channel_id=1, source_target_pairs={{0,4},{1,5},{2,6},{3,7},{4,0},{5,1},{6,2},{7,3},{8,12},{9,13},{10,... | collective-permute-start | bytes 1277960 | tf_op jit(solution)/shard_map/ppermute | solution.py:526
  72.2 1.9 collective-permute-start.3
  76.1 2.3 collective-permute-start.5
  80.9 14.7 %shard_map.92 = (f32[16,8,8,256]{3,2,1,0:T(8,128)}, f32[9,8,8,256]{3,2,1,0:T(8,128)}, f32[9,8,8,256]{3,2,1,0:T(8,128)}) custom-call(s32[3]{0:T(128)} %pad_add_fusion.ids, f32[19]{0:T(128)} %stack.69.weights, f32[16,8,8,256]{3,2,1,0:T(8,128)} %copy-done.3, f32[9,8,8,256]{3,2,1,0:T(8,128)} %collective-permute-done.6.above_k, ...), custom_call_target="tpu_custom_call" | custom-call | tf_op jit(solution)/shard_map/pallas_call | solution.py:579
  95.6 3.6 %collective-permute-start.10 = (f32[9,8,8,256]{3,2,1,0:T(8,128)}, f32[9,8,8,256]{3,2,1,0:T(8,128)S(1)}, u32[]{:S(2)}, u32[]{:S(2)}) collective-permute-start(f32[9,8,8,256]{3,2,1,0:T(8,128)} %get-tuple-element.89), channel_id=1, source_target_pairs={{0,1},{1,2},{2,3},{3,6},{6,7},{7,4},{4,5},{5,8},{8,9},{9,10},{10,1... | collective-permute-start | bytes 1769480 | tf_op jit(solution)/shard_map/ppermute | solution.py:530
  99.2 1.3 collective-permute-start.11
  101.0 2.3 collective-permute-done.11.below.late_below
  103.3 11.8 %collective-permute-start.12 = (f32[2,208,256]{2,1,0:T(8,128)S(1)}, f32[2,208,256]{2,1,0:T(8,128)S(1)}, u32[]{:S(2)}, u32[]{:S(2)}) collective-permute-start(f32[2,208,256]{2,1,0:T(8,128)S(1)} %copy-done.15), channel_id=1, source_target_pairs={{0,10},{1,11},{2,8},{3,9},{4,14},{5,15},{6,12},{7,13},{8,2},{9,3},... | collective-permute-start | bytes 1277960 | tf_op jit(solution)/shard_map/ppermute | solution.py:526
  115.1 15.4 %collective-permute-start.14 = (f32[2,208,256]{2,1,0:T(8,128)S(1)}, f32[2,208,256]{2,1,0:T(8,128)S(1)}, u32[]{:S(2)}, u32[]{:S(2)}) collective-permute-start(f32[2,208,256]{2,1,0:T(8,128)S(1)} %copy-done.13), channel_id=1, source_target_pairs={{0,14},{1,15},{2,12},{3,13},{4,10},{5,11},{6,8},{7,9},{8,6},{9,7},... | collective-permute-start | bytes 1277960 | tf_op jit(solution)/shard_map/ppermute | solution.py:526
  130.6 14.6 %shard_map.93.early = f32[18,8,8,256]{3,2,1,0:T(8,128)} custom-call(s32[3]{0:T(128)} %pad_add_fusion.ids, f32[19]{0:T(128)} %stack.69.weights, f32[16,8,8,256]{3,2,1,0:T(8,128)} %copy-done.3, f32[9,8,8,256]{3,2,1,0:T(8,128)} %collective-permute-done.6.above_k, f32[9,8,8,256]{3,2,1,0:T(8,128)} %collective-permute-done.7.below_k, ...), custom_call_target="tpu_custom_call" | custom-call | tf_op jit(solution)/shard_map/pallas_call | solution.py:594
  145.2 7.8 %collective-permute-done.14.refs_7_ = f32[2,208,256]{2,1,0:T(8,128)S(1)} collective-permute-done((f32[2,208,256]{2,1,0:T(8,128)S(1)}, f32[2,208,256]{2,1,0:T(8,128)S(1)}, u32[]{:S(2)}, u32[]{:S(2)}) %collective-permute-start.14) | collective-permute-done | bytes 426016 | tf_op jit(solution)/shard_map/ppermute | solution.py:526
  153.0 3.4 %shard_map.94 = (f32[2,18,8,8,256]{4,3,2,1,0:T(8,128)S(1)}, f32[16,8,8,256]{3,2,1,0:T(8,128)S(1)}) custom-call(s32[3]{0:T(128)S(1)} %copy-done.10, f32[2,208,256]{2,1,0:T(8,128)S(1)} %copy-done.9, f32[2,208,256]{2,1,0:T(8,128)S(1)} %collective-permute-done.2.refs_1_, f32[2,208,256]{2,1,0:T(8,128)S(1)} %collective-permute-done.3.refs_2_, ...), custom_call_target="tpu_custom_call" | custom-call | tf_op jit(solution)/shard_map/pallas_call | solution.py:599
  158.6 7.3 %shard_map.95 = f32[8,2,2,8,8,256]{5,4,3,2,1,0:T(8,128)S(1)} custom-call(s32[3]{0:T(128)S(1)} %copy-done.10, f32[16,8,8,256]{3,2,1,0:T(8,128)S(1)} %copy-done.4, f32[9,8,8,256]{3,2,1,0:T(8,128)S(1)} %copy-done.6, f32[9,8,8,256]{3,2,1,0:T(8,128)S(1)} %copy-done.8, f32[18,8,8,256]{3,2,1,0:T(8,128)S(1)} %copy-done, ...), custom_call_target="tpu_custom_call" | custom-call | tf_op jit(solution)/shard_map/pallas_call | solution.py:606
  165.9 35.5 %all_to_all.20.received = f32[8,2,2,8,8,256]{5,4,3,2,1,0:T(8,128)S(1)} all-to-all(f32[8,2,2,8,8,256]{5,4,3,2,1,0:T(8,128)S(1)} %shard_map.95), channel_id=1, replica_groups=mesh['tm'=8,'space'=16] {'tm'}, dimensions={0} | all-to-all | bytes 4194304 | tf_op jit(solution)/shard_map/all_to_all | solution.py:630
  201.5 1.8 shard_map.96
  203.2 40.4 %all_to_all.21.received = f32[128,2,8,256]{3,2,1,0:T(8,128)S(1)} all-to-all(f32[128,2,8,256]{3,2,1,0:T(8,128)S(1)} %shard_map.96), channel_id=1, replica_groups=mesh['tm'=8,'space'=16] {'tm','space'}, dimensions={0} | all-to-all | bytes 4194304 | tf_op jit(solution)/shard_map/all_to_all | solution.py:643
  243.6 2.7 %shard_map.97 = (f32[1,4,256,256]{3,2,1,0:T(8,128)}, f32[4,256,256]{2,1,0:T(8,128)}) custom-call(f32[128,2,8,256]{3,2,1,0:T(8,128)S(1)} %all_to_all.21.received), custom_call_target="tpu_custom_call" | custom-call | tf_op jit(solution)/shard_map/pallas_call | solution.py:644
  (59 shorter events, 12.5 us)
Async XLA Ops:
  2.3 36.1 %collective-permute-start = (f32[4,256,256]{2,1,0:T(8,128)S(1)}, f32[4,256,256]{2,1,0:T(8,128)S(1)}, u32[]{:S(2)}, u32[]{:S(2)}) collective-permute-start(f32[4,256,256]{2,1,0:T(8,128)S(1)} %bitcast_select_fusion), channel_id=1, source_target_pairs={{0,112},{16,0},{32,16},{48,32},{64,48},{80,64},{96,80},{112,96},{1... | collective-permute-start | bytes 3145736 | tf_op jit(solution)/shard_map/ppermute | solution.py:548
  18.4 23.6 %all-to-all-start = ((f32[16,4,16,256]{3,2,1,0:T(8,128)}), f32[16,4,16,256]{3,2,1,0:T(8,128)S(1)}, u32[]{:S(2)}, u32[]{:S(2)}) async-start(f32[16,4,16,256]{3,2,1,0:T(8,128)} %shard_map.87), calls=%async_computation | async-start | bytes 2097152 | tf_op jit(solution)/shard_map/all_to_all | solution.py:559
  23.3 30.6 %collective-permute-start.1 = (f32[8,208,256]{2,1,0:T(8,128)}, f32[8,208,256]{2,1,0:T(8,128)}, u32[]{:S(2)}, u32[]{:S(2)}) collective-permute-start(f32[8,208,256]{2,1,0:T(8,128)} %shard_map.86), channel_id=1, source_target_pairs={{0,1},{1,0},{2,3},{3,2},{4,5},{5,4},{6,7},{7,6},{8,9},{9,8},{10,11... | collective-permute-start | bytes 5111816 | tf_op jit(solution)/shard_map/ppermute | solution.py:564
  38.5 1.0 copy-start.11
  42.0 22.1 %all-to-all-start.1 = ((f32[16,4,16,256]{3,2,1,0:T(8,128)}), f32[16,4,16,256]{3,2,1,0:T(8,128)S(1)}, u32[]{:S(2)}, u32[]{:S(2)}) async-start(f32[16,4,16,256]{3,2,1,0:T(8,128)} %shard_map.88), calls=%async_computation.1 | async-start | bytes 2097152 | tf_op jit(solution)/shard_map/all_to_all | solution.py:565
  48.4 1.0 copy-start.3
  49.4 22.8 %collective-permute-start.6 = (f32[9,8,8,256]{3,2,1,0:T(8,128)S(1)}, f32[9,8,8,256]{3,2,1,0:T(8,128)}, u32[]{:S(2)}, u32[]{:S(2)}) collective-permute-start(f32[9,8,8,256]{3,2,1,0:T(8,128)S(1)} %get-tuple-element.73), channel_id=1, source_target_pairs={{0,1},{1,2},{2,3},{3,6},{6,7},{7,4},{4,5},{5,8},{8,9},{9,10},{10,1... | collective-permute-start | bytes 1769480 | tf_op jit(solution)/shard_map/ppermute | solution.py:530
  52.5 21.6 %collective-permute-start.7 = (f32[9,8,8,256]{3,2,1,0:T(8,128)S(1)}, f32[9,8,8,256]{3,2,1,0:T(8,128)}, u32[]{:S(2)}, u32[]{:S(2)}) collective-permute-start(f32[9,8,8,256]{3,2,1,0:T(8,128)S(1)} %get-tuple-element.74), channel_id=1, source_target_pairs={{1,0},{2,1},{3,2},{6,3},{7,6},{4,7},{5,4},{8,5},{9,8},{10,9},{11,1... | collective-permute-start | bytes 1769480 | tf_op jit(solution)/shard_map/ppermute | solution.py:530
  65.7 1.0 copy-start.1
  66.7 8.6 %collective-permute-start.8 = (f32[8,8,8,256]{3,2,1,0:T(8,128)S(1)}, f32[8,8,8,256]{3,2,1,0:T(8,128)S(1)}, u32[]{:S(2)}, u32[]{:S(2)}) collective-permute-start(f32[8,8,8,256]{3,2,1,0:T(8,128)S(1)} %get-tuple-element.77), channel_id=1, source_target_pairs={{0,1},{1,2},{2,3},{3,6},{6,7},{7,4},{4,5},{5,8},{8,9},{9,10},{10,1... | collective-permute-start | bytes 1572872 | tf_op jit(solution)/shard_map/ppermute | solution.py:530
  68.2 12.6 %collective-permute-start.9 = (f32[8,8,8,256]{3,2,1,0:T(8,128)}, f32[8,8,8,256]{3,2,1,0:T(8,128)}, u32[]{:S(2)}, u32[]{:S(2)}) collective-permute-start(f32[8,8,8,256]{3,2,1,0:T(8,128)} %get-tuple-element.78), channel_id=1, source_target_pairs={{1,0},{2,1},{3,2},{6,3},{7,6},{4,7},{5,4},{8,5},{9,8},{10,9},{11,1... | collective-permute-start | bytes 1572872 | tf_op jit(solution)/shard_map/ppermute | solution.py:530
  69.5 26.0 %collective-permute-start.2 = (f32[2,208,256]{2,1,0:T(8,128)}, f32[2,208,256]{2,1,0:T(8,128)S(1)}, u32[]{:S(2)}, u32[]{:S(2)}) collective-permute-start(f32[2,208,256]{2,1,0:T(8,128)} %get-tuple-element.67), channel_id=1, source_target_pairs={{0,4},{1,5},{2,6},{3,7},{4,0},{5,1},{6,2},{7,3},{8,12},{9,13},{10,... | collective-permute-start | bytes 1277960 | tf_op jit(solution)/shard_map/ppermute | solution.py:526
  72.2 23.3 %collective-permute-start.3 = (f32[2,208,256]{2,1,0:T(8,128)}, f32[2,208,256]{2,1,0:T(8,128)S(1)}, u32[]{:S(2)}, u32[]{:S(2)}) collective-permute-start(f32[2,208,256]{2,1,0:T(8,128)} %get-tuple-element.68), channel_id=1, source_target_pairs={{0,12},{1,13},{2,14},{3,15},{4,8},{5,9},{6,10},{7,11},{8,4},{9,5},... | collective-permute-start | bytes 1277960 | tf_op jit(solution)/shard_map/ppermute | solution.py:526
  74.1 21.4 %collective-permute-start.4 = (f32[2,208,256]{2,1,0:T(8,128)}, f32[2,208,256]{2,1,0:T(8,128)S(1)}, u32[]{:S(2)}, u32[]{:S(2)}) collective-permute-start(f32[2,208,256]{2,1,0:T(8,128)} %get-tuple-element.69), channel_id=1, source_target_pairs={{0,8},{1,9},{2,10},{3,11},{4,12},{5,13},{6,14},{7,15},{8,0},{9,1},... | collective-permute-start | bytes 1277960 | tf_op jit(solution)/shard_map/ppermute | solution.py:526
  76.1 19.5 %collective-permute-start.5 = (f32[2,208,256]{2,1,0:T(8,128)}, f32[2,208,256]{2,1,0:T(8,128)S(1)}, u32[]{:S(2)}, u32[]{:S(2)}) collective-permute-start(f32[2,208,256]{2,1,0:T(8,128)} %get-tuple-element.70), channel_id=1, source_target_pairs={{0,2},{1,3},{2,0},{3,1},{4,6},{5,7},{6,4},{7,5},{8,10},{9,11},{10,... | collective-permute-start | bytes 1277960 | tf_op jit(solution)/shard_map/ppermute | solution.py:526
  80.9 22.4 %copy-start.15 = (f32[2,208,256]{2,1,0:T(8,128)S(1)}, f32[2,208,256]{2,1,0:T(8,128)}, u32[]{:S(2)}) copy-start(f32[2,208,256]{2,1,0:T(8,128)} %get-tuple-element.91) | copy-start | bytes 1277956
  80.9 34.2 %copy-start.14 = (f32[2,208,256]{2,1,0:T(8,128)S(1)}, f32[2,208,256]{2,1,0:T(8,128)}, u32[]{:S(2)}) copy-start(f32[2,208,256]{2,1,0:T(8,128)} %get-tuple-element.92) | copy-start | bytes 1277956
  80.9 34.2 %copy-start.13 = (f32[2,208,256]{2,1,0:T(8,128)S(1)}, f32[2,208,256]{2,1,0:T(8,128)}, u32[]{:S(2)}) copy-start(f32[2,208,256]{2,1,0:T(8,128)} %get-tuple-element.93) | copy-start | bytes 1277956
  95.6 57.5 %copy-start.9 = (f32[2,208,256]{2,1,0:T(8,128)S(1)}, f32[2,208,256]{2,1,0:T(8,128)}, u32[]{:S(2)}) copy-start(f32[2,208,256]{2,1,0:T(8,128)} %get-tuple-element.97.refs_0_) | copy-start | bytes 1277956
  95.6 57.4 %copy-start.10 = (s32[3]{0:T(128)S(1)}, s32[3]{0:T(128)}, u32[]{:S(2)}) copy-start(s32[3]{0:T(128)} %pad_add_fusion.ids) | copy-start | bytes 40
  95.6 5.3 %collective-permute-start.10 = (f32[9,8,8,256]{3,2,1,0:T(8,128)}, f32[9,8,8,256]{3,2,1,0:T(8,128)S(1)}, u32[]{:S(2)}, u32[]{:S(2)}) collective-permute-start(f32[9,8,8,256]{3,2,1,0:T(8,128)} %get-tuple-element.89), channel_id=1, source_target_pairs={{0,1},{1,2},{2,3},{3,6},{6,7},{7,4},{4,5},{5,8},{8,9},{9,10},{10,1... | collective-permute-start | bytes 1769480 | tf_op jit(solution)/shard_map/ppermute | solution.py:530
  99.2 4.1 %collective-permute-start.11 = (f32[9,8,8,256]{3,2,1,0:T(8,128)}, f32[9,8,8,256]{3,2,1,0:T(8,128)S(1)}, u32[]{:S(2)}, u32[]{:S(2)}) collective-permute-start(f32[9,8,8,256]{3,2,1,0:T(8,128)} %get-tuple-element.90), channel_id=1, source_target_pairs={{1,0},{2,1},{3,2},{6,3},{7,6},{4,7},{5,4},{8,5},{9,8},{10,9},{11,1... | collective-permute-start | bytes 1769480 | tf_op jit(solution)/shard_map/ppermute | solution.py:530
  101.0 29.6 %copy-start.5 = (f32[9,8,8,256]{3,2,1,0:T(8,128)}, f32[9,8,8,256]{3,2,1,0:T(8,128)S(1)}, u32[]{:S(2)}) copy-start(f32[9,8,8,256]{3,2,1,0:T(8,128)S(1)} %collective-permute-done.10.above.late_above) | copy-start | bytes 1769476
  103.3 27.3 %copy-start.7 = (f32[9,8,8,256]{3,2,1,0:T(8,128)}, f32[9,8,8,256]{3,2,1,0:T(8,128)S(1)}, u32[]{:S(2)}) copy-start(f32[9,8,8,256]{3,2,1,0:T(8,128)S(1)} %collective-permute-done.11.below.late_below) | copy-start | bytes 1769476
  103.3 41.9 %collective-permute-start.12 = (f32[2,208,256]{2,1,0:T(8,128)S(1)}, f32[2,208,256]{2,1,0:T(8,128)S(1)}, u32[]{:S(2)}, u32[]{:S(2)}) collective-permute-start(f32[2,208,256]{2,1,0:T(8,128)S(1)} %copy-done.15), channel_id=1, source_target_pairs={{0,10},{1,11},{2,8},{3,9},{4,14},{5,15},{6,12},{7,13},{8,2},{9,3},... | collective-permute-start | bytes 1277960 | tf_op jit(solution)/shard_map/ppermute | solution.py:526
  115.1 30.1 %collective-permute-start.13 = (f32[2,208,256]{2,1,0:T(8,128)S(1)}, f32[2,208,256]{2,1,0:T(8,128)S(1)}, u32[]{:S(2)}, u32[]{:S(2)}) collective-permute-start(f32[2,208,256]{2,1,0:T(8,128)S(1)} %copy-done.14), channel_id=1, source_target_pairs={{0,6},{1,7},{2,4},{3,5},{4,2},{5,3},{6,0},{7,1},{8,14},{9,15},{10,... | collective-permute-start | bytes 1277960 | tf_op jit(solution)/shard_map/ppermute | solution.py:526
  115.1 37.9 %collective-permute-start.14 = (f32[2,208,256]{2,1,0:T(8,128)S(1)}, f32[2,208,256]{2,1,0:T(8,128)S(1)}, u32[]{:S(2)}, u32[]{:S(2)}) collective-permute-start(f32[2,208,256]{2,1,0:T(8,128)S(1)} %copy-done.13), channel_id=1, source_target_pairs={{0,14},{1,15},{2,12},{3,13},{4,10},{5,11},{6,8},{7,9},{8,6},{9,7},... | collective-permute-start | bytes 1277960 | tf_op jit(solution)/shard_map/ppermute | solution.py:526
  145.1 11.3 %copy-start = (f32[18,8,8,256]{3,2,1,0:T(8,128)S(1)}, f32[18,8,8,256]{3,2,1,0:T(8,128)}, u32[]{:S(2)}) copy-start(f32[18,8,8,256]{3,2,1,0:T(8,128)} %shard_map.93.early) | copy-start | bytes 3538948
  145.2 11.3 %copy-start.2 = (f32[16,8,8,256]{3,2,1,0:T(8,128)S(1)}, f32[16,8,8,256]{3,2,1,0:T(8,128)}, u32[]{:S(2)}) copy-start(f32[16,8,8,256]{3,2,1,0:T(8,128)} %copy-done.1) | copy-start | bytes 3145732
  145.2 11.3 %copy-start.4 = (f32[16,8,8,256]{3,2,1,0:T(8,128)S(1)}, f32[16,8,8,256]{3,2,1,0:T(8,128)}, u32[]{:S(2)}) copy-start(f32[16,8,8,256]{3,2,1,0:T(8,128)} %get-tuple-element.94.own.late) | copy-start | bytes 3145732
  156.5 1.1 copy-start.6
  157.5 1.1 copy-start.8
  (1 other events, 0.8 us)
